TPU v7x, 32 devices: a whole 2x2x4 slice. The times are simulated.
32 devices in a mesh: len: 8 (over z, x), xs: 4 (over y, core).
Axes of the slice: x: 2, y: 2, z: 4, core: 2. Of those that a mesh axis runs over, the one named last changes fastest.
Arguments:
- right_side: float32 [3, 16, 64, 4096], P(None, None, None, ('len', 'xs')), may hold values from -19 to 19
- mass_field: float32 [16, 64, 4096], P(None, None, ('len', 'xs')), may hold values from 0.5 to 2
- span_lengths: int32 [32], replicated, may hold values from 1 to 256, 4096 in all
- stick_flags: int32 [64], replicated, may hold values from 0 to 1
- normal_load: float32 [64], replicated, may hold values from 0.5 to 4
- prior_friction: float32 [2, 64], replicated, may hold values from -4 to 4
Outputs:
- increment: float32 [3, 16, 64, 4096], P(None, None, None, ('len', 'xs'))
- residual: float32 [3, 16, 64, 4096], P(None, None, None, ('len', 'xs'))
- friction: float32 [2, 64], replicated
Inputs may be any that keep to these rules, and one draw needn't show every extreme that they name: `span_lengths`: the spans sum to 4096; the longest is exactly 256. `stick_flags`: 1 marks a sticking bearing, 0 a sliding one.
All inputs are finite; a program needn't handle non-finite values.
Results may differ from a plain program's by a relative error of at most 0.0003.
Values sent between devices are 32-bit elements; how exact they have to be, the bound alone decides.
No kernel may reach another device: no remote copies, remote signals or barrier semaphores. Data moves between devices by JAX's collectives and lax.ppermute only.
A program may use at most 64 MiB of HBM per device.

v0:
```python
import jax
import jax.numpy as jnp
from jax import lax
from jax.sharding import PartitionSpec as P

ITERS = 3


shear_modulus = 1.0
bulk_modulus = 1.5
elastic_stiffness = 8.0
pendulum_radius = 4.0
vertical_stiffness = 5.0
static_friction = 0.6
kinetic_friction = 0.45


def extended_2(cells, sides, width):
    for axis, dim in sides:
        count = lax.axis_size(axis)
        ends = count - 1
        head = lax.slice_in_dim(cells, 0, width, axis=dim)
        tail = lax.slice_in_dim(cells, cells.shape[dim] - width, cells.shape[dim], axis=dim)
        cells = jnp.concatenate(
            [
                lax.ppermute(tail, axis, [(i, (i + 1) % count) for i in range(ends)]),
                cells,
                lax.ppermute(head, axis, [((i + 1) % count, i) for i in range(ends)]),
            ],
            axis=dim,
        )
    return cells


def window(array, anchor, extent):
    return array[
        ...,
        anchor[0] : anchor[0] + extent[0],
        anchor[1] : anchor[1] + extent[1],
        anchor[2] : anchor[2] + extent[2],
    ]


def shifted(anchor, along_dim, stride):
    moved = list(anchor)
    moved[along_dim] = moved[along_dim] + stride
    return tuple(moved)


def difference(array, anchor, extent, along_dim):
    upper = window(array, shifted(anchor, along_dim, 1), extent)
    lower = window(array, shifted(anchor, along_dim, -1), extent)
    return 0.5 * (upper - lower)


def laplace_at(padded, anchor, extent):
    total = 6.0 * window(padded, anchor, extent)
    for along_dim in range(3):
        for stride in (1, -1):
            total = total - window(padded, shifted(anchor, along_dim, stride), extent)
    return total


def pad_local(array, width):
    widths = [(0, 0)] * array.ndim
    widths[array.ndim - 3] = (width, width)
    widths[array.ndim - 2] = (width, width)
    return jnp.pad(array, widths)


def operate(field, mass_field):
    dims_of = (2, 1, 0)
    extent = field.shape[1:]
    extended = extended_2(field, ((("len", "xs"), 3),), 1)
    extended = pad_local(extended, 1)
    divergence = difference(extended[0], (1, 1, 1), extent, dims_of[0])
    for component in (1, 2):
        divergence = divergence + difference(
            extended[component], (1, 1, 1), extent, dims_of[component]
        )
    div_extended = extended_2(divergence, ((("len", "xs"), 2),), 1)
    div_extended = pad_local(div_extended, 1)
    laplacian = laplace_at(extended, (1, 1, 1), extent)
    gradient = jnp.stack(
        [difference(div_extended, (1, 1, 1), extent, dims_of[c]) for c in range(3)]
    )
    return mass_field[None] * field + shear_modulus * laplacian - bulk_modulus * gradient


def return_map(readout, stick_flags, normal_load, prior_friction):
    coeff = jnp.where(stick_flags == 1, static_friction, kinetic_friction)
    radius = coeff * normal_load
    trial = prior_friction + elastic_stiffness * readout[0:2]
    magnitude = jnp.sqrt(trial[0] * trial[0] + trial[1] * trial[1])
    friction = trial * (radius / jnp.maximum(magnitude, radius))
    horizontal = friction + normal_load / pendulum_radius * readout[0:2]
    vertical = vertical_stiffness * readout[2]
    force = jnp.concatenate([horizontal, vertical[None]], axis=0)
    return (friction, force)


def shards(right_side, mass_field, span_lengths, stick_flags, normal_load, prior_friction):
    local_across = right_side.shape[2]
    local_along = right_side.shape[3]
    bearings = 2 * span_lengths.shape[0]
    ends = jnp.cumsum(span_lengths) - 1
    along_site = jnp.repeat(ends, 2)
    across_site = jnp.tile(
        jnp.array([local_across // 4, 3 * local_across // 4], dtype=jnp.int32),
        span_lengths.shape[0],
    )
    along_start = lax.axis_index(("len", "xs")) * local_along
    along_hit = (
        lax.broadcasted_iota(jnp.int32, (local_along, bearings), 0) + along_start
        == along_site[None, :]
    ).astype(jnp.float32)
    across_hit = (
        lax.broadcasted_iota(jnp.int32, (local_across, bearings), 0) == across_site[None, :]
    ).astype(jnp.float32)
    increment = jnp.zeros_like(right_side)
    solved = right_side
    direction = right_side
    norm_now = lax.psum(jnp.sum(solved * solved), ("len", "xs"))
    for iteration in range(ITERS):
        image = operate(direction, mass_field)
        carried = jnp.zeros((3, 0), jnp.float32)
        curvature, cross_term, image_sq, picked = lax.psum(
            (jnp.sum(direction * image), jnp.sum(solved * image), jnp.sum(image * image), carried),
            ("len", "xs"),
        )
        alpha = norm_now / curvature
        increment = increment + alpha * direction
        solved = solved - alpha * image
        norm_next = norm_now - 2.0 * alpha * cross_term + alpha * alpha * image_sq
        direction = solved + norm_next / norm_now * direction
        norm_now = norm_next
    picked = jnp.einsum("csl,lb->csb", increment[:, 0], along_hit, precision=lax.Precision.HIGHEST)
    readout = lax.psum(jnp.sum(picked * across_hit[None], axis=1), ("len", "xs"))
    friction, force = return_map(readout, stick_flags, normal_load, prior_friction)
    spread = force[:, None, :] * across_hit[None]
    placed = jnp.einsum("csb,lb->csl", spread, along_hit, precision=lax.Precision.HIGHEST)
    residual = solved.at[:, 0].add(-placed)
    return (increment, residual, friction)


def solution(mesh):
    in_specs = (
        P(None, None, None, ("len", "xs")),
        P(None, None, ("len", "xs")),
        P(),
        P(),
        P(),
        P(),
    )
    out_specs = (P(None, None, None, ("len", "xs")), P(None, None, None, ("len", "xs")), P())
    return jax.shard_map(shards, mesh=mesh, in_specs=in_specs, out_specs=out_specs, check_vma=False)
```

profile of v0, /device:TPU:0, one launch (start us, length us, event | category | flops | bytes accessed | tf_op | source)
XLA Modules:
  0.0 326.0 jit_solution(10983758655405784455)
XLA Ops:
  0.6 2.5 fusion.66
  3.6 2.4 collective-permute-start
  8.5 3.2 collective-permute-done.1
  13.4 3.8 %select_maximum_fusion.4 = f32[3,18,66,130]{3,2,1,0:T(8,128)S(1)} fusion(f32[3,16,64,1]{3,2,1,0:T(8,128)} %copy.71, f32[3,16,64,128]{3,2,1,0:T(8,128)S(1)} %copy-done, f32[3,16,64,1]{3,2,1,0:T(8,128)S(1)} %copy.70), kind=kLoop, calls=%fused_computation.8 | loop fusion | flops 6949800 | bytes 3450720 | tf_op jit(solution)/shard_map/concatenate | solution.py:24
  20.1 5.1 %collective-permute-start.3 = (f32[16,64,1]{2,1,0:T(8,128)S(1)}, f32[16,64,1]{2,1,0:T(8,128)S(1)}, u32[]{:S(2)}, u32[]{:S(2)}) collective-permute-start(f32[16,64,1]{2,1,0:T(8,128)S(1)} %get-tuple-element.67), channel_id=1, source_target_pairs={{0,1},{1,2},{2,3},{3,4},{4,5},{5,6},{6,7},{7,8},{8,9},{9,10},{10,1... | collective-permute-start | bytes 12296 | tf_op jit(solution)/shard_map/ppermute | solution.py:26
  25.3 3.9 %fusion.10 = (f32[3,16,64,128]{3,2,1,0:T(8,128)S(1)}, f32[]{:T(128)}) fusion(f32[3,16,64,128]{3,2,1,0:T(8,128)S(1)} %copy-done, f32[3,16,64,1]{3,2,1,0:T(8,128)S(1)} %copy-done.11, f32[3,16,64,1]{3,2,1,0:T(8,128)S(1)} %copy-done.12, f32[3,18,66,130]{3,2,1,0:T(8,128)S(1)} %select_maximum_fusion.4, f32[16,64,128]{2,1,0:T(8,128)S(1)} %copy-done.18), kind=kLoop, calls=%fused_computation.37 | loop fusion | flops 5111807 | bytes 9986052 | tf_op jit(solution)/shard_map/add | solution.py:87
  32.0 51.1 %all-reduce.7 = (f32[]{:T(128)}, f32[]{:T(128)}, f32[]{:T(128)}) all-reduce(f32[]{:T(128)} %get-tuple-element.54, f32[]{:T(128)} %get-tuple-element.25, f32[]{:T(128)} %get-tuple-element.24), channel_id=1, replica_groups=mesh['len'=8,'xs'=4] {'len','xs'}, use_global_device_ids=true, to_apply=%region_1.2 | all-reduce | flops 3 | bytes 24 | tf_op jit(solution)/shard_map/psum | solution.py:123
  87.1 3.8 %multiply_add_fusion.2 = (f32[3,16,64,128]{3,2,0,1:T(8,128)S(1)}, f32[3,16,64,128]{3,2,0,1:T(8,128)}) fusion(f32[3,16,64,128]{3,2,1,0:T(8,128)S(1)} %copy-done, f32[]{:T(128)S(6)} %div.25, f32[3,16,64,128]{3,2,1,0:T(8,128)} %copy-done.7, f32[]{:T(128)S(6)} %div.24, f32[1,16,64,128]{3,2,1,0:T(8,128)} %copy-done.22, f32[1,16,64,128]{3,2,1,0:T(8,128)} %copy-done.21, ...), kind=kLoop, calls=%fused_computation.59 | loop fusion | flops 3145728 | bytes 7864328 | tf_op jit(solution)/shard_map/add | solution.py:135
  90.9 2.3 fusion.65
  93.2 1.9 copy.82
  96.5 1.9 copy.83
  101.7 2.5 collective-permute-done.5
  106.0 4.1 %select_maximum_fusion.2 = f32[3,18,66,130]{3,2,1,0:T(8,128)S(1)} fusion(f32[3,16,64,1]{3,2,1,0:T(8,128)} %copy.86, f32[3,16,64,1]{3,2,1,0:T(8,128)} %copy.84, f32[3,16,64,128]{3,2,0,1:T(8,128)S(1)} %get-tuple-element.38), kind=kLoop, calls=%fused_computation.6 | loop fusion | flops 6949800 | bytes 3450720 | tf_op jit(solution)/shard_map/concatenate | solution.py:24
  115.9 5.9 %collective-permute-start.7 = (f32[16,64,1]{2,1,0:T(8,128)}, f32[16,64,1]{2,1,0:T(8,128)}, u32[]{:S(2)}, u32[]{:S(2)}) collective-permute-start(f32[16,64,1]{2,1,0:T(8,128)} %get-tuple-element.65), channel_id=1, source_target_pairs={{0,1},{1,2},{2,3},{3,4},{4,5},{5,6},{6,7},{7,8},{8,9},{9,10},{10,1... | collective-permute-start | bytes 12296 | tf_op jit(solution)/shard_map/ppermute | solution.py:26
  122.9 1.9 select_maximum_fusion.8
  125.5 2.0 fusion.34
  127.5 4.8 %multiply_reduce_fusion.1 = (f32[]{:T(128)}, f32[]{:T(128)}, f32[]{:T(128)}, f32[3,16,64,128]{3,2,0,1:T(8,128)}) fusion(f32[3,16,64,128]{3,2,0,1:T(8,128)S(1)} %copy-done.5, f32[3,16,64,128]{3,2,0,1:T(8,128)S(1)} %get-tuple-element.38, f32[3,16,64,128]{3,2,1,0:T(8,128)S(1)} %copy.80, f32[3,16,64,1]{3,2,1,0:T(8,128)S(1)} %copy-done.13, ...), kind=kLoop, calls=%fused_computation.56 | loop fusion | flops 8257533 | bytes 17825804 | tf_op jit(solution)/shard_map/reduce_sum | solution.py:128
  132.3 52.2 %all-reduce.6 = (f32[]{:T(128)}, f32[]{:T(128)}, f32[]{:T(128)}) all-reduce(f32[]{:T(128)} %get-tuple-element.28, f32[]{:T(128)} %get-tuple-element.27, f32[]{:T(128)} %get-tuple-element.26), channel_id=1, replica_groups=mesh['len'=8,'xs'=4] {'len','xs'}, use_global_device_ids=true, to_apply=%region_7.8 | all-reduce | flops 3 | bytes 24 | tf_op jit(solution)/shard_map/psum | solution.py:127
  186.6 2.4 multiply_add_fusion.1
  189.0 2.2 fusion.64
  191.2 1.9 copy.97
  194.5 1.9 copy.96
  196.4 3.3 collective-permute-start.8
  199.7 2.7 copy.94
  204.1 1.7 copy.98
  205.9 4.3 %select_maximum_fusion = f32[3,18,66,130]{3,2,1,0:T(8,128)S(1)} fusion(f32[3,16,64,1]{3,2,1,0:T(8,128)} %copy.100, f32[3,16,64,1]{3,2,1,0:T(8,128)} %copy.98, f32[3,16,64,128]{3,2,0,1:T(8,128)} %copy-done.1), kind=kLoop, calls=%fused_computation.4 | loop fusion | flops 6949800 | bytes 3450720 | tf_op jit(solution)/shard_map/concatenate | solution.py:24
  213.6 5.6 %collective-permute-start.11 = (f32[16,64,1]{2,1,0:T(8,128)}, f32[16,64,1]{2,1,0:T(8,128)}, u32[]{:S(2)}, u32[]{:S(2)}) collective-permute-start(f32[16,64,1]{2,1,0:T(8,128)} %get-tuple-element.63), channel_id=1, source_target_pairs={{0,1},{1,2},{2,3},{3,4},{4,5},{5,6},{6,7},{7,8},{8,9},{9,10},{10,1... | collective-permute-start | bytes 12296 | tf_op jit(solution)/shard_map/ppermute | solution.py:26
  219.2 7.7 %fusion.4 = f32[3,16,64,128]{3,2,1,0:T(8,128)} fusion(f32[3,16,64,128]{3,2,1,0:T(8,128)} %copy.94, f32[3,16,64,1]{3,2,1,0:T(8,128)} %copy.98, f32[3,16,64,1]{3,2,1,0:T(8,128)} %copy.100, f32[3,18,66,130]{3,2,1,0:T(8,128)S(1)} %select_maximum_fusion, f32[16,64,128]{2,1,0:T(8,128)S(1)} %copy-done.20), kind=kLoop, calls=%fused_computation.19 | loop fusion | flops 4325376 | bytes 9986048 | tf_op jit(solution)/shard_map/add | solution.py:87
  229.2 2.1 fusion.24
  232.9 45.3 %psum.65 = f32[]{:T(128)} all-reduce(f32[]{:T(128)} %multiply_reduce_fusion), channel_id=1, replica_groups=mesh['len'=8,'xs'=4] {'len','xs'}, use_global_device_ids=true, to_apply=%region_13.14 | all-reduce | flops 1 | bytes 8 | tf_op jit(solution)/shard_map/psum | solution.py:127
  278.9 2.1 multiply_add_fusion
  284.5 39.3 %psum.66 = f32[3,64]{1,0:T(4,128)S(1)} all-reduce(f32[3,64]{1,0:T(4,128)S(1)} %fusion.17), channel_id=1, replica_groups=mesh['len'=8,'xs'=4] {'len','xs'}, use_global_device_ids=true, to_apply=%region_16.17 | all-reduce | flops 192 | bytes 1536 | tf_op jit(solution)/shard_map/psum | solution.py:138
  (130 shorter events, 40.1 us)
Async XLA Ops:
  3.1 4.7 %copy-start.32 = (s32[2]{0:T(128)S(1)}, s32[2]{0:T(128)}, u32[]{:S(2)}) copy-start(s32[2]{0:T(128)} %constant.73.clone) | copy-start | bytes 28
  3.6 4.3 %collective-permute-start = (f32[3,16,64,1]{2,1,3,0:T(8,128)S(1)}, f32[3,16,64,1]{2,1,3,0:T(8,128)S(1)}, u32[]{:S(2)}, u32[]{:S(2)}) collective-permute-start(f32[3,16,64,1]{2,1,3,0:T(8,128)S(1)} %copy.111), channel_id=1, source_target_pairs={{0,1},{1,2},{2,3},{3,4},{4,5},{5,6},{6,7},{7,8},{8,9},{9,10},{10,1... | collective-permute-start | bytes 36872 | tf_op jit(solution)/shard_map/ppermute | solution.py:26
  6.5 5.2 %collective-permute-start.1 = (f32[3,16,64,1]{2,1,3,0:T(8,128)S(1)}, f32[3,16,64,1]{2,1,3,0:T(8,128)S(1)}, u32[]{:S(2)}, u32[]{:S(2)}) collective-permute-start(f32[3,16,64,1]{2,1,3,0:T(8,128)S(1)} %copy.112), channel_id=1, source_target_pairs={{1,0},{2,1},{3,2},{4,3},{5,4},{6,5},{7,6},{8,7},{9,8},{10,9},{11,1... | collective-permute-start | bytes 36872 | tf_op jit(solution)/shard_map/ppermute | solution.py:28
  7.9 5.5 %copy-start = (f32[3,16,64,128]{3,2,1,0:T(8,128)S(1)}, f32[3,16,64,128]{3,2,1,0:T(8,128)}, u32[]{:S(2)}) copy-start(f32[3,16,64,128]{3,2,1,0:T(8,128)} %param.9) | copy-start | bytes 4718596
  8.5 8.8 %copy-start.10 = (f32[3,16,64,1]{3,2,1,0:T(8,128)}, f32[3,16,64,1]{3,2,1,0:T(8,128)S(1)}, u32[]{:S(2)}) copy-start(f32[3,16,64,1]{3,2,1,0:T(8,128)S(1)} %copy.70) | copy-start | bytes 36868
  17.6 7.6 %copy-start.12 = (f32[3,16,64,1]{3,2,1,0:T(8,128)S(1)}, f32[3,16,64,1]{3,2,1,0:T(8,128)}, u32[]{:S(2)}) copy-start(f32[3,16,64,1]{3,2,1,0:T(8,128)} %copy.71) | copy-start | bytes 36868
  18.5 6.8 %copy-start.11 = (f32[3,16,64,1]{3,2,1,0:T(8,128)S(1)}, f32[3,16,64,1]{3,2,1,0:T(8,128)}, u32[]{:S(2)}) copy-start(f32[3,16,64,1]{3,2,1,0:T(8,128)} %copy-done.10) | copy-start | bytes 36868
  18.5 6.8 %copy-start.18 = (f32[16,64,128]{2,1,0:T(8,128)S(1)}, f32[16,64,128]{2,1,0:T(8,128)}, u32[]{:S(2)}) copy-start(f32[16,64,128]{2,1,0:T(8,128)} %param.10) | copy-start | bytes 1572868
  18.7 10.4 %collective-permute-start.2 = (f32[16,64,1]{2,1,0:T(8,128)S(1)}, f32[16,64,1]{2,1,0:T(8,128)S(1)}, u32[]{:S(2)}, u32[]{:S(2)}) collective-permute-start(f32[16,64,1]{2,1,0:T(8,128)S(1)} %get-tuple-element.68), channel_id=1, source_target_pairs={{1,0},{2,1},{3,2},{4,3},{5,4},{6,5},{7,6},{8,7},{9,8},{10,9},{11,1... | collective-permute-start | bytes 12296 | tf_op jit(solution)/shard_map/ppermute | solution.py:28
  20.1 9.0 %collective-permute-start.3 = (f32[16,64,1]{2,1,0:T(8,128)S(1)}, f32[16,64,1]{2,1,0:T(8,128)S(1)}, u32[]{:S(2)}, u32[]{:S(2)}) collective-permute-start(f32[16,64,1]{2,1,0:T(8,128)S(1)} %get-tuple-element.67), channel_id=1, source_target_pairs={{0,1},{1,2},{2,3},{3,4},{4,5},{5,6},{6,7},{7,8},{8,9},{9,10},{10,1... | collective-permute-start | bytes 12296 | tf_op jit(solution)/shard_map/ppermute | solution.py:26
  93.2 6.7 %copy-start.31 = (s32[32]{0:T(128)S(1)}, s32[32]{0:T(128)}, u32[]{:S(2)}) copy-start(s32[32]{0:T(128)} %param.11) | copy-start | bytes 388
  95.2 4.9 %collective-permute-start.4 = (f32[3,16,64,1]{2,1,3,0:T(8,128)S(1)}, f32[3,16,64,1]{2,1,3,0:T(8,128)S(1)}, u32[]{:S(2)}, u32[]{:S(2)}) collective-permute-start(f32[3,16,64,1]{2,1,3,0:T(8,128)S(1)} %copy.82), channel_id=1, source_target_pairs={{0,1},{1,2},{2,3},{3,4},{4,5},{5,6},{6,7},{7,8},{8,9},{9,10},{10,1... | collective-permute-start | bytes 36872 | tf_op jit(solution)/shard_map/ppermute | solution.py:26
  98.4 5.9 %collective-permute-start.5 = (f32[3,16,64,1]{2,1,3,0:T(8,128)S(1)}, f32[3,16,64,1]{2,1,3,0:T(8,128)S(1)}, u32[]{:S(2)}, u32[]{:S(2)}) collective-permute-start(f32[3,16,64,1]{2,1,3,0:T(8,128)S(1)} %copy.83), channel_id=1, source_target_pairs={{1,0},{2,1},{3,2},{4,3},{5,4},{6,5},{7,6},{8,7},{9,8},{10,9},{11,1... | collective-permute-start | bytes 36872 | tf_op jit(solution)/shard_map/ppermute | solution.py:28
  114.6 7.4 %collective-permute-start.6 = (f32[16,64,1]{2,1,0:T(8,128)}, f32[16,64,1]{2,1,0:T(8,128)}, u32[]{:S(2)}, u32[]{:S(2)}) collective-permute-start(f32[16,64,1]{2,1,0:T(8,128)} %get-tuple-element.66), channel_id=1, source_target_pairs={{1,0},{2,1},{3,2},{4,3},{5,4},{6,5},{7,6},{8,7},{9,8},{10,9},{11,1... | collective-permute-start | bytes 12296 | tf_op jit(solution)/shard_map/ppermute | solution.py:28
  115.9 7.0 %collective-permute-start.7 = (f32[16,64,1]{2,1,0:T(8,128)}, f32[16,64,1]{2,1,0:T(8,128)}, u32[]{:S(2)}, u32[]{:S(2)}) collective-permute-start(f32[16,64,1]{2,1,0:T(8,128)} %get-tuple-element.65), channel_id=1, source_target_pairs={{0,1},{1,2},{2,3},{3,4},{4,5},{5,6},{6,7},{7,8},{8,9},{9,10},{10,1... | collective-permute-start | bytes 12296 | tf_op jit(solution)/shard_map/ppermute | solution.py:26
  121.9 5.5 %copy-start.14 = (f32[3,16,64,1]{3,2,1,0:T(8,128)S(1)}, f32[3,16,64,1]{3,2,1,0:T(8,128)}, u32[]{:S(2)}) copy-start(f32[3,16,64,1]{3,2,1,0:T(8,128)} %copy.86) | copy-start | bytes 36868
  122.9 4.5 %copy-start.5 = (f32[3,16,64,128]{3,2,0,1:T(8,128)S(1)}, f32[3,16,64,128]{3,2,0,1:T(8,128)}, u32[]{:S(2)}) copy-start(f32[3,16,64,128]{3,2,0,1:T(8,128)} %get-tuple-element.39) | copy-start | bytes 4718596
  122.9 4.5 %copy-start.13 = (f32[3,16,64,1]{3,2,1,0:T(8,128)S(1)}, f32[3,16,64,1]{3,2,1,0:T(8,128)}, u32[]{:S(2)}) copy-start(f32[3,16,64,1]{3,2,1,0:T(8,128)} %copy.84) | copy-start | bytes 36868
  193.2 9.2 %collective-permute-start.9 = (f32[3,16,64,1]{2,1,3,0:T(8,128)S(1)}, f32[3,16,64,1]{2,1,3,0:T(8,128)S(1)}, u32[]{:S(2)}, u32[]{:S(2)}) collective-permute-start(f32[3,16,64,1]{2,1,3,0:T(8,128)S(1)} %copy.97), channel_id=1, source_target_pairs={{1,0},{2,1},{3,2},{4,3},{5,4},{6,5},{7,6},{8,7},{9,8},{10,9},{11,1... | collective-permute-start | bytes 36872 | tf_op jit(solution)/shard_map/ppermute | solution.py:28
  196.4 7.7 %collective-permute-start.8 = (f32[3,16,64,1]{2,1,3,0:T(8,128)S(1)}, f32[3,16,64,1]{2,1,3,0:T(8,128)S(1)}, u32[]{:S(2)}, u32[]{:S(2)}) collective-permute-start(f32[3,16,64,1]{2,1,3,0:T(8,128)S(1)} %copy.96), channel_id=1, source_target_pairs={{0,1},{1,2},{2,3},{3,4},{4,5},{5,6},{6,7},{7,8},{8,9},{9,10},{10,1... | collective-permute-start | bytes 36872 | tf_op jit(solution)/shard_map/ppermute | solution.py:26
  211.2 8.0 %copy-start.20 = (f32[16,64,128]{2,1,0:T(8,128)S(1)}, f32[16,64,128]{2,1,0:T(8,128)}, u32[]{:S(2)}) copy-start(f32[16,64,128]{2,1,0:T(8,128)} %param.10) | copy-start | bytes 1572868
  212.4 14.5 %collective-permute-start.10 = (f32[16,64,1]{2,1,0:T(8,128)}, f32[16,64,1]{2,1,0:T(8,128)}, u32[]{:S(2)}, u32[]{:S(2)}) collective-permute-start(f32[16,64,1]{2,1,0:T(8,128)} %get-tuple-element.64), channel_id=1, source_target_pairs={{1,0},{2,1},{3,2},{4,3},{5,4},{6,5},{7,6},{8,7},{9,8},{10,9},{11,1... | collective-permute-start | bytes 12296 | tf_op jit(solution)/shard_map/ppermute | solution.py:28
  213.6 13.2 %collective-permute-start.11 = (f32[16,64,1]{2,1,0:T(8,128)}, f32[16,64,1]{2,1,0:T(8,128)}, u32[]{:S(2)}, u32[]{:S(2)}) collective-permute-start(f32[16,64,1]{2,1,0:T(8,128)} %get-tuple-element.63), channel_id=1, source_target_pairs={{0,1},{1,2},{2,3},{3,4},{4,5},{5,6},{6,7},{7,8},{8,9},{9,10},{10,1... | collective-permute-start | bytes 12296 | tf_op jit(solution)/shard_map/ppermute | solution.py:26
  229.2 3.5 %copy-start.24 = (f32[1,16,64,128]{3,2,0,1:T(8,128)}, f32[1,16,64,128]{3,2,0,1:T(8,128)S(1)}, u32[]{:S(2)}) copy-start(f32[1,16,64,128]{3,2,0,1:T(8,128)S(1)} %get-tuple-element.57) | copy-start | bytes 1572868
  229.2 3.5 %copy-start.26 = (f32[1,16,64,128]{3,2,0,1:T(8,128)}, f32[1,16,64,128]{3,2,0,1:T(8,128)S(1)}, u32[]{:S(2)}) copy-start(f32[1,16,64,128]{3,2,0,1:T(8,128)S(1)} %get-tuple-element.58) | copy-start | bytes 1572868
  278.9 2.8 copy-start.15
  278.9 2.9 copy-start.25
  278.9 3.0 copy-start.27
  278.9 3.2 copy-start.29
  282.8 40.9 %copy-start.30 = (f32[2,64]{1,0:T(2,128)S(1)}, f32[2,64]{1,0:T(2,128)}, u32[]{:S(2)}) copy-start(f32[2,64]{1,0:T(2,128)} %param.14) | copy-start | bytes 1540
  282.9 40.9 %copy-start.33 = (f32[64]{0:T(128)S(1)}, f32[64]{0:T(128)}, u32[]{:S(2)}) copy-start(f32[64]{0:T(128)} %param.13) | copy-start | bytes 772
  282.9 40.9 %copy-start.34 = (s32[64]{0:T(128)S(1)}, s32[64]{0:T(128)}, u32[]{:S(2)}) copy-start(s32[64]{0:T(128)} %param.12) | copy-start | bytes 772
  (15 other events, 27.0 us)
where the time goes:
time: 327 us; the launch traced here: 326 us
  blocking collectives  188 us (57%)
  other arithmetic  53.7 us (16%)
  local copies, waits for them, and re-layouts  37.7 us (12%)
  starting transfers between devices  31.5 us (10%)
  between operations  8.05 us (2%)
  waiting for transfers between devices  6.56 us (2%)
    psum x2, blocking collectives, shards(): lax.psum((jnp.sum(direction * image), jnp.sum(solved * image), jnp.sum(im...  97.5 us
    psum x1, blocking collectives, shards(): norm_now = lax.psum(jnp.sum(solved * solved), ('len', 'xs'))  51.1 us
    psum x1, blocking collectives, shards(): lax.psum(jnp.sum(picked * across_hit[None], axis=1), ('len', 'xs'))  39.3 us
    ppermute x6, starting transfers between devices, extended_2(): lax.ppermute(tail, axis, [(i, (i + 1) % count) for i in range(ends)])  23.5 us
    concatenate x6, other arithmetic, extended_2(): jnp.concatenate([lax.ppermute(tail, axis, [(i, (i + 1) % count) for i in...  16.4 us
    slice x8, local copies, waits for them, and re-layouts, extended_2(): lax.slice_in_dim(cells, cells.shape[dim] - width, cells.shape[dim], axis=...  13.3 us
    add x2, other arithmetic, operate(): mass_field[None] * field + shear_modulus * laplacian  11.5 us
    ppermute x6, starting transfers between devices, extended_2(): lax.ppermute(head, axis, [((i + 1) % count, i) for i in range(ends)])  8.06 us
  transfers between devices with their start and end apart: 12, of which 3 were waited for; matrix products, arithmetic and copies ran while one was open for 7% of the time, Pallas kernels for 0%

commit v1 on v0

v1 whole, which is shorter than its diff:
```python
import functools

import jax
import jax.numpy as jnp
from jax import lax
from jax.experimental import pallas as pl
from jax.experimental.pallas import tpu as pltpu
from jax.sharding import PartitionSpec as P

ITERS = 3
SHIFT = 4.0
BULK = 1.5
ELASTIC = 8.0
RADIUS = 4.0
VERTICAL = 5.0
STATIC = 0.6
KINETIC = 0.45

AXES = ("len", "xs")
LANES = 128
PAD = 8
GROUP = 8
CHUNK = 16
HIGH = lax.Precision.HIGHEST


def turn(x, amount):
    return pltpu.roll(x, amount % LANES, x.ndim - 1)


def lane_iota(shape):
    return lax.broadcasted_iota(jnp.int32, shape, len(shape) - 1)


def pack_kernel(
    right_hbm, mass_hbm, spans, even,
    field, mass, message_a, message_b, ends,
    sems,
):
    depth, across = mass.shape[0], mass.shape[1]
    copies = [
        pltpu.make_async_copy(
            right_hbm.at[c], field.at[c, pl.ds(1, depth), pl.ds(PAD, across)], sems.at[c]
        )
        for c in range(3)
    ]
    copies.append(pltpu.make_async_copy(mass_hbm, mass, sems.at[3]))
    for copy in copies:
        copy.start()
    for c in range(3):
        for slab in (0, depth + 1):
            field[c, slab] = jnp.zeros(field.shape[2:], jnp.float32)

        def clear(d, carry, c=c):
            blank = jnp.zeros((PAD, LANES), jnp.float32)
            field[c, d, 0:PAD, :] = blank
            field[c, d, PAD + across :, :] = blank
            return carry

        lax.fori_loop(1, depth + 1, clear, 0)
    piers = spans.shape[1]
    bearings = 2 * piers
    variants = ends.shape[0]
    lane = lane_iota((piers, LANES))
    pier = lax.broadcasted_iota(jnp.int32, (piers, LANES), 0)
    lengths = jnp.broadcast_to(spans[...].astype(jnp.float32), (8, piers))
    for z in range(variants):
        if bearings <= LANES:
            bearing = lane - z * bearings
        else:
            bearing = lane + z * LANES
        upto = jnp.where(pier * 2 <= bearing, 1.0, 0.0)
        total = jnp.dot(lengths, upto, precision=HIGH, preferred_element_type=jnp.float32)
        inside = (bearing[0:1] >= 0) & (bearing[0:1] < bearings)
        ends[z : z + 1, :] = jnp.where(inside, total[0:1] - 1.0, -1e9)
    spot = lane_iota((across, LANES))
    is_even = even[0, 0] == 1
    for c in range(4):
        copies[c].wait()
        upper = jnp.zeros((across, LANES), jnp.float32)
        lower = jnp.zeros((across, LANES), jnp.float32)
        for d in range(depth):
            slab = field[c, d + 1, PAD : PAD + across, :] if c < 3 else mass[d]
            mine = (spot >= GROUP * d) & (spot < GROUP * (d + 1))
            upper = jnp.where(mine, turn(slab, GROUP * d + 6), upper)
            lower = jnp.where(mine, turn(slab, GROUP * d + 2), lower)
        message_a[c] = jnp.where(is_even, upper, lower)
        message_b[c] = jnp.where(is_even, lower, upper)


def basis_kernel(
    info, field, mass, message_a, message_b, got_a, got_b, ends,
    first, second, third, payload,
    div, packed, packed_div, edge, inner, packed_diag, sums, picked,
):
    depth, across = mass.shape[0], mass.shape[1]
    is_even = info[0, 0] == 1
    has = (info[0, 1].astype(jnp.float32), info[0, 2].astype(jnp.float32))
    start = info[0, 3].astype(jnp.float32)
    rows = pl.ds(PAD, across)
    above = pl.ds(PAD + 1, across)
    below = pl.ds(PAD - 1, across)
    spot = lane_iota((across, LANES))
    plane = spot % GROUP

    def blank_edges(ref, leading):
        for at in leading:
            ref[at + (slice(0, PAD),)] = jnp.zeros((PAD, LANES), jnp.float32)
            ref[at + (slice(PAD + across, None),)] = jnp.zeros((PAD, LANES), jnp.float32)

    blank_edges(packed, [(s, c) for s in range(2) for c in range(3)])
    blank_edges(packed_div, [(s,) for s in range(2)])
    for ref in (first, second):
        for c in range(3):
            ref[c, 0] = jnp.zeros(ref.shape[2:], jnp.float32)
            ref[c, depth + 1] = jnp.zeros(ref.shape[2:], jnp.float32)
    div[0] = jnp.zeros(div.shape[1:], jnp.float32)
    div[depth + 1] = jnp.zeros(div.shape[1:], jnp.float32)

    def clear(d, carry):
        blank = jnp.zeros((PAD, LANES), jnp.float32)
        for c in range(3):
            for ref in (first, second):
                ref[c, d, 0:PAD, :] = blank
                ref[c, d, PAD + across :, :] = blank
        div[d, 0:PAD, :] = blank
        div[d, PAD + across :, :] = blank
        return carry

    lax.fori_loop(1, depth + 1, clear, 0)

    for c in range(4):
        mine_a, mine_b, from_a, from_b = message_a[c], message_b[c], got_a[c], got_b[c]
        own_upper = jnp.where(is_even, mine_a, mine_b)
        own_lower = jnp.where(is_even, mine_b, mine_a)
        left = jnp.where(plane < 6, jnp.where(is_even, from_b, from_a), own_upper)
        right = jnp.where(plane < 2, own_lower, jnp.where(is_even, from_a, from_b))
        if c < 3:
            packed[0, c, rows, :] = left
            packed[1, c, rows, :] = right
        else:
            packed_diag[0] = left + (6.0 - SHIFT)
            packed_diag[1] = right + (6.0 - SHIFT)

    def deeper(x):
        return jnp.where(spot < LANES - GROUP, turn(x, -GROUP), 0.0)

    def shallower(x):
        return jnp.where(spot >= GROUP, turn(x, GROUP), 0.0)

    def packed_divergence():
        for s in range(2):
            x0 = packed[s, 0, rows, :]
            x2 = packed[s, 2, rows, :]
            w = turn(x0, -1) - turn(x0, 1)
            w = w + (packed[s, 1, above, :] - packed[s, 1, below, :])
            w = w + (deeper(x2) - shallower(x2))
            packed_div[s, rows, :] = w * (0.25 * BULK * has[s])

    def fill_edge():
        for c in range(3):
            edge[c] = jnp.where(plane == 5, packed[0, c, rows, :], turn(packed[1, c, rows, :], 2))
        edge[3] = jnp.where(plane == 5, packed_div[0, rows, :], turn(packed_div[1, rows, :], 2))

    def packed_step():
        for s in range(2):
            w = packed_div[s, rows, :]
            slopes = (
                turn(w, -1) - turn(w, 1),
                packed_div[s, above, :] - packed_div[s, below, :],
                deeper(w) - shallower(w),
            )
            for c in range(3):
                x = packed[s, c, rows, :]
                total = (turn(x, -1) + turn(x, 1)) + (deeper(x) + shallower(x))
                total = total + (packed[s, c, above, :] + packed[s, c, below, :])
                image = packed_diag[s] * x - total - slopes[c]
                packed[s, c, rows, :] = image * has[s]

    def insert_inner():
        for c in range(3):
            own = inner[c]
            packed[0, c, rows, :] = jnp.where(plane < 6, packed[0, c, rows, :], own)
            packed[1, c, rows, :] = jnp.where(plane < 2, turn(own, -4), packed[1, c, rows, :])

    zero_sum = jnp.zeros((8, LANES), jnp.float32)
    chunks = range(0, across, CHUNK)

    def folded(x):
        return sum(x[i : i + 8] for i in range(0, CHUNK, 8))

    def step(source, target, target_pad, last):
        lane = lane_iota((CHUNK, LANES))
        at_left = lane == 0
        at_right = lane == LANES - 1

        def both(x, beside):
            return (
                jnp.where(at_left, beside, turn(x, 1)),
                jnp.where(at_right, beside, turn(x, -1)),
            )

        def divergence(d, carry):
            amount = LANES - 5 - GROUP * d
            for r in chunks:
                here = pl.ds(PAD + r, CHUNK)
                beside = pltpu.roll(edge[0, r : r + CHUNK, :], amount, 1)
                left, right = both(source[0, d + 1, here, :], beside)
                w = right - left
                w = w + (
                    source[1, d + 1, pl.ds(PAD + r + 1, CHUNK), :]
                    - source[1, d + 1, pl.ds(PAD + r - 1, CHUNK), :]
                )
                w = w + (source[2, d + 2, here, :] - source[2, d, here, :])
                div[d + 1, here, :] = w * (0.25 * BULK)
            return carry

        lax.fori_loop(0, depth, divergence, 0)

        def image(d, carry):
            norm, cross = carry
            amount = LANES - 5 - GROUP * d
            place = GROUP * d + 6
            mine = (lane >= GROUP * d + 4) & (lane < GROUP * d + 8)
            for r in chunks:
                here = pl.ds(PAD + r, CHUNK)
                up = pl.ds(PAD + r + 1, CHUNK)
                down = pl.ds(PAD + r - 1, CHUNK)
                diag = mass[d, r : r + CHUNK, :] + (6.0 - SHIFT)
                w_left, w_right = both(
                    div[d + 1, here, :], pltpu.roll(edge[3, r : r + CHUNK, :], amount, 1)
                )
                slopes = (
                    w_right - w_left,
                    div[d + 1, up, :] - div[d + 1, down, :],
                    div[d + 2, here, :] - div[d, here, :],
                )
                for c in range(3):
                    x = source[c, d + 1, here, :]
                    left, right = both(x, pltpu.roll(edge[c, r : r + CHUNK, :], amount, 1))
                    total = (left + right) + (source[c, d, here, :] + source[c, d + 2, here, :])
                    total = total + (source[c, d + 1, up, :] + source[c, d + 1, down, :])
                    out = diag * x - total - slopes[c]
                    target[c, d + target_pad[0], pl.ds(target_pad[1] + r, CHUNK), :] = out
                    if not last:
                        inner[c, r : r + CHUNK, :] = jnp.where(
                            mine, pltpu.roll(out, lax.rem(place, LANES), 1), inner[c, r : r + CHUNK, :]
                        )
                    norm = norm + folded(x * x)
                    cross = cross + folded(x * out)
            return norm, cross

        return lax.fori_loop(0, depth, image, (zero_sum, zero_sum))

    packed_divergence()
    fill_edge()
    moments = list(step(field, first, (1, PAD), False))
    packed_step()
    insert_inner()
    packed_divergence()
    fill_edge()
    moments += step(first, second, (1, PAD), False)
    packed_step()
    insert_inner()
    packed_divergence()
    fill_edge()
    moments += step(second, third, (0, 0), True)

    variants = ends.shape[0]
    per = payload_per(variants, info)
    pieces = 1 if per > 1 else variants
    blocks = 9 * pieces
    bearing_rows = -(-blocks // per)
    picked[...] = jnp.zeros(picked.shape, jnp.float32)
    for block in range(blocks):
        value, piece = block // pieces, block % pieces
        row, z = block // per, (block % per if per > 1 else piece)
        ref, c = (field, first, second)[value // 3], value % 3
        for side in range(2):
            at = PAD + (1 + 2 * side) * across // 4
            column = (2 * z + side) * LANES
            picked[row : row + 1, column : column + LANES] = ref[c, 1, at : at + 1, :]
    along = lax.broadcasted_iota(jnp.int32, (LANES, LANES), 0).astype(jnp.float32) + start
    parity = lane_iota((LANES, LANES)) % 2
    total = jnp.zeros((picked.shape[0], LANES), jnp.float32)
    for z in range(variants):
        site = jnp.broadcast_to(ends[z : z + 1, :], (LANES, LANES)) == along
        for side in range(2):
            column = (2 * z + side) * LANES
            hit = jnp.where(site & (parity == side), 1.0, 0.0)
            total = total + jnp.dot(
                picked[:, column : column + LANES], hit,
                precision=HIGH, preferred_element_type=jnp.float32,
            )
    sums[...] = jnp.zeros(sums.shape, jnp.float32)
    sums[0:bearing_rows, :] = total[0:bearing_rows]
    low = lane_iota((1, LANES)) < LANES // 2
    for pair in range(3):
        halves = []
        for moment in moments[2 * pair : 2 * pair + 2]:
            flat = jnp.sum(moment, axis=0, keepdims=True)
            halves.append(flat + turn(flat, LANES // 2))
        sums[bearing_rows + pair : bearing_rows + pair + 1, :] = jnp.where(low, *halves)
    out = sums[...]
    for device in range(payload.shape[0]):
        payload[device] = out


def payload_per(variants, info):
    return info.shape[1] - 4


def coefficients(moment):
    def dot(a, b):
        total = None
        for i, left in enumerate(a):
            for j, right in enumerate(b):
                term = left * right * moment[i + j]
                total = term if total is None else total + term
        return total

    one = jnp.ones_like(moment[0])
    solved, direction, increment = [one], [one], []
    norm = moment[0]
    for iteration in range(ITERS):
        image = [SHIFT * p for p in direction] + [jnp.zeros_like(one)]
        for i, p in enumerate(direction):
            image[i + 1] = image[i + 1] + p
        alpha = norm / dot(direction, image)
        increment = [
            alpha * p + (increment[i] if i < len(increment) else 0.0) for i, p in enumerate(direction)
        ]
        solved = [
            (solved[i] if i < len(solved) else 0.0) - alpha * q for i, q in enumerate(image)
        ]
        if iteration + 1 < ITERS:
            after = dot(solved, solved)
            ratio = after / norm
            direction = [
                s + (ratio * direction[i] if i < len(direction) else 0.0)
                for i, s in enumerate(solved)
            ]
            norm = after
    return increment, solved


def combine_kernel(
    info, gathered, field, first, second, third, ends, stick, load, prior,
    increment_hbm, residual_hbm, friction,
    increment, residual, forces, sems,
):
    depth, across = third.shape[1], third.shape[2]
    start = info[0, 3].astype(jnp.float32)
    bearings = load.shape[1]
    variants = ends.shape[0]
    per = payload_per(variants, info)
    pieces = 1 if per > 1 else variants
    width = min(bearings, LANES)
    bearing_rows = -(-9 * pieces // per)
    parts = [gathered[i] for i in range(gathered.shape[0])]
    while len(parts) > 1:
        parts = [sum(parts[i : i + 2]) for i in range(0, len(parts), 2)]
    total = parts[0]
    low = lane_iota((1, LANES)) < LANES // 2
    moments = []
    for n in range(6):
        row = total[bearing_rows + n // 2 : bearing_rows + n // 2 + 1]
        row = jnp.where(low == (n % 2 == 0), row, 0.0)
        moments.append(jnp.sum(row, axis=1, keepdims=True))
    grow, keep = coefficients(moments)

    forces[...] = jnp.zeros(forces.shape, jnp.float32)
    lane = lane_iota((1, width))
    for piece in range(pieces):
        span = slice(piece * LANES, piece * LANES + width)
        readout = []
        for c in range(3):
            value = None
            for k in range(ITERS):
                block = (3 * k + c) * pieces + piece
                row = total[block // per : block // per + 1]
                if per > 1 and block % per:
                    row = turn(row, LANES - (block % per) * bearings)
                term = grow[k] * row[:, :width]
                value = term if value is None else value + term
            readout.append(value)
        weight = load[:, span]
        radius = jnp.where(stick[:, span] == 1, STATIC, KINETIC) * weight
        trial = [prior[c : c + 1, span] + ELASTIC * readout[c] for c in range(2)]
        magnitude = jnp.sqrt(trial[0] * trial[0] + trial[1] * trial[1])
        scale = radius / jnp.maximum(magnitude, radius)
        held = [t * scale for t in trial]
        for c in range(2):
            friction[c : c + 1, span] = held[c]
        force = [held[c] + weight / RADIUS * readout[c] for c in range(2)] + [VERTICAL * readout[2]]
        for c in range(3):
            for side in range(2):
                forces[2 * c + side : 2 * c + side + 1, span] = jnp.where(
                    lane % 2 == side, force[c], 0.0
                )
    along = lax.broadcasted_iota(jnp.int32, (LANES, LANES), 0).astype(jnp.float32) + start
    placed = jnp.zeros((8, LANES), jnp.float32)
    for piece in range(pieces):
        site = jnp.broadcast_to(ends[piece : piece + 1, :], (LANES, LANES)) == along
        placed = placed + lax.dot_general(
            forces[:, piece * LANES : (piece + 1) * LANES], jnp.where(site, 1.0, 0.0),
            (((1,), (1,)), ((), ())), precision=HIGH, preferred_element_type=jnp.float32,
        )

    grow = [jnp.broadcast_to(g, (CHUNK, LANES)) for g in grow]
    keep = [jnp.broadcast_to(g, (CHUNK, LANES)) for g in keep]

    def level(d, c):
        for r in range(0, across, CHUNK):
            here = pl.ds(PAD + r, CHUNK)
            v = [ref[c, d + 1, here, :] for ref in (field, first, second)]
            v.append(third[c, d, r : r + CHUNK, :])
            increment[c, d, r : r + CHUNK, :] = grow[0] * v[0] + grow[1] * v[1] + grow[2] * v[2]
            residual[c, d, r : r + CHUNK, :] = (
                keep[0] * v[0] + keep[1] * v[1] + (keep[2] * v[2] + keep[3] * v[3])
            )

    def run(c, begin, end):
        def body(d, carry):
            level(d, c)
            return carry

        lax.fori_loop(begin, end, body, 0)

    copies = []

    def send(c, begin, end):
        for which, (ref, hbm) in enumerate(((increment, increment_hbm), (residual, residual_hbm))):
            part = pl.ds(begin, end - begin)
            copy = pltpu.make_async_copy(
                ref.at[c, part], hbm.at[c, part], sems.at[which, 2 * c + (begin > 0)]
            )
            copy.start()
            copies.append(copy)

    half = depth // 2
    for c in range(3):
        run(c, 0, half)
        for side in range(2):
            at = (1 + 2 * side) * across // 4
            residual[c, 0, at : at + 1, :] = (
                residual[c, 0, at : at + 1, :] - placed[2 * c + side : 2 * c + side + 1]
            )
        send(c, 0, half)
        run(c, half, depth)
        send(c, half, depth)
    for copy in copies:
        copy.wait()


def vmem_spec():
    return pl.BlockSpec(memory_space=pltpu.VMEM)


def smem_spec():
    return pl.BlockSpec(memory_space=pltpu.SMEM)


def shards(count, right_side, mass_field, span_lengths, stick_flags, normal_load, prior_friction):
    f32 = jnp.float32
    depth, across, along = right_side.shape[1:]
    piers = span_lengths.shape[0]
    bearings = 2 * piers
    per = LANES // bearings if bearings <= LANES else 1
    variants = per if bearings <= LANES else bearings // LANES
    pieces = 1 if per > 1 else variants
    bearing_rows = -(-9 * pieces // per)
    rows = -(-(bearing_rows + 3) // 8) * 8
    pick_rows = -(-bearing_rows // 8) * 8
    index = lax.axis_index(AXES)
    even = (index % 2 == 0).astype(jnp.int32).reshape(1, 1)
    padded = (depth + 2, across + 2 * PAD, along)
    limit = pltpu.CompilerParams(vmem_limit_bytes=32 * 1024 * 1024)
    field, mass, message_a, message_b, ends = pl.pallas_call(
        pack_kernel,
        out_shape=(
            pltpu.VMEM((3,) + padded, f32),
            pltpu.VMEM((depth, across, along), f32),
            jax.ShapeDtypeStruct((4, across, LANES), f32),
            jax.ShapeDtypeStruct((4, across, LANES), f32),
            jax.ShapeDtypeStruct((variants, LANES), f32),
        ),
        in_specs=[
            pl.BlockSpec(memory_space=pl.ANY), pl.BlockSpec(memory_space=pl.ANY),
            vmem_spec(), smem_spec(),
        ],
        out_specs=(vmem_spec(),) * 5,
        scratch_shapes=[pltpu.SemaphoreType.DMA((4,))],
        compiler_params=limit,
        name="pack",
    )(right_side, mass_field, span_lengths.reshape(1, piers), even)

    pairs_a = [p for i in range(0, count - 1, 2) for p in ((i, i + 1), (i + 1, i))]
    pairs_b = [p for i in range(1, count - 1, 2) for p in ((i, i + 1), (i + 1, i))]
    got_b = lax.ppermute(message_b, AXES, pairs_b)
    got_a = lax.ppermute(message_a, AXES, pairs_a)

    info = jnp.stack(
        [
            (index % 2 == 0).astype(jnp.int32),
            (index > 0).astype(jnp.int32),
            (index < count - 1).astype(jnp.int32),
            (index * along).astype(jnp.int32),
        ]
        + [jnp.int32(0)] * per
    ).reshape(1, 4 + per)
    first, second, third, payload = pl.pallas_call(
        basis_kernel,
        out_shape=(
            pltpu.VMEM((3,) + padded, f32),
            pltpu.VMEM((3,) + padded, f32),
            pltpu.VMEM((3, depth, across, along), f32),
            jax.ShapeDtypeStruct((count, rows, LANES), f32),
        ),
        in_specs=[smem_spec()] + [vmem_spec()] * 7,
        out_specs=(vmem_spec(),) * 4,
        scratch_shapes=[
            pltpu.VMEM(padded, f32),
            pltpu.VMEM((2, 3, across + 2 * PAD, LANES), f32),
            pltpu.VMEM((2, across + 2 * PAD, LANES), f32),
            pltpu.VMEM((4, across, LANES), f32),
            pltpu.VMEM((3, across, LANES), f32),
            pltpu.VMEM((2, across, LANES), f32),
            pltpu.VMEM((rows, LANES), f32),
            pltpu.VMEM((pick_rows, 2 * variants * LANES), f32),
        ],
        compiler_params=limit,
        name="basis",
    )(info, field, mass, message_a, message_b, got_a, got_b, ends)

    gathered = lax.all_to_all(payload, AXES, 0, 0)

    increment, residual, friction = pl.pallas_call(
        combine_kernel,
        out_shape=(
            jax.ShapeDtypeStruct(right_side.shape, f32),
            jax.ShapeDtypeStruct(right_side.shape, f32),
            jax.ShapeDtypeStruct((2, bearings), f32),
        ),
        in_specs=[smem_spec()] + [vmem_spec()] * 9,
        out_specs=(
            pl.BlockSpec(memory_space=pl.ANY), pl.BlockSpec(memory_space=pl.ANY), vmem_spec(),
        ),
        scratch_shapes=[
            pltpu.VMEM(right_side.shape, f32),
            pltpu.VMEM(right_side.shape, f32),
            pltpu.VMEM((8, pieces * LANES), f32),
            pltpu.SemaphoreType.DMA((2, 6)),
        ],
        compiler_params=limit,
        name="combine",
    )(
        info, gathered, field, first, second, third, ends,
        stick_flags.reshape(1, bearings), normal_load.reshape(1, bearings), prior_friction,
    )
    return increment, residual, friction


def solution(mesh):
    count = mesh.shape["len"] * mesh.shape["xs"]
    along = P(None, None, None, AXES)
    in_specs = (along, P(None, None, AXES), P(), P(), P(), P())
    return jax.shard_map(
        functools.partial(shards, count), mesh=mesh,
        in_specs=in_specs, out_specs=(along, along, P()), check_vma=False,
    )
```

time: 327 us -> 51.1 us (0.16)
  blocking collectives: 188 us -> 21.1 us
  other arithmetic: 53.7 us -> 0 us
  local copies, waits for them, and re-layouts: 37.7 us -> 3.2 us
  starting transfers between devices: 31.5 us -> 1.17 us
  Pallas kernels: 0 us -> 24.5 us
  between operations: 8.05 us -> 0.71 us
  waiting for transfers between devices: 6.56 us -> 0.22 us
    psum x4 -> x0, blocking collectives: 188 us -> none  [the longest x2 97.5 us: shards(): lax.psum((jnp.sum(direction * image), jnp.sum(solved * image), jnp.sum(im...]
    ppermute x12 -> x2, starting transfers between devices: 31.5 us -> 1.17 us  [the longest x1 0.66 us: shards(): got_b = lax.ppermute(message_b, AXES, pairs_b)]
    pallas_call x0 -> x3, Pallas kernels: none -> 24.5 us  [the longest x1 19.1 us: shards(): pl.pallas_call(basis_kernel, out_shape=(pltpu.VMEM((3,) + padded, f32), p...]
    add x11 -> x0, other arithmetic: 22.8 us -> none  [the longest x2 11.5 us: operate(): mass_field[None] * field + shear_modulus * laplacian]
    all_to_all x0 -> x1, blocking collectives: none -> 21.1 us  [shards(): gathered = lax.all_to_all(payload, AXES, 0, 0)]
    slice x10 -> x0, local copies, waits for them, and re-layouts: 17.1 us -> none  [the longest x8 13.3 us: extended_2(): lax.slice_in_dim(cells, cells.shape[dim] - width, cells.shape[dim], axis=...]
    concatenate x7 -> x0, other arithmetic: 16.4 us -> none  [the longest x6 16.4 us: extended_2(): jnp.concatenate([lax.ppermute(tail, axis, [(i, (i + 1) % count) for i in...]
    ppermute x6 -> x0, local copies, waits for them, and re-layouts: 9.09 us -> none  [the longest x3 5.12 us: extended_2(): lax.ppermute(head, axis, [((i + 1) % count, i) for i in range(ends)])]
  transfers between devices with their start and end apart: 12 -> 2, of which waited for: 3 -> 1; matrix products, arithmetic and copies ran while one was open for 7% -> 0% of each run, Pallas kernels for 0% -> 0%
where the time goes in v1:
time: 51.1 us; the launch traced here: 50.8 us
  Pallas kernels  24.5 us (48%)
  blocking collectives  21.1 us (41%)
  local copies, waits for them, and re-layouts  3.2 us (6%)
  starting transfers between devices  1.17 us (2%)
  between operations  0.71 us (1%)
    all_to_all x1, blocking collectives, shards(): gathered = lax.all_to_all(payload, AXES, 0, 0)  21.1 us
    pallas_call x1, Pallas kernels, shards(): pl.pallas_call(basis_kernel, out_shape=(pltpu.VMEM((3,) + padded, f32), p...  19.1 us
    pallas_call x1, Pallas kernels, shards(): pl.pallas_call(combine_kernel, out_shape=(jax.ShapeDtypeStruct(right_side...  3.46 us
    unnamed x12, local copies, waits for them, and re-layouts  3.11 us
    pallas_call x1, Pallas kernels, shards(): pl.pallas_call(pack_kernel, out_shape=(pltpu.VMEM((3,) + padded, f32), pl...  1.98 us
  transfers between devices with their start and end apart: 2, of which 1 were waited for; matrix products, arithmetic and copies ran while one was open for 0% of the time, Pallas kernels for 0%

profile of v1, /device:TPU:0, one launch (start us, length us, event | category | flops | bytes accessed | tf_op | source)
XLA Modules:
  0.0 50.8 jit_solution(593934942853842228)
XLA Ops:
  0.6 0.0 copy-start
  0.7 1.4 %copy-done = f32[3,16,64,128]{3,2,1,0:T(8,128)S(1)} copy-done((f32[3,16,64,128]{3,2,1,0:T(8,128)S(1)}, f32[3,16,64,128]{3,2,1,0:T(8,128)}, u32[]{:S(2)}) %copy-start) | copy-done | bytes 1572888
  2.1 0.0 copy-start.1
  2.1 1.0 %copy-done.1 = f32[16,64,128]{2,1,0:T(8,128)S(1)} copy-done((f32[16,64,128]{2,1,0:T(8,128)S(1)}, f32[16,64,128]{2,1,0:T(8,128)}, u32[]{:S(2)}) %copy-start.1) | copy-done | bytes 524312
  3.1 0.0 copy-start.5
  3.1 0.7 %copy-done.5 = s32[32]{0:T(128)S(1)} copy-done((s32[32]{0:T(128)S(1)}, s32[32]{0:T(128)}, u32[]{:S(2)}) %copy-start.5) | copy-done | bytes 152
  3.8 2.0 %pack.1 = (f32[3,18,80,128]{3,2,1,0:T(8,128)S(1)}, f32[16,64,128]{2,1,0:T(8,128)S(1)}, f32[4,64,128]{2,1,0:T(8,128)S(1)}, f32[4,64,128]{2,1,0:T(8,128)S(1)}, f32[2,128]{1,0:T(2,128)S(1)}) custom-call(f32[3,16,64,128]{3,2,1,0:T(8,128)S(1)} %copy-done, f32[16,64,128]{2,1,0:T(8,128)S(1)} %copy-done.1, s32[1,32]{1,0:T(1,128)S(1)} %bitcast.13, s32[1,1]{1,0:T(1,128)} %bitcast.6.even), custom_call_target="tpu_custom_call" | custom-call | tf_op jit(solution)/shard_map/pack/pallas_call | solution.py:479
  5.7 0.5 %collective-permute-start = (f32[4,64,128]{2,1,0:T(8,128)S(1)}, f32[4,64,128]{2,1,0:T(8,128)S(1)}, u32[]{:S(2)}, u32[]{:S(2)}) collective-permute-start(f32[4,64,128]{2,1,0:T(8,128)S(1)} %get-tuple-element.14.message_a), channel_id=1, source_target_pairs={{0,1},{1,0},{2,3},{3,2},{4,5},{5,4},{6,7},{7,6},{8,9},{9,8},{10,11... | collective-permute-start | bytes 393224 | tf_op jit(solution)/shard_map/ppermute | solution.py:501
  6.3 0.7 %collective-permute-start.1 = (f32[4,64,128]{2,1,0:T(8,128)S(1)}, f32[4,64,128]{2,1,0:T(8,128)S(1)}, u32[]{:S(2)}, u32[]{:S(2)}) collective-permute-start(f32[4,64,128]{2,1,0:T(8,128)S(1)} %get-tuple-element.15.message_b), channel_id=1, source_target_pairs={{1,2},{2,1},{3,4},{4,3},{5,6},{6,5},{7,8},{8,7},{9,10},{10,9},{11,... | collective-permute-start | bytes 393224 | tf_op jit(solution)/shard_map/ppermute | solution.py:500
  6.9 0.1 stack.27
  7.0 0.2 collective-permute-done.got_a
  7.2 0.0 collective-permute-done.1.got_b
  7.2 0.0 copy-start.2
  7.2 0.0 copy-start.3
  7.3 0.0 copy-start.4
  7.3 19.1 %basis.1 = (f32[3,18,80,128]{3,2,1,0:T(8,128)S(1)}, f32[3,18,80,128]{3,2,1,0:T(8,128)S(1)}, f32[3,16,64,128]{3,2,1,0:T(8,128)S(1)}, f32[32,8,128]{2,1,0:T(8,128)S(1)}) custom-call(s32[1,6]{1,0:T(1,128)S(1)} %bitcast.9, f32[3,18,80,128]{3,2,1,0:T(8,128)S(1)} %get-tuple-element.12.field, f32[16,64,128]{2,1,0:T(8,128)S(1)} %get-tuple-element.13.mass, ...), custom_call_target="tpu_custom_call" | custom-call | tf_op jit(solution)/shard_map/basis/pallas_call | solution.py:512
  26.3 21.1 %all_to_all.5.gathered = f32[32,8,128]{2,1,0:T(8,128)S(1)} all-to-all(f32[32,8,128]{2,1,0:T(8,128)S(1)} %get-tuple-element.17), channel_id=1, replica_groups=mesh['len'=8,'xs'=4] {'len','xs'}, dimensions={0} | all-to-all | bytes 262144 | tf_op jit(solution)/shard_map/all_to_all | solution.py:536
  47.4 0.0 copy-done.2
  47.4 0.0 copy-done.3
  47.4 0.0 copy-done.4
  47.4 3.5 %combine.1 = (f32[3,16,64,128]{3,2,1,0:T(8,128)}, f32[3,16,64,128]{3,2,1,0:T(8,128)}, f32[2,64]{1,0:T(2,128)}) custom-call(s32[1,6]{1,0:T(1,128)S(1)} %bitcast.10, f32[32,8,128]{2,1,0:T(8,128)S(1)} %all_to_all.5.gathered, f32[3,18,80,128]{3,2,1,0:T(8,128)S(1)} %get-tuple-element.12.field, f32[3,18,80,128]{3,2,1,0:T(8,128)S(1)} %get-tuple-element.18.first, ...), custom_call_target="tpu_custom_call" | custom-call | tf_op jit(solution)/shard_map/combine/pallas_call | solution.py:538
  (1 shorter events, 0.0 us)
Async XLA Ops:
  0.6 1.4 %copy-start = (f32[3,16,64,128]{3,2,1,0:T(8,128)S(1)}, f32[3,16,64,128]{3,2,1,0:T(8,128)}, u32[]{:S(2)}) copy-start(f32[3,16,64,128]{3,2,1,0:T(8,128)} %right_hbm.1) | copy-start | bytes 4718596
  2.1 1.0 %copy-start.1 = (f32[16,64,128]{2,1,0:T(8,128)S(1)}, f32[16,64,128]{2,1,0:T(8,128)}, u32[]{:S(2)}) copy-start(f32[16,64,128]{2,1,0:T(8,128)} %mass_hbm.1) | copy-start | bytes 1572868
  3.1 0.7 %copy-start.5 = (s32[32]{0:T(128)S(1)}, s32[32]{0:T(128)}, u32[]{:S(2)}) copy-start(s32[32]{0:T(128)} %param.8) | copy-start | bytes 388
  5.7 1.5 %collective-permute-start = (f32[4,64,128]{2,1,0:T(8,128)S(1)}, f32[4,64,128]{2,1,0:T(8,128)S(1)}, u32[]{:S(2)}, u32[]{:S(2)}) collective-permute-start(f32[4,64,128]{2,1,0:T(8,128)S(1)} %get-tuple-element.14.message_a), channel_id=1, source_target_pairs={{0,1},{1,0},{2,3},{3,2},{4,5},{5,4},{6,7},{7,6},{8,9},{9,8},{10,11... | collective-permute-start | bytes 393224 | tf_op jit(solution)/shard_map/ppermute | solution.py:501
  6.3 1.0 %collective-permute-start.1 = (f32[4,64,128]{2,1,0:T(8,128)S(1)}, f32[4,64,128]{2,1,0:T(8,128)S(1)}, u32[]{:S(2)}, u32[]{:S(2)}) collective-permute-start(f32[4,64,128]{2,1,0:T(8,128)S(1)} %get-tuple-element.15.message_b), channel_id=1, source_target_pairs={{1,2},{2,1},{3,4},{4,3},{5,6},{6,5},{7,8},{8,7},{9,10},{10,9},{11,... | collective-permute-start | bytes 393224 | tf_op jit(solution)/shard_map/ppermute | solution.py:500
  7.2 40.1 %copy-start.2 = (f32[2,64]{1,0:T(2,128)S(1)}, f32[2,64]{1,0:T(2,128)}, u32[]{:S(2)}) copy-start(f32[2,64]{1,0:T(2,128)} %prior.1) | copy-start | bytes 1540
  7.2 40.1 %copy-start.3 = (s32[64]{0:T(128)S(1)}, s32[64]{0:T(128)}, u32[]{:S(2)}) copy-start(s32[64]{0:T(128)} %param.9) | copy-start | bytes 772
  7.3 40.1 %copy-start.4 = (f32[64]{0:T(128)S(1)}, f32[64]{0:T(128)}, u32[]{:S(2)}) copy-start(f32[64]{0:T(128)} %param.10) | copy-start | bytes 772

commit v2 on v1

v2 whole, which is shorter than its diff:
```python
import functools

import jax
import jax.numpy as jnp
from jax import lax
from jax.experimental import pallas as pl
from jax.experimental.pallas import tpu as pltpu
from jax.sharding import PartitionSpec as P

ITERS = 3
SHIFT = 4.0
BULK = 1.5
ELASTIC = 8.0
RADIUS = 4.0
VERTICAL = 5.0
STATIC = 0.6
KINETIC = 0.45

AXES = ("len", "xs")
LANES = 128
ROWS = 8
PAD = 8
EDGE = 16
HALF = EDGE // 2
BLOCKS = LANES // EDGE
PITCH = 3 * ROWS
CHUNK = 16
HIGH = lax.Precision.HIGHEST
LIMIT = pltpu.CompilerParams(vmem_limit_bytes=32 * 1024 * 1024)


def turn(x, amount):
    return pltpu.roll(x, amount % LANES, x.ndim - 1)


def lane_iota(shape):
    return lax.broadcasted_iota(jnp.int32, shape, len(shape) - 1)


def loop(count, step, body, init):
    def several(i, carry):
        for j in range(step):
            carry = body(i * step + j, carry)
        return carry

    return lax.fori_loop(0, count // step, several, init)


def device_index():
    return lax.axis_index(AXES[0]) * lax.axis_size(AXES[1]) + lax.axis_index(AXES[1])


def clear_padding(ref, lead, depth, across):
    for slab in (0, depth + 1):
        ref[lead + (slab,)] = jnp.zeros((across + 2 * PAD, LANES), jnp.float32)
    blank = jnp.zeros((PAD, LANES), jnp.float32)
    for d in range(1, depth + 1):
        ref[lead + (d, slice(0, PAD))] = blank
        ref[lead + (d, slice(PAD + across, None))] = blank


def pack_kernel(right_hbm, mass_hbm, field, mass, packed, message_a, message_b, sems):
    depth, across = mass.shape[0], mass.shape[1]
    copies = [
        pltpu.make_async_copy(
            right_hbm.at[c], field.at[c, pl.ds(1, depth), pl.ds(PAD, across)], sems.at[c]
        )
        for c in range(3)
    ]
    copies.append(pltpu.make_async_copy(mass_hbm, mass, sems.at[3]))
    for copy in copies:
        copy.start()
    for c in range(3):
        clear_padding(field, (c,), depth, across)
    is_even = device_index() % 2 == 0
    lane = lane_iota((ROWS, LANES))
    block_of = lane // EDGE
    first_half = lane % EDGE < HALF
    for c in range(4):
        copies[c].wait()
        edges = []
        for d in range(depth):
            edge = None
            for b in range(across // ROWS):
                row = pl.ds(b * ROWS + (PAD if c < 3 else 0), ROWS)
                tile = field[c, d + 1, row, :] if c < 3 else mass[d, row, :]
                moved = turn(tile, EDGE * b + HALF)
                edge = moved if edge is None else jnp.where(block_of == b, moved, edge)
            packed[c, d] = edge
            edges.append(edge)
        for d in range(depth // 2):
            low, high = edges[d], edges[d + depth // 2]
            rightward = jnp.where(first_half, low, turn(high, HALF))
            leftward = jnp.where(first_half, turn(low, -HALF), high)
            message_a[c, d] = jnp.where(is_even, rightward, leftward)
            message_b[c, d] = jnp.where(is_even, leftward, rightward)


def folded(x):
    return sum(x[i : i + ROWS] for i in range(0, x.shape[0], ROWS))


def cyclic_step(source, mass, div, store, moments, step):
    depth, across = mass.shape[0], mass.shape[1]
    chunks = range(0, across, CHUNK)

    def divergence(d, carry):
        for r in chunks:
            here, up, down = (pl.ds(PAD + r + by, CHUNK) for by in (0, 1, -1))
            x = source[0, d + 1, here, :]
            w = turn(x, -1) - turn(x, 1)
            w = w + (source[1, d + 1, up, :] - source[1, d + 1, down, :])
            w = w + (source[2, d + 2, here, :] - source[2, d, here, :])
            div[d + 1, here, :] = w * (0.25 * BULK)
        return carry

    loop(depth, step, divergence, 0)
    lane = lane_iota((CHUNK, LANES))
    inside = (lane >= 2) & (lane < LANES - 2)

    def image(d, carry):
        norm, cross = carry
        for r in chunks:
            here, up, down = (pl.ds(PAD + r + by, CHUNK) for by in (0, 1, -1))
            diag = mass[d, r : r + CHUNK, :] + (6.0 - SHIFT)
            w = div[d + 1, here, :]
            norms, crosses = [], []
            for c in range(3):
                x = source[c, d + 1, here, :]
                if c == 0:
                    total = turn(x + w, -1) + turn(x - w, 1)
                else:
                    total = turn(x, -1) + turn(x, 1)
                if c == 1:
                    total = total + (div[d + 1, up, :] - div[d + 1, down, :])
                if c == 2:
                    total = total + (div[d + 2, here, :] - div[d, here, :])
                total = total + (source[c, d, here, :] + source[c, d + 2, here, :])
                total = total + (source[c, d + 1, up, :] + source[c, d + 1, down, :])
                out = diag * x - total
                store(c, d, r, out)
                norms.append(x * x)
                crosses.append(jnp.where(inside, x, 0.0) * out)
            norm = norm + folded(norms[0] + norms[1] + norms[2])
            cross = cross + folded(crosses[0] + crosses[1] + crosses[2])
        return norm, cross

    norm, cross = loop(depth, step, image, (jnp.zeros((ROWS, LANES), jnp.float32),) * 2)
    moments[0] = norm
    moments[1] = cross


def first_kernel(field, mass, spans, first_raw, moments, ends, div):
    depth, across = mass.shape[0], mass.shape[1]
    clear_padding(div, (), depth, across)

    def store(c, d, r, out):
        first_raw[c, d, r : r + CHUNK, :] = out

    cyclic_step(field, mass, div, store, moments, 4)
    piers = spans.shape[1]
    bearings = 2 * piers
    lane = lane_iota((piers, LANES))
    pier = lax.broadcasted_iota(jnp.int32, (piers, LANES), 0)
    lengths = jnp.broadcast_to(spans[...].astype(jnp.float32), (ROWS, piers))
    for z in range(ends.shape[0]):
        bearing = lane - z * bearings if bearings <= LANES else lane + z * LANES
        upto = jnp.where(pier * 2 <= bearing, 1.0, 0.0)
        total = jnp.dot(lengths, upto, precision=HIGH, preferred_element_type=jnp.float32)
        inside = (bearing[0:1] >= 0) & (bearing[0:1] < bearings)
        ends[z : z + 1, :] = jnp.where(inside, total[0:1] - 1.0, -1e9)


def basis_kernel(
    per, field, mass, packed, got_a, got_b, first_raw, early, ends,
    first, second, third_raw, fix, payload,
    div, edge, edge_div, edge_diag, fixes, moments, sums, picked,
):
    depth, across = mass.shape[0], mass.shape[1]
    index = device_index()
    count = lax.axis_size(AXES[0]) * lax.axis_size(AXES[1])
    is_even = index % 2 == 0
    lane = lane_iota((ROWS, LANES))
    first_half = lane % EDGE < HALF
    ones = jnp.ones((ROWS, LANES), jnp.float32)
    keep = (
        jnp.where(first_half & (index == 0), 0.0, ones),
        jnp.where(jnp.logical_not(first_half) & (index == count - 1), 0.0, ones),
    )
    both = range(2)
    comps = range(3)
    half = depth // 2
    blank = jnp.zeros((ROWS, LANES), jnp.float32)

    def row_of(d):
        return (d + 1) * PITCH + ROWS

    for c in range(4):
        for d in range(half):
            a, b = got_a[c, d], got_b[c, d]
            from_left = jnp.where(is_even, b, a)
            from_right = jnp.where(is_even, a, b)
            low, high = packed[c, d], packed[c, d + half]
            for at, left, right in (
                (
                    d,
                    jnp.where(first_half, from_left, low),
                    jnp.where(first_half, low, turn(from_right, HALF)),
                ),
                (
                    d + half,
                    jnp.where(first_half, turn(from_left, -HALF), high),
                    jnp.where(first_half, high, from_right),
                ),
            ):
                if c < 3:
                    edge[0, c, pl.ds(row_of(at), ROWS), :] = left
                    edge[1, c, pl.ds(row_of(at), ROWS), :] = right
                else:
                    edge_diag[0, at] = left + (6.0 - SHIFT)
                    edge_diag[1, at] = right + (6.0 - SHIFT)
    for s in both:
        for c in comps:
            edge[s, c, pl.ds(ROWS, ROWS), :] = blank
            edge[s, c, pl.ds(row_of(depth), ROWS), :] = blank
        edge_div[s, pl.ds(ROWS, ROWS), :] = blank
        edge_div[s, pl.ds(row_of(depth), ROWS), :] = blank

    def join_blocks(ref, lead):
        for d in (0, half):
            base = row_of(d)
            last = ref[lead + (pl.ds(base + ROWS - 1, half, stride=PITCH), slice(None))]
            ahead = ref[lead + (pl.ds(base, half, stride=PITCH), slice(None))]
            spot = lane_iota((half, LANES))
            ref[lead + (pl.ds(base - 1, half, stride=PITCH), slice(None))] = jnp.where(
                spot >= EDGE, turn(last, EDGE), 0.0
            )
            ref[lead + (pl.ds(base + ROWS, half, stride=PITCH), slice(None))] = jnp.where(
                spot < LANES - EDGE, turn(ahead, -EDGE), 0.0
            )

    def at(s, c, d, by=0):
        return edge[s, c, pl.ds(row_of(d) + by, ROWS), :]

    def div_at(s, d, by=0):
        return edge_div[s, pl.ds(row_of(d) + by, ROWS), :]

    middle = (lane % EDGE >= HALF - 2) & (lane % EDGE < HALF + 2)

    def edge_step(level):
        for s in both:
            for c in comps:
                join_blocks(edge, (s, c))
        for s in both:
            for d in range(depth):
                x = at(s, 0, d)
                w = turn(x, -1) - turn(x, 1)
                w = w + (at(s, 1, d, 1) - at(s, 1, d, -1))
                w = w + (at(s, 2, d + 1) - at(s, 2, d - 1))
                edge_div[s, pl.ds(row_of(d), ROWS), :] = w * ((0.25 * BULK) * keep[s])
            join_blocks(edge_div, (s,))
        cross = blank
        for c in comps:
            images = []
            for d in range(depth):
                pair = []
                for s in both:
                    x = at(s, c, d)
                    if c == 0:
                        w = div_at(s, d)
                        total = turn(x + w, -1) + turn(x - w, 1)
                    else:
                        total = turn(x, -1) + turn(x, 1)
                    if c == 1:
                        total = total + (div_at(s, d, 1) - div_at(s, d, -1))
                    if c == 2:
                        total = total + (div_at(s, d + 1) - div_at(s, d - 1))
                    total = total + (at(s, c, d - 1) + at(s, c, d + 1))
                    total = total + (at(s, c, d, 1) + at(s, c, d, -1))
                    pair.append((edge_diag[s, d] * x - total) * keep[s])
                images.append(pair)
                old = packed[c, d] if level == 0 else fixes[level - 1, c, d]
                new = jnp.where(first_half, pair[1], pair[0])
                if level + 1 < ITERS:
                    fixes[level, c, d] = new
                else:
                    fix[c, d] = new
                cross = cross + old * new
            for d in range(depth):
                for s in both:
                    edge[s, c, pl.ds(row_of(d), ROWS), :] = images[d][s]
        return jnp.where(middle, cross, 0.0)

    crosses = [edge_step(level) for level in range(ITERS)]

    clear_padding(div, (), depth, across)
    for c in comps:
        clear_padding(first, (c,), depth, across)
        clear_padding(second, (c,), depth, across)

    spot = lane_iota((CHUNK, LANES))
    outside = (spot < 2) | (spot >= LANES - 2)

    def mended(level, c, d, r, value):
        edges = fixes[level, c, d]
        moved = [turn(edges, -(EDGE * ((r + i) // ROWS) + HALF)) for i in range(0, CHUNK, ROWS)]
        return jnp.where(outside, jnp.concatenate(moved, axis=0), value)

    def mend_first(d, carry):
        for c in comps:
            for r in range(0, across, CHUNK):
                first[c, d + 1, pl.ds(PAD + r, CHUNK), :] = mended(
                    0, c, d, r, first_raw[c, d, r : r + CHUNK, :]
                )
        return carry

    loop(depth, 2, mend_first, 0)

    def store_second(c, d, r, out):
        second[c, d + 1, pl.ds(PAD + r, CHUNK), :] = mended(1, c, d, r, out)

    def store_third(c, d, r, out):
        third_raw[c, d, r : r + CHUNK, :] = out

    cyclic_step(first, mass, div, store_second, moments.at[0], 2)
    cyclic_step(second, mass, div, store_third, moments.at[1], 4)
    parts = [
        early[0], early[1] + crosses[0],
        moments[0, 0], moments[0, 1] + crosses[1],
        moments[1, 0], moments[1, 1] + crosses[2],
    ]

    variants = ends.shape[0]
    pieces = 1 if per > 1 else variants
    blocks = 3 * ITERS * pieces
    bearing_rows = -(-blocks // per)
    picked[...] = jnp.zeros(picked.shape, jnp.float32)
    for block in range(blocks):
        value, piece = block // pieces, block % pieces
        row, z = block // per, (block % per if per > 1 else piece)
        ref, c = (field, first, second)[value // 3], value % 3
        for side in both:
            place = PAD + (1 + 2 * side) * across // 4
            column = (2 * z + side) * LANES
            picked[row : row + 1, column : column + LANES] = ref[c, 1, place : place + 1, :]
    start = (index * LANES).astype(jnp.float32)
    along = lax.broadcasted_iota(jnp.int32, (LANES, LANES), 0).astype(jnp.float32) + start
    parity = lane_iota((LANES, LANES)) % 2
    total = jnp.zeros((picked.shape[0], LANES), jnp.float32)
    for z in range(variants):
        site = jnp.broadcast_to(ends[z : z + 1, :], (LANES, LANES)) == along
        for side in both:
            column = (2 * z + side) * LANES
            hit = jnp.where(site & (parity == side), 1.0, 0.0)
            total = total + jnp.dot(
                picked[:, column : column + LANES], hit,
                precision=HIGH, preferred_element_type=jnp.float32,
            )
    sums[...] = jnp.zeros(sums.shape, jnp.float32)
    sums[0:bearing_rows, :] = total[0:bearing_rows]
    low = lane_iota((1, LANES)) < LANES // 2
    for pair in range(3):
        halves = []
        for part in parts[2 * pair : 2 * pair + 2]:
            flat = jnp.sum(part, axis=0, keepdims=True)
            halves.append(flat + turn(flat, LANES // 2))
        sums[bearing_rows + pair : bearing_rows + pair + 1, :] = jnp.where(low, *halves)
    out = sums[...]
    for device in range(payload.shape[0]):
        payload[device] = out


def coefficients(moment):
    def dot(a, b):
        total = None
        for i, left in enumerate(a):
            for j, right in enumerate(b):
                term = left * right * moment[i + j]
                total = term if total is None else total + term
        return total

    one = jnp.ones_like(moment[0])
    solved, direction, increment = [one], [one], []
    norm = moment[0]
    for iteration in range(ITERS):
        image = [SHIFT * p for p in direction] + [jnp.zeros_like(one)]
        for i, p in enumerate(direction):
            image[i + 1] = image[i + 1] + p
        alpha = norm / dot(direction, image)
        increment = [
            alpha * p + (increment[i] if i < len(increment) else 0.0) for i, p in enumerate(direction)
        ]
        solved = [
            (solved[i] if i < len(solved) else 0.0) - alpha * q for i, q in enumerate(image)
        ]
        if iteration + 1 < ITERS:
            after = dot(solved, solved)
            ratio = after / norm
            direction = [
                s + (ratio * direction[i] if i < len(direction) else 0.0)
                for i, s in enumerate(solved)
            ]
            norm = after
    return increment, solved


def combine_kernel(
    per, gathered, field, first, second, third_raw, fix, ends, stick, load, prior,
    increment_hbm, residual_hbm, friction,
    increment, residual, forces, sems,
):
    depth, across = third_raw.shape[1], third_raw.shape[2]
    start = (device_index() * LANES).astype(jnp.float32)
    bearings = load.shape[1]
    variants = ends.shape[0]
    pieces = 1 if per > 1 else variants
    width = min(bearings, LANES)
    bearing_rows = -(-9 * pieces // per)
    parts = [gathered[i] for i in range(gathered.shape[0])]
    while len(parts) > 1:
        parts = [sum(parts[i : i + 2]) for i in range(0, len(parts), 2)]
    total = parts[0]
    low = lane_iota((1, LANES)) < LANES // 2
    moments = []
    for n in range(6):
        row = total[bearing_rows + n // 2 : bearing_rows + n // 2 + 1]
        row = jnp.where(low == (n % 2 == 0), row, 0.0)
        moments.append(jnp.sum(row, axis=1, keepdims=True))
    grow, keep = coefficients(moments)

    forces[...] = jnp.zeros(forces.shape, jnp.float32)
    lane = lane_iota((1, width))
    for piece in range(pieces):
        span = slice(piece * LANES, piece * LANES + width)
        readout = []
        for c in range(3):
            value = None
            for k in range(ITERS):
                block = (3 * k + c) * pieces + piece
                row = total[block // per : block // per + 1]
                if per > 1 and block % per:
                    row = turn(row, LANES - (block % per) * bearings)
                term = grow[k] * row[:, :width]
                value = term if value is None else value + term
            readout.append(value)
        weight = load[:, span]
        radius = jnp.where(stick[:, span] == 1, STATIC, KINETIC) * weight
        trial = [prior[c : c + 1, span] + ELASTIC * readout[c] for c in range(2)]
        magnitude = jnp.sqrt(trial[0] * trial[0] + trial[1] * trial[1])
        scale = radius / jnp.maximum(magnitude, radius)
        held = [t * scale for t in trial]
        for c in range(2):
            friction[c : c + 1, span] = held[c]
        force = [held[c] + weight / RADIUS * readout[c] for c in range(2)] + [VERTICAL * readout[2]]
        for c in range(3):
            for side in range(2):
                forces[2 * c + side : 2 * c + side + 1, span] = jnp.where(
                    lane % 2 == side, force[c], 0.0
                )
    along = lax.broadcasted_iota(jnp.int32, (LANES, LANES), 0).astype(jnp.float32) + start
    placed = jnp.zeros((8, LANES), jnp.float32)
    for piece in range(pieces):
        site = jnp.broadcast_to(ends[piece : piece + 1, :], (LANES, LANES)) == along
        placed = placed + lax.dot_general(
            forces[:, piece * LANES : (piece + 1) * LANES], jnp.where(site, 1.0, 0.0),
            (((1,), (1,)), ((), ())), precision=HIGH, preferred_element_type=jnp.float32,
        )

    grow = [jnp.broadcast_to(g, (CHUNK, LANES)) for g in grow]
    keep = [jnp.broadcast_to(g, (CHUNK, LANES)) for g in keep]

    spot = lane_iota((CHUNK, LANES))
    outside = (spot < 2) | (spot >= LANES - 2)

    def run(c, begin, end):
        def body(i, carry):
            d = begin + i
            edges = fix[c, d]
            for r in range(0, across, CHUNK):
                here = pl.ds(PAD + r, CHUNK)
                v = [ref[c, d + 1, here, :] for ref in (field, first, second)]
                moved = [
                    turn(edges, -(EDGE * ((r + j) // ROWS) + HALF)) for j in range(0, CHUNK, ROWS)
                ]
                v.append(
                    jnp.where(
                        outside, jnp.concatenate(moved, axis=0), third_raw[c, d, r : r + CHUNK, :]
                    )
                )
                increment[c, d, r : r + CHUNK, :] = grow[0] * v[0] + grow[1] * v[1] + grow[2] * v[2]
                residual[c, d, r : r + CHUNK, :] = (
                    keep[0] * v[0] + keep[1] * v[1] + (keep[2] * v[2] + keep[3] * v[3])
                )
            return carry

        loop(end - begin, 4, body, 0)

    copies = []

    def send(c, begin, end):
        for which, (ref, hbm) in enumerate(((increment, increment_hbm), (residual, residual_hbm))):
            part = pl.ds(begin, end - begin)
            copy = pltpu.make_async_copy(
                ref.at[c, part], hbm.at[c, part], sems.at[which, 2 * c + (begin > 0)]
            )
            copy.start()
            copies.append(copy)

    half = depth // 2
    for c in range(3):
        run(c, 0, half)
        for side in range(2):
            at = (1 + 2 * side) * across // 4
            residual[c, 0, at : at + 1, :] = (
                residual[c, 0, at : at + 1, :] - placed[2 * c + side : 2 * c + side + 1]
            )
        send(c, 0, half)
        run(c, half, depth)
        send(c, half, depth)
    for copy in copies:
        copy.wait()


def vmem_spec():
    return pl.BlockSpec(memory_space=pltpu.VMEM)


def hbm_spec():
    return pl.BlockSpec(memory_space=pltpu.HBM)


def pack_call(right_side, mass_field):
    f32 = jnp.float32
    depth, across, along = mass_field.shape
    half = depth // 2
    return pl.pallas_call(
        pack_kernel,
        out_shape=(
            pltpu.VMEM((3, depth + 2, across + 2 * PAD, along), f32),
            pltpu.VMEM((depth, across, along), f32),
            pltpu.VMEM((4, depth, ROWS, LANES), f32),
            jax.ShapeDtypeStruct((4, half, ROWS, LANES), f32),
            jax.ShapeDtypeStruct((4, half, ROWS, LANES), f32),
        ),
        in_specs=[hbm_spec()] * 2,
        out_specs=(vmem_spec(),) * 5,
        scratch_shapes=[pltpu.SemaphoreType.DMA((4,))],
        compiler_params=LIMIT,
        name="pack",
    )(right_side, mass_field)


def first_call(field, mass, spans, variants):
    f32 = jnp.float32
    depth, across, along = mass.shape
    return pl.pallas_call(
        first_kernel,
        out_shape=(
            pltpu.VMEM((3, depth, across, along), f32),
            pltpu.VMEM((2, ROWS, LANES), f32),
            pltpu.VMEM((variants, LANES), f32),
        ),
        in_specs=[vmem_spec()] * 3,
        out_specs=(vmem_spec(),) * 3,
        scratch_shapes=[pltpu.VMEM((depth + 2, across + 2 * PAD, along), f32)],
        compiler_params=LIMIT,
        cost_estimate=pl.CostEstimate(flops=20_000_000, bytes_accessed=4_000_000, transcendentals=0),
        name="first",
    )(field, mass, spans)


def basis_call(per, rows, field, mass, packed, got_a, got_b, first_raw, early, ends, count):
    f32 = jnp.float32
    depth, across, along = mass.shape
    variants = ends.shape[0]
    padded = (depth + 2, across + 2 * PAD, along)
    return pl.pallas_call(
        functools.partial(basis_kernel, per),
        out_shape=(
            pltpu.VMEM((3,) + padded, f32),
            pltpu.VMEM((3,) + padded, f32),
            pltpu.VMEM((3, depth, across, along), f32),
            pltpu.VMEM((3, depth, ROWS, LANES), f32),
            jax.ShapeDtypeStruct((count, rows, LANES), f32),
        ),
        in_specs=[vmem_spec()] * 8,
        out_specs=(vmem_spec(),) * 5,
        scratch_shapes=[
            pltpu.VMEM(padded, f32),
            pltpu.VMEM((2, 3, (depth + 2) * PITCH, LANES), f32),
            pltpu.VMEM((2, (depth + 2) * PITCH, LANES), f32),
            pltpu.VMEM((2, depth, ROWS, LANES), f32),
            pltpu.VMEM((ITERS - 1, 3, depth, ROWS, LANES), f32),
            pltpu.VMEM((2, 2, ROWS, LANES), f32),
            pltpu.VMEM((rows, LANES), f32),
            pltpu.VMEM((rows, 2 * variants * LANES), f32),
        ],
        compiler_params=LIMIT,
        name="basis",
    )(field, mass, packed, got_a, got_b, first_raw, early, ends)


def combine_call(per, gathered, field, first, second, third_raw, fix, ends, stick, load, prior):
    f32 = jnp.float32
    shape = third_raw.shape
    bearings = load.shape[1]
    return pl.pallas_call(
        functools.partial(combine_kernel, per),
        out_shape=(
            jax.ShapeDtypeStruct(shape, f32),
            jax.ShapeDtypeStruct(shape, f32),
            jax.ShapeDtypeStruct((2, bearings), f32),
        ),
        in_specs=[vmem_spec()] * 10,
        out_specs=(hbm_spec(), hbm_spec(), vmem_spec()),
        scratch_shapes=[
            pltpu.VMEM(shape, f32),
            pltpu.VMEM(shape, f32),
            pltpu.VMEM((ROWS, max(bearings, LANES)), f32),
            pltpu.SemaphoreType.DMA((2, 6)),
        ],
        compiler_params=LIMIT,
        name="combine",
    )(gathered, field, first, second, third_raw, fix, ends, stick, load, prior)


def shards(count, right_side, mass_field, span_lengths, stick_flags, normal_load, prior_friction):
    piers = span_lengths.shape[0]
    bearings = 2 * piers
    per = LANES // bearings if bearings <= LANES else 1
    variants = per if bearings <= LANES else bearings // LANES
    pieces = 1 if per > 1 else variants
    rows = -(-(-(-3 * ITERS * pieces // per) + 3) // ROWS) * ROWS

    field, mass, packed, message_a, message_b = pack_call(right_side, mass_field)
    pairs_a = [p for i in range(0, count - 1, 2) for p in ((i, i + 1), (i + 1, i))]
    pairs_b = [p for i in range(1, count - 1, 2) for p in ((i, i + 1), (i + 1, i))]
    got_b = lax.ppermute(message_b, AXES, pairs_b)
    got_a = lax.ppermute(message_a, AXES, pairs_a)
    first_raw, early, ends = first_call(field, mass, span_lengths.reshape(1, piers), variants)
    first, second, third_raw, fix, payload = basis_call(
        per, rows, field, mass, packed, got_a, got_b, first_raw, early, ends, count
    )
    gathered = lax.all_to_all(payload, AXES, 0, 0)
    return combine_call(
        per, gathered, field, first, second, third_raw, fix, ends,
        stick_flags.reshape(1, bearings), normal_load.reshape(1, bearings), prior_friction,
    )


def solution(mesh):
    count = mesh.shape["len"] * mesh.shape["xs"]
    along = P(None, None, None, AXES)
    in_specs = (along, P(None, None, AXES), P(), P(), P(), P())
    return jax.shard_map(
        functools.partial(shards, count), mesh=mesh,
        in_specs=in_specs, out_specs=(along, along, P()), check_vma=False,
    )
```

time: 51.1 us -> 37.9 us (0.74)
  Pallas kernels: 24.5 us -> 14 us
  blocking collectives: 21.1 us -> 19.3 us
  local copies, waits for them, and re-layouts: 3.2 us -> 2.46 us
    pallas_call x3 -> x4, Pallas kernels: 24.5 us -> 14 us  [the longest x1 7.52 us: basis_call(): pl.pallas_call(functools.partial(basis_kernel, per), out_shape=(pltpu.VME...]
    all_to_all x1, blocking collectives: 21.1 us -> 19.3 us  [shards(): gathered = lax.all_to_all(payload, AXES, 0, 0)]
    unnamed x12, local copies, waits for them, and re-layouts: 3.11 us -> 2.46 us
  transfers between devices with their start and end apart: 2 -> 2, of which waited for: 1 -> 0; matrix products, arithmetic and copies ran while one was open for 0% -> 0% of each run, Pallas kernels for 0% -> 5%
where the time goes in v2:
time: 37.9 us; the launch traced here: 37.7 us
  blocking collectives  19.3 us (51%)
  Pallas kernels  14 us (37%)
  local copies, waits for them, and re-layouts  2.46 us (6%)
  starting transfers between devices  1.17 us (3%)
  between operations  0.72 us (2%)
    all_to_all x1, blocking collectives, shards(): gathered = lax.all_to_all(payload, AXES, 0, 0)  19.3 us
    pallas_call x1, Pallas kernels, basis_call(): pl.pallas_call(functools.partial(basis_kernel, per), out_shape=(pltpu.VME...  7.52 us
    pallas_call x1, Pallas kernels, combine_call(): pl.pallas_call(functools.partial(combine_kernel, per), out_shape=(jax.Sha...  3.14 us
    unnamed x12, local copies, waits for them, and re-layouts  2.46 us
    pallas_call x1, Pallas kernels, first_call(): pl.pallas_call(first_kernel, out_shape=(pltpu.VMEM((3, depth, across, alo...  2.04 us
    pallas_call x1, Pallas kernels, pack_call(): pl.pallas_call(pack_kernel, out_shape=(pltpu.VMEM((3, depth + 2, across +...  1.33 us
  transfers between devices with their start and end apart: 2, of which 0 were waited for; matrix products, arithmetic and copies ran while one was open for 0% of the time, Pallas kernels for 5%

profile of v2, /device:TPU:0, one launch (start us, length us, event | category | flops | bytes accessed | tf_op | source)
XLA Modules:
  0.0 37.7 jit_solution(9293826352910717424)
XLA Ops:
  0.6 0.0 copy-start
  0.6 1.4 %copy-done = f32[3,16,64,128]{3,2,1,0:T(8,128)S(1)} copy-done((f32[3,16,64,128]{3,2,1,0:T(8,128)S(1)}, f32[3,16,64,128]{3,2,1,0:T(8,128)}, u32[]{:S(2)}) %copy-start) | copy-done | bytes 1572888
  2.0 0.0 copy-start.1
  2.0 1.0 %copy-done.1 = f32[16,64,128]{2,1,0:T(8,128)S(1)} copy-done((f32[16,64,128]{2,1,0:T(8,128)S(1)}, f32[16,64,128]{2,1,0:T(8,128)}, u32[]{:S(2)}) %copy-start.1) | copy-done | bytes 524312
  3.1 0.0 copy-start.3
  3.1 1.3 %pack.1 = (f32[3,18,80,128]{3,2,1,0:T(8,128)S(1)}, f32[16,64,128]{2,1,0:T(8,128)S(1)}, f32[4,16,8,128]{3,2,1,0:T(8,128)S(1)}, f32[4,8,8,128]{3,2,1,0:T(8,128)S(1)}, f32[4,8,8,128]{3,2,1,0:T(8,128)S(1)}) custom-call(f32[3,16,64,128]{3,2,1,0:T(8,128)S(1)} %copy-done, f32[16,64,128]{2,1,0:T(8,128)S(1)} %copy-done.1), custom_call_target="tpu_custom_call" | custom-call | tf_op jit(solution)/shard_map/pack/pallas_call | solution.py:536
  4.4 0.5 %collective-permute-start = (f32[4,8,8,128]{3,2,1,0:T(8,128)S(1)}, f32[4,8,8,128]{3,2,1,0:T(8,128)S(1)}, u32[]{:S(2)}, u32[]{:S(2)}) collective-permute-start(f32[4,8,8,128]{3,2,1,0:T(8,128)S(1)} %get-tuple-element.19), channel_id=1, source_target_pairs={{0,1},{1,0},{2,3},{3,2},{4,5},{5,4},{6,7},{7,6},{8,9},{9,8},{10,11... | collective-permute-start | bytes 393224 | tf_op jit(solution)/shard_map/ppermute | solution.py:639
  4.9 0.7 %collective-permute-start.1 = (f32[4,8,8,128]{3,2,1,0:T(8,128)S(1)}, f32[4,8,8,128]{3,2,1,0:T(8,128)S(1)}, u32[]{:S(2)}, u32[]{:S(2)}) collective-permute-start(f32[4,8,8,128]{3,2,1,0:T(8,128)S(1)} %get-tuple-element.20), channel_id=1, source_target_pairs={{1,2},{2,1},{3,4},{4,3},{5,6},{6,5},{7,8},{8,7},{9,10},{10,9},{11,... | collective-permute-start | bytes 393224 | tf_op jit(solution)/shard_map/ppermute | solution.py:638
  5.6 0.0 copy-done.3
  5.6 2.0 %first.1 = (f32[3,16,64,128]{3,2,1,0:T(8,128)S(1)}, f32[2,8,128]{2,1,0:T(8,128)S(1)}, f32[2,128]{1,0:T(2,128)S(1)}) custom-call(f32[3,18,80,128]{3,2,1,0:T(8,128)S(1)} %get-tuple-element.16.field, f32[16,64,128]{2,1,0:T(8,128)S(1)} %get-tuple-element.17.mass, s32[1,32]{1,0:T(1,128)S(1)} %bitcast.3), custom_call_target="tpu_custom_call" | custom-call | flops 20000000 | bytes 4000000 | tf_op jit(solution)/shard_map/first/pallas_call | solution.py:556
  7.7 0.0 collective-permute-done.got_a
  7.7 0.0 collective-permute-done.1.got_b
  7.7 0.0 copy-start.2
  7.7 0.0 copy-start.4
  7.7 0.0 copy-start.5
  7.7 7.5 %basis.1 = (f32[3,18,80,128]{3,2,1,0:T(8,128)S(1)}, f32[3,18,80,128]{3,2,1,0:T(8,128)S(1)}, f32[3,16,64,128]{3,2,1,0:T(8,128)S(1)}, f32[3,16,8,128]{3,2,1,0:T(8,128)S(1)}, f32[32,8,128]{2,1,0:T(8,128)S(1)}) custom-call(f32[3,18,80,128]{3,2,1,0:T(8,128)S(1)} %get-tuple-element.16.field, f32[16,64,128]{2,1,0:T(8,128)S(1)} %get-tuple-element.17.mass, ...), custom_call_target="tpu_custom_call" | custom-call | tf_op jit(solution)/shard_map/basis/pallas_call | solution.py:577
  15.2 19.3 %all_to_all.5.gathered = f32[32,8,128]{2,1,0:T(8,128)S(1)} all-to-all(f32[32,8,128]{2,1,0:T(8,128)S(1)} %get-tuple-element.24), channel_id=1, replica_groups=mesh['len'=8,'xs'=4] {'len','xs'}, dimensions={0} | all-to-all | bytes 262144 | tf_op jit(solution)/shard_map/all_to_all | solution.py:644
  34.5 0.0 copy-done.2
  34.5 0.0 copy-done.4
  34.5 0.0 copy-done.5
  34.5 3.1 %combine.1 = (f32[3,16,64,128]{3,2,1,0:T(8,128)}, f32[3,16,64,128]{3,2,1,0:T(8,128)}, f32[2,64]{1,0:T(2,128)}) custom-call(f32[32,8,128]{2,1,0:T(8,128)S(1)} %all_to_all.5.gathered, f32[3,18,80,128]{3,2,1,0:T(8,128)S(1)} %get-tuple-element.16.field, f32[3,18,80,128]{3,2,1,0:T(8,128)S(1)} %get-tuple-element.25.first, ...), custom_call_target="tpu_custom_call" | custom-call | tf_op jit(solution)/shard_map/combine/pallas_call | solution.py:607
Async XLA Ops:
  0.6 1.4 %copy-start = (f32[3,16,64,128]{3,2,1,0:T(8,128)S(1)}, f32[3,16,64,128]{3,2,1,0:T(8,128)}, u32[]{:S(2)}) copy-start(f32[3,16,64,128]{3,2,1,0:T(8,128)} %right_hbm.1) | copy-start | bytes 4718596
  2.0 1.0 %copy-start.1 = (f32[16,64,128]{2,1,0:T(8,128)S(1)}, f32[16,64,128]{2,1,0:T(8,128)}, u32[]{:S(2)}) copy-start(f32[16,64,128]{2,1,0:T(8,128)} %mass_hbm.1) | copy-start | bytes 1572868
  3.1 2.5 %copy-start.3 = (s32[32]{0:T(128)S(1)}, s32[32]{0:T(128)}, u32[]{:S(2)}) copy-start(s32[32]{0:T(128)} %param.8) | copy-start | bytes 388
  4.4 3.2 %collective-permute-start = (f32[4,8,8,128]{3,2,1,0:T(8,128)S(1)}, f32[4,8,8,128]{3,2,1,0:T(8,128)S(1)}, u32[]{:S(2)}, u32[]{:S(2)}) collective-permute-start(f32[4,8,8,128]{3,2,1,0:T(8,128)S(1)} %get-tuple-element.19), channel_id=1, source_target_pairs={{0,1},{1,0},{2,3},{3,2},{4,5},{5,4},{6,7},{7,6},{8,9},{9,8},{10,11... | collective-permute-start | bytes 393224 | tf_op jit(solution)/shard_map/ppermute | solution.py:639
  4.9 2.7 %collective-permute-start.1 = (f32[4,8,8,128]{3,2,1,0:T(8,128)S(1)}, f32[4,8,8,128]{3,2,1,0:T(8,128)S(1)}, u32[]{:S(2)}, u32[]{:S(2)}) collective-permute-start(f32[4,8,8,128]{3,2,1,0:T(8,128)S(1)} %get-tuple-element.20), channel_id=1, source_target_pairs={{1,2},{2,1},{3,4},{4,3},{5,6},{6,5},{7,8},{8,7},{9,10},{10,9},{11,... | collective-permute-start | bytes 393224 | tf_op jit(solution)/shard_map/ppermute | solution.py:638
  7.7 26.8 %copy-start.2 = (f32[2,64]{1,0:T(2,128)S(1)}, f32[2,64]{1,0:T(2,128)}, u32[]{:S(2)}) copy-start(f32[2,64]{1,0:T(2,128)} %prior.1) | copy-start | bytes 1540
  7.7 26.8 %copy-start.4 = (s32[64]{0:T(128)S(1)}, s32[64]{0:T(128)}, u32[]{:S(2)}) copy-start(s32[64]{0:T(128)} %param.9) | copy-start | bytes 772
  7.7 26.8 %copy-start.5 = (f32[64]{0:T(128)S(1)}, f32[64]{0:T(128)}, u32[]{:S(2)}) copy-start(f32[64]{0:T(128)} %param.10) | copy-start | bytes 772

commit v3 on v2

--- a/solution.py
+++ b/solution.py
@@ -25,6 +25,7 @@
 BLOCKS = LANES // EDGE
 PITCH = 3 * ROWS
 CHUNK = 16
+PIECE = 4
 HIGH = lax.Precision.HIGHEST
 LIMIT = pltpu.CompilerParams(vmem_limit_bytes=32 * 1024 * 1024)
 
@@ -83,7 +84,11 @@
             edge = None
             for b in range(across // ROWS):
                 row = pl.ds(b * ROWS + (PAD if c < 3 else 0), ROWS)
-                tile = field[c, d + 1, row, :] if c < 3 else mass[d, row, :]
+                if c < 3:
+                    tile = field[c, d + 1, row, :]
+                else:
+                    tile = mass[d, row, :] + (6.0 - SHIFT)
+                    mass[d, row, :] = tile
                 moved = turn(tile, EDGE * b + HALF)
                 edge = moved if edge is None else jnp.where(block_of == b, moved, edge)
             packed[c, d] = edge
@@ -100,7 +105,7 @@
     return sum(x[i : i + ROWS] for i in range(0, x.shape[0], ROWS))
 
 
-def cyclic_step(source, mass, div, store, moments, step):
+def cyclic_step(source, mass, div, store, step):
     depth, across = mass.shape[0], mass.shape[1]
     chunks = range(0, across, CHUNK)
 
@@ -115,14 +120,12 @@
         return carry
 
     loop(depth, step, divergence, 0)
-    lane = lane_iota((CHUNK, LANES))
-    inside = (lane >= 2) & (lane < LANES - 2)
 
     def image(d, carry):
         norm, cross = carry
         for r in chunks:
             here, up, down = (pl.ds(PAD + r + by, CHUNK) for by in (0, 1, -1))
-            diag = mass[d, r : r + CHUNK, :] + (6.0 - SHIFT)
+            diag = mass[d, r : r + CHUNK, :]
             w = div[d + 1, here, :]
             norms, crosses = [], []
             for c in range(3):
@@ -140,24 +143,37 @@
                 out = diag * x - total
                 store(c, d, r, out)
                 norms.append(x * x)
-                crosses.append(jnp.where(inside, x, 0.0) * out)
+                crosses.append(x * out)
             norm = norm + folded(norms[0] + norms[1] + norms[2])
             cross = cross + folded(crosses[0] + crosses[1] + crosses[2])
         return norm, cross
 
-    norm, cross = loop(depth, step, image, (jnp.zeros((ROWS, LANES), jnp.float32),) * 2)
-    moments[0] = norm
-    moments[1] = cross
-
-
-def first_kernel(field, mass, spans, first_raw, moments, ends, div):
+    return loop(depth, step, image, (jnp.zeros((ROWS, LANES), jnp.float32),) * 2)
+
+
+def interior(value, margin):
+    lane = lane_iota(value.shape)
+    return jnp.where((lane >= margin) & (lane < LANES - margin), value, 0.0)
+
+
+def cyclic_kernel(field, mass, spans, first, second, moments, ends, div):
     depth, across = mass.shape[0], mass.shape[1]
     clear_padding(div, (), depth, across)
-
-    def store(c, d, r, out):
-        first_raw[c, d, r : r + CHUNK, :] = out
-
-    cyclic_step(field, mass, div, store, moments, 4)
+    for c in range(3):
+        clear_padding(first, (c,), depth, across)
+
+    def store_first(c, d, r, out):
+        first[c, d + 1, pl.ds(PAD + r, CHUNK), :] = out
+
+    def store_second(c, d, r, out):
+        second[c, d, r : r + CHUNK, :] = out
+
+    norm, cross = cyclic_step(field, mass, div, store_first, 4)
+    moments[0] = norm
+    moments[1] = interior(cross, 2)
+    norm, cross = cyclic_step(first, mass, div, store_second, 4)
+    moments[2] = interior(norm, 2)
+    moments[3] = interior(cross, 4)
     piers = spans.shape[1]
     bearings = 2 * piers
     lane = lane_iota((piers, LANES))
@@ -171,10 +187,22 @@
         ends[z : z + 1, :] = jnp.where(inside, total[0:1] - 1.0, -1e9)
 
 
+def mended(value, edges, row, margin):
+    moved = [
+        turn(edges, -(EDGE * ((row + i) // ROWS) + HALF)) for i in range(0, value.shape[0], ROWS)
+    ]
+    spot = lane_iota(value.shape)
+    return jnp.where(
+        (spot < margin) | (spot >= LANES - margin),
+        moved[0] if len(moved) == 1 else jnp.concatenate(moved, axis=0),
+        value,
+    )
+
+
 def basis_kernel(
-    per, field, mass, packed, got_a, got_b, first_raw, early, ends,
-    first, second, third_raw, fix, payload,
-    div, edge, edge_div, edge_diag, fixes, moments, sums, picked,
+    per, field, mass, packed, got_a, got_b, first, second_raw, early, ends,
+    second, third, fix_first, fix_third, payload,
+    div, edge, edge_div, edge_diag, fix_second, sums, picked,
 ):
     depth, across = mass.shape[0], mass.shape[1]
     index = device_index()
@@ -217,8 +245,8 @@
                     edge[0, c, pl.ds(row_of(at), ROWS), :] = left
                     edge[1, c, pl.ds(row_of(at), ROWS), :] = right
                 else:
-                    edge_diag[0, at] = left + (6.0 - SHIFT)
-                    edge_diag[1, at] = right + (6.0 - SHIFT)
+                    edge_diag[0, at] = left
+                    edge_diag[1, at] = right
     for s in both:
         for c in comps:
             edge[s, c, pl.ds(ROWS, ROWS), :] = blank
@@ -245,7 +273,11 @@
     def div_at(s, d, by=0):
         return edge_div[s, pl.ds(row_of(d) + by, ROWS), :]
 
-    middle = (lane % EDGE >= HALF - 2) & (lane % EDGE < HALF + 2)
+    def middle(value, margin):
+        spot = lane % EDGE
+        return jnp.where((spot >= HALF - margin) & (spot < HALF + margin), value, 0.0)
+
+    fixes = (packed, fix_first, fix_second, fix_third)
 
     def edge_step(level):
         for s in both:
@@ -259,7 +291,7 @@
                 w = w + (at(s, 2, d + 1) - at(s, 2, d - 1))
                 edge_div[s, pl.ds(row_of(d), ROWS), :] = w * ((0.25 * BULK) * keep[s])
             join_blocks(edge_div, (s,))
-        cross = blank
+        norm, cross = blank, blank
         for c in comps:
             images = []
             for d in range(depth):
@@ -279,55 +311,44 @@
                     total = total + (at(s, c, d, 1) + at(s, c, d, -1))
                     pair.append((edge_diag[s, d] * x - total) * keep[s])
                 images.append(pair)
-                old = packed[c, d] if level == 0 else fixes[level - 1, c, d]
+                old = fixes[level][c, d]
                 new = jnp.where(first_half, pair[1], pair[0])
-                if level + 1 < ITERS:
-                    fixes[level, c, d] = new
-                else:
-                    fix[c, d] = new
+                fixes[level + 1][c, d] = new
+                norm = norm + old * old
                 cross = cross + old * new
             for d in range(depth):
                 for s in both:
                     edge[s, c, pl.ds(row_of(d), ROWS), :] = images[d][s]
-        return jnp.where(middle, cross, 0.0)
-
-    crosses = [edge_step(level) for level in range(ITERS)]
+        return norm, cross
+
+    edge_sums = [edge_step(level) for level in range(ITERS)]
 
     clear_padding(div, (), depth, across)
     for c in comps:
-        clear_padding(first, (c,), depth, across)
         clear_padding(second, (c,), depth, across)
 
-    spot = lane_iota((CHUNK, LANES))
-    outside = (spot < 2) | (spot >= LANES - 2)
-
-    def mended(level, c, d, r, value):
-        edges = fixes[level, c, d]
-        moved = [turn(edges, -(EDGE * ((r + i) // ROWS) + HALF)) for i in range(0, CHUNK, ROWS)]
-        return jnp.where(outside, jnp.concatenate(moved, axis=0), value)
-
-    def mend_first(d, carry):
+    def mend(d, carry):
         for c in comps:
+            edges = fix_second[c, d]
             for r in range(0, across, CHUNK):
-                first[c, d + 1, pl.ds(PAD + r, CHUNK), :] = mended(
-                    0, c, d, r, first_raw[c, d, r : r + CHUNK, :]
+                second[c, d + 1, pl.ds(PAD + r, CHUNK), :] = mended(
+                    second_raw[c, d, r : r + CHUNK, :], edges, r, 4
                 )
         return carry
 
-    loop(depth, 2, mend_first, 0)
-
-    def store_second(c, d, r, out):
-        second[c, d + 1, pl.ds(PAD + r, CHUNK), :] = mended(1, c, d, r, out)
+    loop(depth, 4, mend, 0)
 
     def store_third(c, d, r, out):
-        third_raw[c, d, r : r + CHUNK, :] = out
-
-    cyclic_step(first, mass, div, store_second, moments.at[0], 2)
-    cyclic_step(second, mass, div, store_third, moments.at[1], 4)
+        third[c, d, r : r + CHUNK, :] = out
+
+    norm, cross = cyclic_step(second, mass, div, store_third, 4)
     parts = [
-        early[0], early[1] + crosses[0],
-        moments[0, 0], moments[0, 1] + crosses[1],
-        moments[1, 0], moments[1, 1] + crosses[2],
+        early[0],
+        early[1] + middle(edge_sums[0][1], 2),
+        early[2] + middle(edge_sums[1][0], 2),
+        early[3] + middle(edge_sums[1][1], 4),
+        norm,
+        interior(cross, 2) + middle(edge_sums[2][1], 2),
     ]
 
     variants = ends.shape[0]
@@ -342,7 +363,12 @@
         for side in both:
             place = PAD + (1 + 2 * side) * across // 4
             column = (2 * z + side) * LANES
-            picked[row : row + 1, column : column + LANES] = ref[c, 1, place : place + 1, :]
+            here = ref[c, 1, place : place + 1, :]
+            if ref is first:
+                r = place - PAD
+                edges = fix_first[c, 0, r % ROWS : r % ROWS + 1, :]
+                here = mended(here, edges, r, 2)
+            picked[row : row + 1, column : column + LANES] = here
     start = (index * LANES).astype(jnp.float32)
     along = lax.broadcasted_iota(jnp.int32, (LANES, LANES), 0).astype(jnp.float32) + start
     parity = lane_iota((LANES, LANES)) % 2
@@ -405,11 +431,11 @@
 
 
 def combine_kernel(
-    per, gathered, field, first, second, third_raw, fix, ends, stick, load, prior,
+    per, gathered, field, first, second, third, fix_first, fix_third, ends, stick, load, prior,
     increment_hbm, residual_hbm, friction,
     increment, residual, forces, sems,
 ):
-    depth, across = third_raw.shape[1], third_raw.shape[2]
+    depth, across = third.shape[1], third.shape[2]
     start = (device_index() * LANES).astype(jnp.float32)
     bearings = load.shape[1]
     variants = ends.shape[0]
@@ -469,56 +495,43 @@
     grow = [jnp.broadcast_to(g, (CHUNK, LANES)) for g in grow]
     keep = [jnp.broadcast_to(g, (CHUNK, LANES)) for g in keep]
 
-    spot = lane_iota((CHUNK, LANES))
-    outside = (spot < 2) | (spot >= LANES - 2)
-
     def run(c, begin, end):
-        def body(i, carry):
-            d = begin + i
-            edges = fix[c, d]
+        for d in range(begin, end):
+            edges = fix_first[c, d], fix_third[c, d]
             for r in range(0, across, CHUNK):
                 here = pl.ds(PAD + r, CHUNK)
                 v = [ref[c, d + 1, here, :] for ref in (field, first, second)]
-                moved = [
-                    turn(edges, -(EDGE * ((r + j) // ROWS) + HALF)) for j in range(0, CHUNK, ROWS)
-                ]
-                v.append(
-                    jnp.where(
-                        outside, jnp.concatenate(moved, axis=0), third_raw[c, d, r : r + CHUNK, :]
-                    )
-                )
+                v.append(third[c, d, r : r + CHUNK, :])
+                v[1] = mended(v[1], edges[0], r, 2)
+                v[3] = mended(v[3], edges[1], r, 2)
                 increment[c, d, r : r + CHUNK, :] = grow[0] * v[0] + grow[1] * v[1] + grow[2] * v[2]
                 residual[c, d, r : r + CHUNK, :] = (
                     keep[0] * v[0] + keep[1] * v[1] + (keep[2] * v[2] + keep[3] * v[3])
                 )
-            return carry
-
-        loop(end - begin, 4, body, 0)
-
-    copies = []
-
-    def send(c, begin, end):
-        for which, (ref, hbm) in enumerate(((increment, increment_hbm), (residual, residual_hbm))):
-            part = pl.ds(begin, end - begin)
-            copy = pltpu.make_async_copy(
-                ref.at[c, part], hbm.at[c, part], sems.at[which, 2 * c + (begin > 0)]
-            )
-            copy.start()
-            copies.append(copy)
-
-    half = depth // 2
+
+    def copy(which, c, begin):
+        ref, hbm = ((increment, increment_hbm), (residual, residual_hbm))[which]
+        part = pl.ds(begin, PIECE)
+        return pltpu.make_async_copy(
+            ref.at[c, part], hbm.at[c, part], sems.at[which, c, begin // PIECE]
+        )
+
+    starts = range(0, depth, PIECE)
     for c in range(3):
-        run(c, 0, half)
-        for side in range(2):
-            at = (1 + 2 * side) * across // 4
-            residual[c, 0, at : at + 1, :] = (
-                residual[c, 0, at : at + 1, :] - placed[2 * c + side : 2 * c + side + 1]
-            )
-        send(c, 0, half)
-        run(c, half, depth)
-        send(c, half, depth)
-    for copy in copies:
-        copy.wait()
+        for begin in starts:
+            run(c, begin, begin + PIECE)
+            if begin == 0:
+                for side in range(2):
+                    at = (1 + 2 * side) * across // 4
+                    residual[c, 0, at : at + 1, :] = (
+                        residual[c, 0, at : at + 1, :] - placed[2 * c + side : 2 * c + side + 1]
+                    )
+            for which in range(2):
+                copy(which, c, begin).start()
+    for c in range(3):
+        for begin in starts:
+            for which in range(2):
+                copy(which, c, begin).wait()
 
 
 def vmem_spec():
@@ -547,62 +560,67 @@
         scratch_shapes=[pltpu.SemaphoreType.DMA((4,))],
         compiler_params=LIMIT,
         name="pack",
-    )(right_side, mass_field)
-
-
-def first_call(field, mass, spans, variants):
+    )(
+        pltpu.with_memory_space_constraint(right_side, pltpu.HBM),
+        pltpu.with_memory_space_constraint(mass_field, pltpu.HBM),
+    )
+
+
+def cyclic_call(field, mass, spans, variants):
     f32 = jnp.float32
     depth, across, along = mass.shape
+    padded = (depth + 2, across + 2 * PAD, along)
     return pl.pallas_call(
-        first_kernel,
+        cyclic_kernel,
         out_shape=(
+            pltpu.VMEM((3,) + padded, f32),
             pltpu.VMEM((3, depth, across, along), f32),
-            pltpu.VMEM((2, ROWS, LANES), f32),
+            pltpu.VMEM((4, ROWS, LANES), f32),
             pltpu.VMEM((variants, LANES), f32),
         ),
         in_specs=[vmem_spec()] * 3,
-        out_specs=(vmem_spec(),) * 3,
-        scratch_shapes=[pltpu.VMEM((depth + 2, across + 2 * PAD, along), f32)],
+        out_specs=(vmem_spec(),) * 4,
+        scratch_shapes=[pltpu.VMEM(padded, f32)],
         compiler_params=LIMIT,
-        cost_estimate=pl.CostEstimate(flops=20_000_000, bytes_accessed=4_000_000, transcendentals=0),
-        name="first",
+        cost_estimate=pl.CostEstimate(flops=40_000_000, bytes_accessed=8_000_000, transcendentals=0),
+        name="cyclic",
     )(field, mass, spans)
 
 
-def basis_call(per, rows, field, mass, packed, got_a, got_b, first_raw, early, ends, count):
+def basis_call(per, rows, field, mass, packed, got_a, got_b, first, second_raw, early, ends, count):
     f32 = jnp.float32
     depth, across, along = mass.shape
     variants = ends.shape[0]
     padded = (depth + 2, across + 2 * PAD, along)
+    edges = (3, depth, ROWS, LANES)
     return pl.pallas_call(
         functools.partial(basis_kernel, per),
         out_shape=(
             pltpu.VMEM((3,) + padded, f32),
-            pltpu.VMEM((3,) + padded, f32),
             pltpu.VMEM((3, depth, across, along), f32),
-            pltpu.VMEM((3, depth, ROWS, LANES), f32),
+            pltpu.VMEM(edges, f32),
+            pltpu.VMEM(edges, f32),
             jax.ShapeDtypeStruct((count, rows, LANES), f32),
         ),
-        in_specs=[vmem_spec()] * 8,
+        in_specs=[vmem_spec()] * 9,
         out_specs=(vmem_spec(),) * 5,
         scratch_shapes=[
             pltpu.VMEM(padded, f32),
             pltpu.VMEM((2, 3, (depth + 2) * PITCH, LANES), f32),
             pltpu.VMEM((2, (depth + 2) * PITCH, LANES), f32),
             pltpu.VMEM((2, depth, ROWS, LANES), f32),
-            pltpu.VMEM((ITERS - 1, 3, depth, ROWS, LANES), f32),
-            pltpu.VMEM((2, 2, ROWS, LANES), f32),
+            pltpu.VMEM(edges, f32),
             pltpu.VMEM((rows, LANES), f32),
             pltpu.VMEM((rows, 2 * variants * LANES), f32),
         ],
         compiler_params=LIMIT,
         name="basis",
-    )(field, mass, packed, got_a, got_b, first_raw, early, ends)
-
-
-def combine_call(per, gathered, field, first, second, third_raw, fix, ends, stick, load, prior):
+    )(field, mass, packed, got_a, got_b, first, second_raw, early, ends)
+
+
+def combine_call(per, gathered, field, first, second, third, fixes, ends, stick, load, prior):
     f32 = jnp.float32
-    shape = third_raw.shape
+    shape = third.shape
     bearings = load.shape[1]
     return pl.pallas_call(
         functools.partial(combine_kernel, per),
@@ -611,17 +629,17 @@
             jax.ShapeDtypeStruct(shape, f32),
             jax.ShapeDtypeStruct((2, bearings), f32),
         ),
-        in_specs=[vmem_spec()] * 10,
+        in_specs=[vmem_spec()] * 11,
         out_specs=(hbm_spec(), hbm_spec(), vmem_spec()),
         scratch_shapes=[
             pltpu.VMEM(shape, f32),
             pltpu.VMEM(shape, f32),
             pltpu.VMEM((ROWS, max(bearings, LANES)), f32),
-            pltpu.SemaphoreType.DMA((2, 6)),
+            pltpu.SemaphoreType.DMA((2, 3, shape[1] // PIECE)),
         ],
         compiler_params=LIMIT,
         name="combine",
-    )(gathered, field, first, second, third_raw, fix, ends, stick, load, prior)
+    )(gathered, field, first, second, third, *fixes, ends, stick, load, prior)
 
 
 def shards(count, right_side, mass_field, span_lengths, stick_flags, normal_load, prior_friction):
@@ -637,13 +655,15 @@
     pairs_b = [p for i in range(1, count - 1, 2) for p in ((i, i + 1), (i + 1, i))]
     got_b = lax.ppermute(message_b, AXES, pairs_b)
     got_a = lax.ppermute(message_a, AXES, pairs_a)
-    first_raw, early, ends = first_call(field, mass, span_lengths.reshape(1, piers), variants)
-    first, second, third_raw, fix, payload = basis_call(
-        per, rows, field, mass, packed, got_a, got_b, first_raw, early, ends, count
+    first, second_raw, early, ends = cyclic_call(
+        field, mass, span_lengths.reshape(1, piers), variants
+    )
+    second, third, fix_first, fix_third, payload = basis_call(
+        per, rows, field, mass, packed, got_a, got_b, first, second_raw, early, ends, count
     )
     gathered = lax.all_to_all(payload, AXES, 0, 0)
     return combine_call(
-        per, gathered, field, first, second, third_raw, fix, ends,
+        per, gathered, field, first, second, third, (fix_first, fix_third), ends,
         stick_flags.reshape(1, bearings), normal_load.reshape(1, bearings), prior_friction,
     )
 

time: 37.9 us -> 33.3 us (0.88)
  local copies, waits for them, and re-layouts: 2.46 us -> 0.02 us
  blocking collectives: 19.3 us -> 17.6 us
  Pallas kernels: 14 us -> 13.6 us
    pallas_call x1, Pallas kernels: 7.52 us -> 4.63 us  [basis_call(): pl.pallas_call(functools.partial(basis_kernel, per), out_shape=(pltpu.VME...]
    unnamed x12 -> x8, local copies, waits for them, and re-layouts: 2.46 us -> 0.02 us
    all_to_all x1, blocking collectives: 19.3 us -> 17.6 us  [shards(): gathered = lax.all_to_all(payload, AXES, 0, 0)]
    pallas_call x1, Pallas kernels: 2.04 us -> 3.7 us  [cyclic_call(): pl.pallas_call(cyclic_kernel, out_shape=(pltpu.VMEM((3,) + padded, f32),...]
    pallas_call x1, Pallas kernels: 1.33 us -> 2.2 us  [pack_call(): pl.pallas_call(pack_kernel, out_shape=(pltpu.VMEM((3, depth + 2, across +...]
  transfers between devices with their start and end apart: 2 -> 2, of which waited for: 0 -> 0; matrix products, arithmetic and copies ran while one was open for 0% -> 0% of each run, Pallas kernels for 5% -> 11%
where the time goes in v3:
time: 33.3 us; the launch traced here: 33.1 us
  blocking collectives  17.6 us (53%)
  Pallas kernels  13.6 us (41%)
  starting transfers between devices  1.17 us (4%)
  between operations  0.72 us (2%)
    all_to_all x1, blocking collectives, shards(): gathered = lax.all_to_all(payload, AXES, 0, 0)  17.6 us
    pallas_call x1, Pallas kernels, basis_call(): pl.pallas_call(functools.partial(basis_kernel, per), out_shape=(pltpu.VME...  4.63 us
    pallas_call x1, Pallas kernels, cyclic_call(): pl.pallas_call(cyclic_kernel, out_shape=(pltpu.VMEM((3,) + padded, f32),...  3.7 us
    pallas_call x1, Pallas kernels, combine_call(): pl.pallas_call(functools.partial(combine_kernel, per), out_shape=(jax.Sha...  3.05 us
    pallas_call x1, Pallas kernels, pack_call(): pl.pallas_call(pack_kernel, out_shape=(pltpu.VMEM((3, depth + 2, across +...  2.2 us
  transfers between devices with their start and end apart: 2, of which 0 were waited for; matrix products, arithmetic and copies ran while one was open for 0% of the time, Pallas kernels for 11%

profile of v3, /device:TPU:0, one launch (start us, length us, event | category | flops | bytes accessed | tf_op | source)
XLA Modules:
  0.0 33.1 jit_solution(3617655714161307799)
XLA Ops:
  0.6 0.0 copy-start.1
  0.6 2.2 %pack.1 = (f32[3,18,80,128]{3,2,1,0:T(8,128)S(1)}, f32[16,64,128]{2,1,0:T(8,128)S(1)}, f32[4,16,8,128]{3,2,1,0:T(8,128)S(1)}, f32[4,8,8,128]{3,2,1,0:T(8,128)S(1)}, f32[4,8,8,128]{3,2,1,0:T(8,128)S(1)}) custom-call(f32[3,16,64,128]{3,2,1,0:T(8,128)} %right_hbm.1, f32[16,64,128]{2,1,0:T(8,128)} %mass_hbm.1), custom_call_target="tpu_custom_call" | custom-call | tf_op jit(solution)/shard_map/pack/pallas_call | solution.py:549
  2.8 0.5 %collective-permute-start = (f32[4,8,8,128]{3,2,1,0:T(8,128)S(1)}, f32[4,8,8,128]{3,2,1,0:T(8,128)S(1)}, u32[]{:S(2)}, u32[]{:S(2)}) collective-permute-start(f32[4,8,8,128]{3,2,1,0:T(8,128)S(1)} %get-tuple-element.20), channel_id=1, source_target_pairs={{0,1},{1,0},{2,3},{3,2},{4,5},{5,4},{6,7},{7,6},{8,9},{9,8},{10,11... | collective-permute-start | bytes 393224 | tf_op jit(solution)/shard_map/ppermute | solution.py:657
  3.4 0.7 %collective-permute-start.1 = (f32[4,8,8,128]{3,2,1,0:T(8,128)S(1)}, f32[4,8,8,128]{3,2,1,0:T(8,128)S(1)}, u32[]{:S(2)}, u32[]{:S(2)}) collective-permute-start(f32[4,8,8,128]{3,2,1,0:T(8,128)S(1)} %get-tuple-element.21), channel_id=1, source_target_pairs={{1,2},{2,1},{3,4},{4,3},{5,6},{6,5},{7,8},{8,7},{9,10},{10,9},{11,... | collective-permute-start | bytes 393224 | tf_op jit(solution)/shard_map/ppermute | solution.py:656
  4.0 0.0 copy-done.1
  4.0 3.7 %cyclic.1 = (f32[3,18,80,128]{3,2,1,0:T(8,128)S(1)}, f32[3,16,64,128]{3,2,1,0:T(8,128)S(1)}, f32[4,8,128]{2,1,0:T(8,128)S(1)}, f32[2,128]{1,0:T(2,128)S(1)}) custom-call(f32[3,18,80,128]{3,2,1,0:T(8,128)S(1)} %get-tuple-element.17.field, f32[16,64,128]{2,1,0:T(8,128)S(1)} %get-tuple-element.18.mass, s32[1,32]{1,0:T(1,128)S(1)} %bitcast.3), custom_call_target="tpu_custom_call" | custom-call | flops 40000000 | bytes 8000000 | tf_op jit(solution)/shard_map/cyclic/pallas_call | solution.py:573
  7.8 0.0 collective-permute-done.got_a
  7.8 0.0 collective-permute-done.1.got_b
  7.8 0.0 copy-start
  7.8 0.0 copy-start.2
  7.8 0.0 copy-start.3
  7.8 4.6 %basis.1 = (f32[3,18,80,128]{3,2,1,0:T(8,128)S(1)}, f32[3,16,64,128]{3,2,1,0:T(8,128)S(1)}, f32[3,16,8,128]{3,2,1,0:T(8,128)S(1)}, f32[3,16,8,128]{3,2,1,0:T(8,128)S(1)}, f32[32,8,128]{2,1,0:T(8,128)S(1)}) custom-call(f32[3,18,80,128]{3,2,1,0:T(8,128)S(1)} %get-tuple-element.17.field, f32[16,64,128]{2,1,0:T(8,128)S(1)} %get-tuple-element.18.mass, ...), custom_call_target="tpu_custom_call" | custom-call | tf_op jit(solution)/shard_map/basis/pallas_call | solution.py:596
  12.4 17.6 %all_to_all.5.gathered = f32[32,8,128]{2,1,0:T(8,128)S(1)} all-to-all(f32[32,8,128]{2,1,0:T(8,128)S(1)} %get-tuple-element.26), channel_id=1, replica_groups=mesh['len'=8,'xs'=4] {'len','xs'}, dimensions={0} | all-to-all | bytes 262144 | tf_op jit(solution)/shard_map/all_to_all | solution.py:664
  30.1 0.0 copy-done
  30.1 0.0 copy-done.2
  30.1 0.0 copy-done.3
  30.1 3.0 %combine.1 = (f32[3,16,64,128]{3,2,1,0:T(8,128)}, f32[3,16,64,128]{3,2,1,0:T(8,128)}, f32[2,64]{1,0:T(2,128)}) custom-call(f32[32,8,128]{2,1,0:T(8,128)S(1)} %all_to_all.5.gathered, f32[3,18,80,128]{3,2,1,0:T(8,128)S(1)} %get-tuple-element.17.field, f32[3,18,80,128]{3,2,1,0:T(8,128)S(1)} %get-tuple-element.22.first, ...), custom_call_target="tpu_custom_call" | custom-call | tf_op jit(solution)/shard_map/combine/pallas_call | solution.py:625
Async XLA Ops:
  0.6 3.4 %copy-start.1 = (s32[32]{0:T(128)S(1)}, s32[32]{0:T(128)}, u32[]{:S(2)}) copy-start(s32[32]{0:T(128)} %param.8) | copy-start | bytes 388
  2.8 4.9 %collective-permute-start = (f32[4,8,8,128]{3,2,1,0:T(8,128)S(1)}, f32[4,8,8,128]{3,2,1,0:T(8,128)S(1)}, u32[]{:S(2)}, u32[]{:S(2)}) collective-permute-start(f32[4,8,8,128]{3,2,1,0:T(8,128)S(1)} %get-tuple-element.20), channel_id=1, source_target_pairs={{0,1},{1,0},{2,3},{3,2},{4,5},{5,4},{6,7},{7,6},{8,9},{9,8},{10,11... | collective-permute-start | bytes 393224 | tf_op jit(solution)/shard_map/ppermute | solution.py:657
  3.4 4.4 %collective-permute-start.1 = (f32[4,8,8,128]{3,2,1,0:T(8,128)S(1)}, f32[4,8,8,128]{3,2,1,0:T(8,128)S(1)}, u32[]{:S(2)}, u32[]{:S(2)}) collective-permute-start(f32[4,8,8,128]{3,2,1,0:T(8,128)S(1)} %get-tuple-element.21), channel_id=1, source_target_pairs={{1,2},{2,1},{3,4},{4,3},{5,6},{6,5},{7,8},{8,7},{9,10},{10,9},{11,... | collective-permute-start | bytes 393224 | tf_op jit(solution)/shard_map/ppermute | solution.py:656
  7.8 22.3 %copy-start = (f32[2,64]{1,0:T(2,128)S(1)}, f32[2,64]{1,0:T(2,128)}, u32[]{:S(2)}) copy-start(f32[2,64]{1,0:T(2,128)} %prior.1) | copy-start | bytes 1540
  7.8 22.3 %copy-start.2 = (s32[64]{0:T(128)S(1)}, s32[64]{0:T(128)}, u32[]{:S(2)}) copy-start(s32[64]{0:T(128)} %param.9) | copy-start | bytes 772
  7.8 22.3 %copy-start.3 = (f32[64]{0:T(128)S(1)}, f32[64]{0:T(128)}, u32[]{:S(2)}) copy-start(f32[64]{0:T(128)} %param.10) | copy-start | bytes 772

commit v4 on v3

--- a/solution.py
+++ b/solution.py
@@ -25,7 +25,7 @@
 BLOCKS = LANES // EDGE
 PITCH = 3 * ROWS
 CHUNK = 16
-PIECE = 4
+PIECE = 16
 HIGH = lax.Precision.HIGHEST
 LIMIT = pltpu.CompilerParams(vmem_limit_bytes=32 * 1024 * 1024)
 
@@ -323,34 +323,6 @@
 
     edge_sums = [edge_step(level) for level in range(ITERS)]
 
-    clear_padding(div, (), depth, across)
-    for c in comps:
-        clear_padding(second, (c,), depth, across)
-
-    def mend(d, carry):
-        for c in comps:
-            edges = fix_second[c, d]
-            for r in range(0, across, CHUNK):
-                second[c, d + 1, pl.ds(PAD + r, CHUNK), :] = mended(
-                    second_raw[c, d, r : r + CHUNK, :], edges, r, 4
-                )
-        return carry
-
-    loop(depth, 4, mend, 0)
-
-    def store_third(c, d, r, out):
-        third[c, d, r : r + CHUNK, :] = out
-
-    norm, cross = cyclic_step(second, mass, div, store_third, 4)
-    parts = [
-        early[0],
-        early[1] + middle(edge_sums[0][1], 2),
-        early[2] + middle(edge_sums[1][0], 2),
-        early[3] + middle(edge_sums[1][1], 4),
-        norm,
-        interior(cross, 2) + middle(edge_sums[2][1], 2),
-    ]
-
     variants = ends.shape[0]
     pieces = 1 if per > 1 else variants
     blocks = 3 * ITERS * pieces
@@ -359,15 +331,17 @@
     for block in range(blocks):
         value, piece = block // pieces, block % pieces
         row, z = block // per, (block % per if per > 1 else piece)
-        ref, c = (field, first, second)[value // 3], value % 3
+        level, c = value // 3, value % 3
         for side in both:
-            place = PAD + (1 + 2 * side) * across // 4
+            place = (1 + 2 * side) * across // 4
             column = (2 * z + side) * LANES
-            here = ref[c, 1, place : place + 1, :]
-            if ref is first:
-                r = place - PAD
-                edges = fix_first[c, 0, r % ROWS : r % ROWS + 1, :]
-                here = mended(here, edges, r, 2)
+            if level < 2:
+                here = (field, first)[level][c, 1, PAD + place : PAD + place + 1, :]
+            else:
+                here = second_raw[c, 0, place : place + 1, :]
+            if level:
+                edges = fixes[level][c, 0, place % ROWS : place % ROWS + 1, :]
+                here = mended(here, edges, place, 2 * level)
             picked[row : row + 1, column : column + LANES] = here
     start = (index * LANES).astype(jnp.float32)
     along = lax.broadcasted_iota(jnp.int32, (LANES, LANES), 0).astype(jnp.float32) + start
@@ -382,6 +356,35 @@
                 picked[:, column : column + LANES], hit,
                 precision=HIGH, preferred_element_type=jnp.float32,
             )
+
+    clear_padding(div, (), depth, across)
+    for c in comps:
+        clear_padding(second, (c,), depth, across)
+
+    def mend(d, carry):
+        for c in comps:
+            edges = fix_second[c, d]
+            for r in range(0, across, CHUNK):
+                second[c, d + 1, pl.ds(PAD + r, CHUNK), :] = mended(
+                    second_raw[c, d, r : r + CHUNK, :], edges, r, 4
+                )
+        return carry
+
+    loop(depth, 4, mend, 0)
+
+    def store_third(c, d, r, out):
+        third[c, d, r : r + CHUNK, :] = out
+
+    norm, cross = cyclic_step(second, mass, div, store_third, 4)
+    parts = [
+        early[0],
+        early[1] + middle(edge_sums[0][1], 2),
+        early[2] + middle(edge_sums[1][0], 2),
+        early[3] + middle(edge_sums[1][1], 4),
+        norm,
+        interior(cross, 2) + middle(edge_sums[2][1], 2),
+    ]
+
     sums[...] = jnp.zeros(sums.shape, jnp.float32)
     sums[0:bearing_rows, :] = total[0:bearing_rows]
     low = lane_iota((1, LANES)) < LANES // 2
@@ -432,8 +435,8 @@
 
 def combine_kernel(
     per, gathered, field, first, second, third, fix_first, fix_third, ends, stick, load, prior,
-    increment_hbm, residual_hbm, friction,
-    increment, residual, forces, sems,
+    increment_hbm, residual_hbm, friction_hbm,
+    increment, residual, friction, forces, sems, friction_sem,
 ):
     depth, across = third.shape[1], third.shape[2]
     start = (device_index() * LANES).astype(jnp.float32)
@@ -483,6 +486,8 @@
                 forces[2 * c + side : 2 * c + side + 1, span] = jnp.where(
                     lane % 2 == side, force[c], 0.0
                 )
+    friction_copy = pltpu.make_async_copy(friction, friction_hbm, friction_sem)
+    friction_copy.start()
     along = lax.broadcasted_iota(jnp.int32, (LANES, LANES), 0).astype(jnp.float32) + start
     placed = jnp.zeros((8, LANES), jnp.float32)
     for piece in range(pieces):
@@ -492,20 +497,20 @@
             (((1,), (1,)), ((), ())), precision=HIGH, preferred_element_type=jnp.float32,
         )
 
-    grow = [jnp.broadcast_to(g, (CHUNK, LANES)) for g in grow]
-    keep = [jnp.broadcast_to(g, (CHUNK, LANES)) for g in keep]
+    grow = [jnp.broadcast_to(g, (ROWS, LANES)) for g in grow]
+    keep = [jnp.broadcast_to(g, (ROWS, LANES)) for g in keep]
 
     def run(c, begin, end):
         for d in range(begin, end):
             edges = fix_first[c, d], fix_third[c, d]
-            for r in range(0, across, CHUNK):
-                here = pl.ds(PAD + r, CHUNK)
+            for r in range(0, across, ROWS):
+                here = pl.ds(PAD + r, ROWS)
                 v = [ref[c, d + 1, here, :] for ref in (field, first, second)]
-                v.append(third[c, d, r : r + CHUNK, :])
+                v.append(third[c, d, r : r + ROWS, :])
                 v[1] = mended(v[1], edges[0], r, 2)
                 v[3] = mended(v[3], edges[1], r, 2)
-                increment[c, d, r : r + CHUNK, :] = grow[0] * v[0] + grow[1] * v[1] + grow[2] * v[2]
-                residual[c, d, r : r + CHUNK, :] = (
+                increment[c, d, r : r + ROWS, :] = grow[0] * v[0] + grow[1] * v[1] + grow[2] * v[2]
+                residual[c, d, r : r + ROWS, :] = (
                     keep[0] * v[0] + keep[1] * v[1] + (keep[2] * v[2] + keep[3] * v[3])
                 )
 
@@ -528,6 +533,7 @@
                     )
             for which in range(2):
                 copy(which, c, begin).start()
+    friction_copy.wait()
     for c in range(3):
         for begin in starts:
             for which in range(2):
@@ -630,12 +636,14 @@
             jax.ShapeDtypeStruct((2, bearings), f32),
         ),
         in_specs=[vmem_spec()] * 11,
-        out_specs=(hbm_spec(), hbm_spec(), vmem_spec()),
+        out_specs=(hbm_spec(),) * 3,
         scratch_shapes=[
             pltpu.VMEM(shape, f32),
             pltpu.VMEM(shape, f32),
+            pltpu.VMEM((2, bearings), f32),
             pltpu.VMEM((ROWS, max(bearings, LANES)), f32),
             pltpu.SemaphoreType.DMA((2, 3, shape[1] // PIECE)),
+            pltpu.SemaphoreType.DMA(()),
         ],
         compiler_params=LIMIT,
         name="combine",
@@ -653,8 +661,8 @@
     field, mass, packed, message_a, message_b = pack_call(right_side, mass_field)
     pairs_a = [p for i in range(0, count - 1, 2) for p in ((i, i + 1), (i + 1, i))]
     pairs_b = [p for i in range(1, count - 1, 2) for p in ((i, i + 1), (i + 1, i))]
+    got_a = lax.ppermute(message_a, AXES, pairs_a)
     got_b = lax.ppermute(message_b, AXES, pairs_b)
-    got_a = lax.ppermute(message_a, AXES, pairs_a)
     first, second_raw, early, ends = cyclic_call(
         field, mass, span_lengths.reshape(1, piers), variants
     )

time: 33.3 us -> 32.3 us (0.970)
  Pallas kernels: 13.6 us -> 12.6 us
    pallas_call x1, Pallas kernels: 3.05 us -> 2.31 us  [combine_call(): pl.pallas_call(functools.partial(combine_kernel, per), out_shape=(jax.Sha...]
  transfers between devices with their start and end apart: 2 -> 2, of which waited for: 0 -> 0; matrix products, arithmetic and copies ran while one was open for 0% -> 0% of each run, Pallas kernels for 11% -> 12%
where the time goes in v4:
time: 32.3 us; the launch traced here: 32.2 us
  blocking collectives  17.6 us (54%)
  Pallas kernels  12.6 us (39%)
  starting transfers between devices  1.17 us (4%)
  between operations  0.72 us (2%)
    all_to_all x1, blocking collectives, shards(): gathered = lax.all_to_all(payload, AXES, 0, 0)  17.6 us
    pallas_call x1, Pallas kernels, basis_call(): pl.pallas_call(functools.partial(basis_kernel, per), out_shape=(pltpu.VME...  4.41 us
    pallas_call x1, Pallas kernels, cyclic_call(): pl.pallas_call(cyclic_kernel, out_shape=(pltpu.VMEM((3,) + padded, f32),...  3.7 us
    pallas_call x1, Pallas kernels, combine_call(): pl.pallas_call(functools.partial(combine_kernel, per), out_shape=(jax.Sha...  2.31 us
    pallas_call x1, Pallas kernels, pack_call(): pl.pallas_call(pack_kernel, out_shape=(pltpu.VMEM((3, depth + 2, across +...  2.2 us
    ppermute x1, starting transfers between devices, shards(): got_b = lax.ppermute(message_b, AXES, pairs_b)  0.66 us
  transfers between devices with their start and end apart: 2, of which 0 were waited for; matrix products, arithmetic and copies ran while one was open for 0% of the time, Pallas kernels for 12%

profile of v4, /device:TPU:0, one launch (start us, length us, event | category | flops | bytes accessed | tf_op | source)
XLA Modules:
  0.0 32.2 jit_solution(17305476306176348186)
XLA Ops:
  0.6 0.0 copy-start.1
  0.6 2.2 %pack.1 = (f32[3,18,80,128]{3,2,1,0:T(8,128)S(1)}, f32[16,64,128]{2,1,0:T(8,128)S(1)}, f32[4,16,8,128]{3,2,1,0:T(8,128)S(1)}, f32[4,8,8,128]{3,2,1,0:T(8,128)S(1)}, f32[4,8,8,128]{3,2,1,0:T(8,128)S(1)}) custom-call(f32[3,16,64,128]{3,2,1,0:T(8,128)} %right_hbm.1, f32[16,64,128]{2,1,0:T(8,128)} %mass_hbm.1), custom_call_target="tpu_custom_call" | custom-call | tf_op jit(solution)/shard_map/pack/pallas_call | solution.py:555
  2.8 0.5 %collective-permute-start = (f32[4,8,8,128]{3,2,1,0:T(8,128)S(1)}, f32[4,8,8,128]{3,2,1,0:T(8,128)S(1)}, u32[]{:S(2)}, u32[]{:S(2)}) collective-permute-start(f32[4,8,8,128]{3,2,1,0:T(8,128)S(1)} %get-tuple-element.20), channel_id=1, source_target_pairs={{0,1},{1,0},{2,3},{3,2},{4,5},{5,4},{6,7},{7,6},{8,9},{9,8},{10,11... | collective-permute-start | bytes 393224 | tf_op jit(solution)/shard_map/ppermute | solution.py:664
  3.4 0.7 %collective-permute-start.1 = (f32[4,8,8,128]{3,2,1,0:T(8,128)S(1)}, f32[4,8,8,128]{3,2,1,0:T(8,128)S(1)}, u32[]{:S(2)}, u32[]{:S(2)}) collective-permute-start(f32[4,8,8,128]{3,2,1,0:T(8,128)S(1)} %get-tuple-element.21), channel_id=1, source_target_pairs={{1,2},{2,1},{3,4},{4,3},{5,6},{6,5},{7,8},{8,7},{9,10},{10,9},{11,... | collective-permute-start | bytes 393224 | tf_op jit(solution)/shard_map/ppermute | solution.py:665
  4.0 0.0 copy-done.1
  4.0 3.7 %cyclic.1 = (f32[3,18,80,128]{3,2,1,0:T(8,128)S(1)}, f32[3,16,64,128]{3,2,1,0:T(8,128)S(1)}, f32[4,8,128]{2,1,0:T(8,128)S(1)}, f32[2,128]{1,0:T(2,128)S(1)}) custom-call(f32[3,18,80,128]{3,2,1,0:T(8,128)S(1)} %get-tuple-element.17.field, f32[16,64,128]{2,1,0:T(8,128)S(1)} %get-tuple-element.18.mass, s32[1,32]{1,0:T(1,128)S(1)} %bitcast.3), custom_call_target="tpu_custom_call" | custom-call | flops 40000000 | bytes 8000000 | tf_op jit(solution)/shard_map/cyclic/pallas_call | solution.py:579
  7.8 0.0 collective-permute-done.got_a
  7.8 0.0 collective-permute-done.1.got_b
  7.8 0.0 copy-start
  7.8 0.0 copy-start.2
  7.8 0.0 copy-start.3
  7.8 4.4 %basis.1 = (f32[3,18,80,128]{3,2,1,0:T(8,128)S(1)}, f32[3,16,64,128]{3,2,1,0:T(8,128)S(1)}, f32[3,16,8,128]{3,2,1,0:T(8,128)S(1)}, f32[3,16,8,128]{3,2,1,0:T(8,128)S(1)}, f32[32,8,128]{2,1,0:T(8,128)S(1)}) custom-call(f32[3,18,80,128]{3,2,1,0:T(8,128)S(1)} %get-tuple-element.17.field, f32[16,64,128]{2,1,0:T(8,128)S(1)} %get-tuple-element.18.mass, ...), custom_call_target="tpu_custom_call" | custom-call | tf_op jit(solution)/shard_map/basis/pallas_call | solution.py:602
  12.2 17.6 %all_to_all.5.gathered = f32[32,8,128]{2,1,0:T(8,128)S(1)} all-to-all(f32[32,8,128]{2,1,0:T(8,128)S(1)} %get-tuple-element.26), channel_id=1, replica_groups=mesh['len'=8,'xs'=4] {'len','xs'}, dimensions={0} | all-to-all | bytes 262144 | tf_op jit(solution)/shard_map/all_to_all | solution.py:672
  29.8 0.0 copy-done
  29.8 0.0 copy-done.2
  29.8 0.0 copy-done.3
  29.8 2.3 %combine.1 = (f32[3,16,64,128]{3,2,1,0:T(8,128)}, f32[3,16,64,128]{3,2,1,0:T(8,128)}, f32[2,64]{1,0:T(2,128)}) custom-call(f32[32,8,128]{2,1,0:T(8,128)S(1)} %all_to_all.5.gathered, f32[3,18,80,128]{3,2,1,0:T(8,128)S(1)} %get-tuple-element.17.field, f32[3,18,80,128]{3,2,1,0:T(8,128)S(1)} %get-tuple-element.22.first, ...), custom_call_target="tpu_custom_call" | custom-call | tf_op jit(solution)/shard_map/combine/pallas_call | solution.py:631
Async XLA Ops:
  0.6 3.4 %copy-start.1 = (s32[32]{0:T(128)S(1)}, s32[32]{0:T(128)}, u32[]{:S(2)}) copy-start(s32[32]{0:T(128)} %param.8) | copy-start | bytes 388
  2.8 4.9 %collective-permute-start = (f32[4,8,8,128]{3,2,1,0:T(8,128)S(1)}, f32[4,8,8,128]{3,2,1,0:T(8,128)S(1)}, u32[]{:S(2)}, u32[]{:S(2)}) collective-permute-start(f32[4,8,8,128]{3,2,1,0:T(8,128)S(1)} %get-tuple-element.20), channel_id=1, source_target_pairs={{0,1},{1,0},{2,3},{3,2},{4,5},{5,4},{6,7},{7,6},{8,9},{9,8},{10,11... | collective-permute-start | bytes 393224 | tf_op jit(solution)/shard_map/ppermute | solution.py:664
  3.4 4.4 %collective-permute-start.1 = (f32[4,8,8,128]{3,2,1,0:T(8,128)S(1)}, f32[4,8,8,128]{3,2,1,0:T(8,128)S(1)}, u32[]{:S(2)}, u32[]{:S(2)}) collective-permute-start(f32[4,8,8,128]{3,2,1,0:T(8,128)S(1)} %get-tuple-element.21), channel_id=1, source_target_pairs={{1,2},{2,1},{3,4},{4,3},{5,6},{6,5},{7,8},{8,7},{9,10},{10,9},{11,... | collective-permute-start | bytes 393224 | tf_op jit(solution)/shard_map/ppermute | solution.py:665
  7.8 22.1 %copy-start = (f32[2,64]{1,0:T(2,128)S(1)}, f32[2,64]{1,0:T(2,128)}, u32[]{:S(2)}) copy-start(f32[2,64]{1,0:T(2,128)} %prior.1) | copy-start | bytes 1540
  7.8 22.1 %copy-start.2 = (s32[64]{0:T(128)S(1)}, s32[64]{0:T(128)}, u32[]{:S(2)}) copy-start(s32[64]{0:T(128)} %param.9) | copy-start | bytes 772
  7.8 22.0 %copy-start.3 = (f32[64]{0:T(128)S(1)}, f32[64]{0:T(128)}, u32[]{:S(2)}) copy-start(f32[64]{0:T(128)} %param.10) | copy-start | bytes 772

commit v5 on v4

--- a/solution.py
+++ b/solution.py
@@ -26,6 +26,7 @@
 PITCH = 3 * ROWS
 CHUNK = 16
 PIECE = 16
+MARGINS = (6, 5, 5)
 HIGH = lax.Precision.HIGHEST
 LIMIT = pltpu.CompilerParams(vmem_limit_bytes=32 * 1024 * 1024)
 
@@ -105,24 +106,42 @@
     return sum(x[i : i + ROWS] for i in range(0, x.shape[0], ROWS))
 
 
-def cyclic_step(source, mass, div, store, step):
+def cyclic_step(source, mass, div, store, step, inner_source=None, inner_div=None):
     depth, across = mass.shape[0], mass.shape[1]
     chunks = range(0, across, CHUNK)
+    block_of = lane_iota((ROWS, LANES)) // EDGE
+
+    def pack(edge, r, tile):
+        for i in range(0, CHUNK, ROWS):
+            b = (r + i) // ROWS
+            moved = turn(tile[i : i + ROWS], EDGE * b + HALF)
+            edge = moved if edge is None else jnp.where(block_of == b, moved, edge)
+        return edge
 
     def divergence(d, carry):
+        edge, edge_div = None, None
         for r in chunks:
             here, up, down = (pl.ds(PAD + r + by, CHUNK) for by in (0, 1, -1))
             x = source[0, d + 1, here, :]
             w = turn(x, -1) - turn(x, 1)
             w = w + (source[1, d + 1, up, :] - source[1, d + 1, down, :])
             w = w + (source[2, d + 2, here, :] - source[2, d, here, :])
-            div[d + 1, here, :] = w * (0.25 * BULK)
+            w = w * (0.25 * BULK)
+            div[d + 1, here, :] = w
+            if inner_source is not None:
+                edge = pack(edge, r, x)
+            if inner_div is not None:
+                edge_div = pack(edge_div, r, w)
+        if inner_source is not None:
+            inner_source[d] = edge
+        if inner_div is not None:
+            inner_div[d] = edge_div
         return carry
 
     loop(depth, step, divergence, 0)
 
     def image(d, carry):
-        norm, cross = carry
+        norm, cross, cross_rest = carry
         for r in chunks:
             here, up, down = (pl.ds(PAD + r + by, CHUNK) for by in (0, 1, -1))
             diag = mass[d, r : r + CHUNK, :]
@@ -145,10 +164,11 @@
                 norms.append(x * x)
                 crosses.append(x * out)
             norm = norm + folded(norms[0] + norms[1] + norms[2])
-            cross = cross + folded(crosses[0] + crosses[1] + crosses[2])
-        return norm, cross
-
-    return loop(depth, step, image, (jnp.zeros((ROWS, LANES), jnp.float32),) * 2)
+            cross = cross + folded(crosses[0])
+            cross_rest = cross_rest + folded(crosses[1] + crosses[2])
+        return norm, cross, cross_rest
+
+    return loop(depth, step, image, (jnp.zeros((ROWS, LANES), jnp.float32),) * 3)
 
 
 def interior(value, margin):
@@ -156,24 +176,33 @@
     return jnp.where((lane >= margin) & (lane < LANES - margin), value, 0.0)
 
 
-def cyclic_kernel(field, mass, spans, first, second, moments, ends, div):
+def cyclic_kernel(field, mass, spans, first, second, third, inner, moments, ends, div):
     depth, across = mass.shape[0], mass.shape[1]
     clear_padding(div, (), depth, across)
     for c in range(3):
         clear_padding(first, (c,), depth, across)
+        clear_padding(second, (c,), depth, across)
 
     def store_first(c, d, r, out):
         first[c, d + 1, pl.ds(PAD + r, CHUNK), :] = out
 
     def store_second(c, d, r, out):
-        second[c, d, r : r + CHUNK, :] = out
-
-    norm, cross = cyclic_step(field, mass, div, store_first, 4)
+        second[c, d + 1, pl.ds(PAD + r, CHUNK), :] = out
+
+    def store_third(c, d, r, out):
+        third[c, d, r : r + CHUNK, :] = out
+
+    norm, cross, cross_rest = cyclic_step(field, mass, div, store_first, 4)
     moments[0] = norm
-    moments[1] = interior(cross, 2)
-    norm, cross = cyclic_step(first, mass, div, store_second, 4)
+    moments[1] = interior(cross + cross_rest, 2)
+    norm, cross, cross_rest = cyclic_step(first, mass, div, store_second, 4, inner.at[0])
     moments[2] = interior(norm, 2)
-    moments[3] = interior(cross, 4)
+    moments[3] = interior(cross + cross_rest, 4)
+    norm, cross, cross_rest = cyclic_step(
+        second, mass, div, store_third, 4, inner.at[1], inner.at[2]
+    )
+    moments[4] = interior(norm, 4)
+    moments[5] = interior(cross, MARGINS[0]) + interior(cross_rest, MARGINS[1])
     piers = spans.shape[1]
     bearings = 2 * piers
     lane = lane_iota((piers, LANES))
@@ -199,12 +228,12 @@
     )
 
 
-def basis_kernel(
-    per, field, mass, packed, got_a, got_b, first, second_raw, early, ends,
-    second, third, fix_first, fix_third, payload,
-    div, edge, edge_div, edge_diag, fix_second, sums, picked,
+def edge_kernel(
+    per, packed, got_a, got_b, inner, field, first, second, early, ends,
+    fix_first, fix_second, fix_third, payload,
+    edge, edge_div, edge_diag, sums, picked,
 ):
-    depth, across = mass.shape[0], mass.shape[1]
+    depth, across = packed.shape[1], first.shape[2] - 2 * PAD
     index = device_index()
     count = lax.axis_size(AXES[0]) * lax.axis_size(AXES[1])
     is_even = index % 2 == 0
@@ -278,6 +307,11 @@
         return jnp.where((spot >= HALF - margin) & (spot < HALF + margin), value, 0.0)
 
     fixes = (packed, fix_first, fix_second, fix_third)
+    last_planes = lane % EDGE >= EDGE - 2
+    first_planes = lane % EDGE < 2
+
+    def joined(s, value, own):
+        return jnp.where(first_planes if s else last_planes, own, value)
 
     def edge_step(level):
         for s in both:
@@ -289,10 +323,12 @@
                 w = turn(x, -1) - turn(x, 1)
                 w = w + (at(s, 1, d, 1) - at(s, 1, d, -1))
                 w = w + (at(s, 2, d + 1) - at(s, 2, d - 1))
-                edge_div[s, pl.ds(row_of(d), ROWS), :] = w * ((0.25 * BULK) * keep[s])
+                w = w * ((0.25 * BULK) * keep[s])
+                edge_div[s, pl.ds(row_of(d), ROWS), :] = joined(s, w, inner[2, d]) if level == 2 else w
             join_blocks(edge_div, (s,))
-        norm, cross = blank, blank
+        norms, crosses = [], []
         for c in comps:
+            norm, cross = blank, blank
             images = []
             for d in range(depth):
                 pair = []
@@ -316,10 +352,15 @@
                 fixes[level + 1][c, d] = new
                 norm = norm + old * old
                 cross = cross + old * new
+            norms.append(norm)
+            crosses.append(cross)
+            if level + 1 == ITERS:
+                continue
             for d in range(depth):
                 for s in both:
-                    edge[s, c, pl.ds(row_of(d), ROWS), :] = images[d][s]
-        return norm, cross
+                    value = images[d][s] if c else joined(s, images[d][s], inner[level, d])
+                    edge[s, c, pl.ds(row_of(d), ROWS), :] = value
+        return norms, crosses
 
     edge_sums = [edge_step(level) for level in range(ITERS)]
 
@@ -335,10 +376,7 @@
         for side in both:
             place = (1 + 2 * side) * across // 4
             column = (2 * z + side) * LANES
-            if level < 2:
-                here = (field, first)[level][c, 1, PAD + place : PAD + place + 1, :]
-            else:
-                here = second_raw[c, 0, place : place + 1, :]
+            here = (field, first, second)[level][c, 1, PAD + place : PAD + place + 1, :]
             if level:
                 edges = fixes[level][c, 0, place % ROWS : place % ROWS + 1, :]
                 here = mended(here, edges, place, 2 * level)
@@ -357,32 +395,16 @@
                 precision=HIGH, preferred_element_type=jnp.float32,
             )
 
-    clear_padding(div, (), depth, across)
-    for c in comps:
-        clear_padding(second, (c,), depth, across)
-
-    def mend(d, carry):
-        for c in comps:
-            edges = fix_second[c, d]
-            for r in range(0, across, CHUNK):
-                second[c, d + 1, pl.ds(PAD + r, CHUNK), :] = mended(
-                    second_raw[c, d, r : r + CHUNK, :], edges, r, 4
-                )
-        return carry
-
-    loop(depth, 4, mend, 0)
-
-    def store_third(c, d, r, out):
-        third[c, d, r : r + CHUNK, :] = out
-
-    norm, cross = cyclic_step(second, mass, div, store_third, 4)
+    def at_edge(values, margins):
+        return sum(middle(v, m) for v, m in zip(values, margins))
+
     parts = [
         early[0],
-        early[1] + middle(edge_sums[0][1], 2),
-        early[2] + middle(edge_sums[1][0], 2),
-        early[3] + middle(edge_sums[1][1], 4),
-        norm,
-        interior(cross, 2) + middle(edge_sums[2][1], 2),
+        early[1] + at_edge(edge_sums[0][1], (2, 2, 2)),
+        early[2] + at_edge(edge_sums[1][0], (2, 2, 2)),
+        early[3] + at_edge(edge_sums[1][1], (4, 4, 4)),
+        early[4] + at_edge(edge_sums[2][0], (4, 4, 4)),
+        early[5] + at_edge(edge_sums[2][1], MARGINS),
     ]
 
     sums[...] = jnp.zeros(sums.shape, jnp.float32)
@@ -434,7 +456,8 @@
 
 
 def combine_kernel(
-    per, gathered, field, first, second, third, fix_first, fix_third, ends, stick, load, prior,
+    per, gathered, field, first, second, third, packed, fix_first, fix_second, fix_third,
+    ends, stick, load, prior,
     increment_hbm, residual_hbm, friction_hbm,
     increment, residual, friction, forces, sems, friction_sem,
 ):
@@ -500,19 +523,20 @@
     grow = [jnp.broadcast_to(g, (ROWS, LANES)) for g in grow]
     keep = [jnp.broadcast_to(g, (ROWS, LANES)) for g in keep]
 
+    def total_of(terms, values):
+        parts = [t * v for t, v in zip(terms, values)]
+        return parts[0] + parts[1] + (parts[2] if len(parts) == 3 else parts[2] + parts[3])
+
     def run(c, begin, end):
         for d in range(begin, end):
-            edges = fix_first[c, d], fix_third[c, d]
+            edges = [ref[c, d] for ref in (packed, fix_first, fix_second, fix_third)]
+            edges = total_of(grow, edges), total_of(keep, edges)
             for r in range(0, across, ROWS):
                 here = pl.ds(PAD + r, ROWS)
                 v = [ref[c, d + 1, here, :] for ref in (field, first, second)]
                 v.append(third[c, d, r : r + ROWS, :])
-                v[1] = mended(v[1], edges[0], r, 2)
-                v[3] = mended(v[3], edges[1], r, 2)
-                increment[c, d, r : r + ROWS, :] = grow[0] * v[0] + grow[1] * v[1] + grow[2] * v[2]
-                residual[c, d, r : r + ROWS, :] = (
-                    keep[0] * v[0] + keep[1] * v[1] + (keep[2] * v[2] + keep[3] * v[3])
-                )
+                for ref, terms, edge in ((increment, grow, edges[0]), (residual, keep, edges[1])):
+                    ref[c, d, r : r + ROWS, :] = mended(total_of(terms, v), edge, r, MARGINS[c])
 
     def copy(which, c, begin):
         ref, hbm = ((increment, increment_hbm), (residual, residual_hbm))[which]
@@ -580,51 +604,44 @@
         cyclic_kernel,
         out_shape=(
             pltpu.VMEM((3,) + padded, f32),
+            pltpu.VMEM((3,) + padded, f32),
             pltpu.VMEM((3, depth, across, along), f32),
-            pltpu.VMEM((4, ROWS, LANES), f32),
+            pltpu.VMEM((3, depth, ROWS, LANES), f32),
+            pltpu.VMEM((6, ROWS, LANES), f32),
             pltpu.VMEM((variants, LANES), f32),
         ),
         in_specs=[vmem_spec()] * 3,
-        out_specs=(vmem_spec(),) * 4,
+        out_specs=(vmem_spec(),) * 6,
         scratch_shapes=[pltpu.VMEM(padded, f32)],
         compiler_params=LIMIT,
-        cost_estimate=pl.CostEstimate(flops=40_000_000, bytes_accessed=8_000_000, transcendentals=0),
+        cost_estimate=pl.CostEstimate(flops=60_000_000, bytes_accessed=12_000_000, transcendentals=0),
         name="cyclic",
     )(field, mass, spans)
 
 
-def basis_call(per, rows, field, mass, packed, got_a, got_b, first, second_raw, early, ends, count):
+def edge_call(per, rows, packed, got_a, got_b, inner, field, first, second, early, ends, count):
     f32 = jnp.float32
-    depth, across, along = mass.shape
+    depth = packed.shape[1]
     variants = ends.shape[0]
-    padded = (depth + 2, across + 2 * PAD, along)
     edges = (3, depth, ROWS, LANES)
     return pl.pallas_call(
-        functools.partial(basis_kernel, per),
-        out_shape=(
-            pltpu.VMEM((3,) + padded, f32),
-            pltpu.VMEM((3, depth, across, along), f32),
-            pltpu.VMEM(edges, f32),
-            pltpu.VMEM(edges, f32),
-            jax.ShapeDtypeStruct((count, rows, LANES), f32),
-        ),
+        functools.partial(edge_kernel, per),
+        out_shape=(pltpu.VMEM(edges, f32),) * 3 + (pltpu.VMEM((count, rows, LANES), f32),),
         in_specs=[vmem_spec()] * 9,
-        out_specs=(vmem_spec(),) * 5,
+        out_specs=(vmem_spec(),) * 4,
         scratch_shapes=[
-            pltpu.VMEM(padded, f32),
             pltpu.VMEM((2, 3, (depth + 2) * PITCH, LANES), f32),
             pltpu.VMEM((2, (depth + 2) * PITCH, LANES), f32),
             pltpu.VMEM((2, depth, ROWS, LANES), f32),
-            pltpu.VMEM(edges, f32),
             pltpu.VMEM((rows, LANES), f32),
             pltpu.VMEM((rows, 2 * variants * LANES), f32),
         ],
         compiler_params=LIMIT,
-        name="basis",
-    )(field, mass, packed, got_a, got_b, first, second_raw, early, ends)
-
-
-def combine_call(per, gathered, field, first, second, third, fixes, ends, stick, load, prior):
+        name="edge",
+    )(packed, got_a, got_b, inner, field, first, second, early, ends)
+
+
+def combine_call(per, gathered, field, first, second, third, edges, ends, stick, load, prior):
     f32 = jnp.float32
     shape = third.shape
     bearings = load.shape[1]
@@ -635,7 +652,7 @@
             jax.ShapeDtypeStruct(shape, f32),
             jax.ShapeDtypeStruct((2, bearings), f32),
         ),
-        in_specs=[vmem_spec()] * 11,
+        in_specs=[vmem_spec()] * 13,
         out_specs=(hbm_spec(),) * 3,
         scratch_shapes=[
             pltpu.VMEM(shape, f32),
@@ -647,7 +664,7 @@
         ],
         compiler_params=LIMIT,
         name="combine",
-    )(gathered, field, first, second, third, *fixes, ends, stick, load, prior)
+    )(gathered, field, first, second, third, *edges, ends, stick, load, prior)
 
 
 def shards(count, right_side, mass_field, span_lengths, stick_flags, normal_load, prior_friction):
@@ -663,15 +680,15 @@
     pairs_b = [p for i in range(1, count - 1, 2) for p in ((i, i + 1), (i + 1, i))]
     got_a = lax.ppermute(message_a, AXES, pairs_a)
     got_b = lax.ppermute(message_b, AXES, pairs_b)
-    first, second_raw, early, ends = cyclic_call(
+    first, second, third, inner, early, ends = cyclic_call(
         field, mass, span_lengths.reshape(1, piers), variants
     )
-    second, third, fix_first, fix_third, payload = basis_call(
-        per, rows, field, mass, packed, got_a, got_b, first, second_raw, early, ends, count
+    *fixes, payload = edge_call(
+        per, rows, packed, got_a, got_b, inner, field, first, second, early, ends, count
     )
     gathered = lax.all_to_all(payload, AXES, 0, 0)
     return combine_call(
-        per, gathered, field, first, second, third, (fix_first, fix_third), ends,
+        per, gathered, field, first, second, third, (packed, *fixes), ends,
         stick_flags.reshape(1, bearings), normal_load.reshape(1, bearings), prior_friction,
     )
 

time: 32.3 us -> 31.2 us (0.966)
  blocking collectives: 17.6 us -> 16.8 us
    pallas_call x1, Pallas kernels: 4.41 us -> 1.93 us  [edge_call(): pl.pallas_call(functools.partial(edge_kernel, per), out_shape=(pltpu.VMEM...]
    pallas_call x1, Pallas kernels: 3.7 us -> 5.91 us  [cyclic_call(): pl.pallas_call(cyclic_kernel, out_shape=(pltpu.VMEM((3,) + padded, f32),...]
    all_to_all x1, blocking collectives: 17.6 us -> 16.8 us  [shards(): gathered = lax.all_to_all(payload, AXES, 0, 0)]
  transfers between devices with their start and end apart: 2 -> 2, of which waited for: 0 -> 0; matrix products, arithmetic and copies ran while one was open for 0% -> 0% of each run, Pallas kernels for 12% -> 19%
where the time goes in v5:
time: 31.2 us; the launch traced here: 31 us
  blocking collectives  16.8 us (54%)
  Pallas kernels  12.3 us (39%)
  starting transfers between devices  1.17 us (4%)
  between operations  0.72 us (2%)
    all_to_all x1, blocking collectives, shards(): gathered = lax.all_to_all(payload, AXES, 0, 0)  16.8 us
    pallas_call x1, Pallas kernels, cyclic_call(): pl.pallas_call(cyclic_kernel, out_shape=(pltpu.VMEM((3,) + padded, f32),...  5.91 us
    pallas_call x1, Pallas kernels, combine_call(): pl.pallas_call(functools.partial(combine_kernel, per), out_shape=(jax.Sha...  2.3 us
    pallas_call x1, Pallas kernels, pack_call(): pl.pallas_call(pack_kernel, out_shape=(pltpu.VMEM((3, depth + 2, across +...  2.2 us
    pallas_call x1, Pallas kernels, edge_call(): pl.pallas_call(functools.partial(edge_kernel, per), out_shape=(pltpu.VMEM...  1.93 us
    ppermute x1, starting transfers between devices, shards(): got_b = lax.ppermute(message_b, AXES, pairs_b)  0.66 us
  transfers between devices with their start and end apart: 2, of which 0 were waited for; matrix products, arithmetic and copies ran while one was open for 0% of the time, Pallas kernels for 19%

profile of v5, /device:TPU:0, one launch (start us, length us, event | category | flops | bytes accessed | tf_op | source)
XLA Modules:
  0.0 31.0 jit_solution(16358363820575688775)
XLA Ops:
  0.6 0.0 copy-start.1
  0.6 2.2 %pack.1 = (f32[3,18,80,128]{3,2,1,0:T(8,128)S(1)}, f32[16,64,128]{2,1,0:T(8,128)S(1)}, f32[4,16,8,128]{3,2,1,0:T(8,128)S(1)}, f32[4,8,8,128]{3,2,1,0:T(8,128)S(1)}, f32[4,8,8,128]{3,2,1,0:T(8,128)S(1)}) custom-call(f32[3,16,64,128]{3,2,1,0:T(8,128)} %right_hbm.1, f32[16,64,128]{2,1,0:T(8,128)} %mass_hbm.1), custom_call_target="tpu_custom_call" | custom-call | tf_op jit(solution)/shard_map/pack/pallas_call | solution.py:579
  2.8 0.5 %collective-permute-start = (f32[4,8,8,128]{3,2,1,0:T(8,128)S(1)}, f32[4,8,8,128]{3,2,1,0:T(8,128)S(1)}, u32[]{:S(2)}, u32[]{:S(2)}) collective-permute-start(f32[4,8,8,128]{3,2,1,0:T(8,128)S(1)} %get-tuple-element.19), channel_id=1, source_target_pairs={{0,1},{1,0},{2,3},{3,2},{4,5},{5,4},{6,7},{7,6},{8,9},{9,8},{10,11... | collective-permute-start | bytes 393224 | tf_op jit(solution)/shard_map/ppermute | solution.py:681
  3.4 0.7 %collective-permute-start.1 = (f32[4,8,8,128]{3,2,1,0:T(8,128)S(1)}, f32[4,8,8,128]{3,2,1,0:T(8,128)S(1)}, u32[]{:S(2)}, u32[]{:S(2)}) collective-permute-start(f32[4,8,8,128]{3,2,1,0:T(8,128)S(1)} %get-tuple-element.20), channel_id=1, source_target_pairs={{1,2},{2,1},{3,4},{4,3},{5,6},{6,5},{7,8},{8,7},{9,10},{10,9},{11,... | collective-permute-start | bytes 393224 | tf_op jit(solution)/shard_map/ppermute | solution.py:682
  4.0 0.0 copy-done.1
  4.0 5.9 %cyclic.1 = (f32[3,18,80,128]{3,2,1,0:T(8,128)S(1)}, f32[3,18,80,128]{3,2,1,0:T(8,128)S(1)}, f32[3,16,64,128]{3,2,1,0:T(8,128)S(1)}, f32[3,16,8,128]{3,2,1,0:T(8...) custom-call(f32[3,18,80,128]{3,2,1,0:T(8,128)S(1)} %get-tuple-element.21.field, ...), custom_call_target="tpu_custom_call" | custom-call | flops 60000000 | bytes 12000000 | tf_op jit(solution)/shard_map/cyclic/pallas_call | solution.py:603
  10.0 0.0 collective-permute-done.got_a
  10.0 0.0 collective-permute-done.1.got_b
  10.0 0.0 copy-start
  10.0 0.0 copy-start.2
  10.0 0.0 copy-start.3
  10.0 1.9 %edge.1 = (f32[3,16,8,128]{3,2,1,0:T(8,128)S(1)}, f32[3,16,8,128]{3,2,1,0:T(8,128)S(1)}, f32[3,16,8,128]{3,2,1,0:T(8,128)S(1)}, f32[32,8,128]{2,1,0:T(8,128)S(1)}) custom-call(f32[4,16,8,128]{3,2,1,0:T(8,128)S(1)} %get-tuple-element.18.packed, f32[4,8,8,128]{3,2,1,0:T(8,128)S(1)} %collective-permute-done.got_a, ...), custom_call_target="tpu_custom_call" | custom-call | tf_op jit(solution)/shard_map/edge/pallas_call | solution.py:627
  11.9 16.8 %all_to_all.5.gathered = f32[32,8,128]{2,1,0:T(8,128)S(1)} all-to-all(f32[32,8,128]{2,1,0:T(8,128)S(1)} %get-tuple-element.28), channel_id=1, replica_groups=mesh['len'=8,'xs'=4] {'len','xs'}, dimensions={0} | all-to-all | bytes 262144 | tf_op jit(solution)/shard_map/all_to_all | solution.py:689
  28.7 0.0 copy-done
  28.7 0.0 copy-done.2
  28.7 0.0 copy-done.3
  28.7 2.3 %combine.1 = (f32[3,16,64,128]{3,2,1,0:T(8,128)}, f32[3,16,64,128]{3,2,1,0:T(8,128)}, f32[2,64]{1,0:T(2,128)}) custom-call(f32[32,8,128]{2,1,0:T(8,128)S(1)} %all_to_all.5.gathered, f32[3,18,80,128]{3,2,1,0:T(8,128)S(1)} %get-tuple-element.21.field, f32[3,18,80,128]{3,2,1,0:T(8,128)S(1)} %get-tuple-element.24.first, ...), custom_call_target="tpu_custom_call" | custom-call | tf_op jit(solution)/shard_map/combine/pallas_call | solution.py:648
Async XLA Ops:
  0.6 3.4 %copy-start.1 = (s32[32]{0:T(128)S(1)}, s32[32]{0:T(128)}, u32[]{:S(2)}) copy-start(s32[32]{0:T(128)} %param.8) | copy-start | bytes 388
  2.8 7.1 %collective-permute-start = (f32[4,8,8,128]{3,2,1,0:T(8,128)S(1)}, f32[4,8,8,128]{3,2,1,0:T(8,128)S(1)}, u32[]{:S(2)}, u32[]{:S(2)}) collective-permute-start(f32[4,8,8,128]{3,2,1,0:T(8,128)S(1)} %get-tuple-element.19), channel_id=1, source_target_pairs={{0,1},{1,0},{2,3},{3,2},{4,5},{5,4},{6,7},{7,6},{8,9},{9,8},{10,11... | collective-permute-start | bytes 393224 | tf_op jit(solution)/shard_map/ppermute | solution.py:681
  3.4 6.6 %collective-permute-start.1 = (f32[4,8,8,128]{3,2,1,0:T(8,128)S(1)}, f32[4,8,8,128]{3,2,1,0:T(8,128)S(1)}, u32[]{:S(2)}, u32[]{:S(2)}) collective-permute-start(f32[4,8,8,128]{3,2,1,0:T(8,128)S(1)} %get-tuple-element.20), channel_id=1, source_target_pairs={{1,2},{2,1},{3,4},{4,3},{5,6},{6,5},{7,8},{8,7},{9,10},{10,9},{11,... | collective-permute-start | bytes 393224 | tf_op jit(solution)/shard_map/ppermute | solution.py:682
  10.0 18.7 %copy-start = (f32[2,64]{1,0:T(2,128)S(1)}, f32[2,64]{1,0:T(2,128)}, u32[]{:S(2)}) copy-start(f32[2,64]{1,0:T(2,128)} %prior.1) | copy-start | bytes 1540
  10.0 18.7 %copy-start.2 = (s32[64]{0:T(128)S(1)}, s32[64]{0:T(128)}, u32[]{:S(2)}) copy-start(s32[64]{0:T(128)} %param.9) | copy-start | bytes 772
  10.0 18.7 %copy-start.3 = (f32[64]{0:T(128)S(1)}, f32[64]{0:T(128)}, u32[]{:S(2)}) copy-start(f32[64]{0:T(128)} %param.10) | copy-start | bytes 772

commit v6 on v5

--- a/solution.py
+++ b/solution.py
@@ -8,7 +8,7 @@
 from jax.sharding import PartitionSpec as P
 
 ITERS = 3
-SHIFT = 4.0
+SHIFT = 6.5
 BULK = 1.5
 ELASTIC = 8.0
 RADIUS = 4.0
@@ -27,6 +27,8 @@
 CHUNK = 16
 PIECE = 16
 MARGINS = (6, 5, 5)
+MOMENTS = 2 * ITERS
+SPREAD = 8
 HIGH = lax.Precision.HIGHEST
 LIMIT = pltpu.CompilerParams(vmem_limit_bytes=32 * 1024 * 1024)
 
@@ -231,7 +233,7 @@
 def edge_kernel(
     per, packed, got_a, got_b, inner, field, first, second, early, ends,
     fix_first, fix_second, fix_third, payload,
-    edge, edge_div, edge_diag, sums, picked,
+    edges, edge_div, edge_diag, sums, picked,
 ):
     depth, across = packed.shape[1], first.shape[2] - 2 * PAD
     index = device_index()
@@ -271,15 +273,16 @@
                 ),
             ):
                 if c < 3:
-                    edge[0, c, pl.ds(row_of(at), ROWS), :] = left
-                    edge[1, c, pl.ds(row_of(at), ROWS), :] = right
+                    edges[0, 0, c, pl.ds(row_of(at), ROWS), :] = left
+                    edges[0, 1, c, pl.ds(row_of(at), ROWS), :] = right
                 else:
                     edge_diag[0, at] = left
                     edge_diag[1, at] = right
     for s in both:
         for c in comps:
-            edge[s, c, pl.ds(ROWS, ROWS), :] = blank
-            edge[s, c, pl.ds(row_of(depth), ROWS), :] = blank
+            for buffer in both:
+                edges[buffer, s, c, pl.ds(ROWS, ROWS), :] = blank
+                edges[buffer, s, c, pl.ds(row_of(depth), ROWS), :] = blank
         edge_div[s, pl.ds(ROWS, ROWS), :] = blank
         edge_div[s, pl.ds(row_of(depth), ROWS), :] = blank
 
@@ -296,9 +299,6 @@
                 spot < LANES - EDGE, turn(ahead, -EDGE), 0.0
             )
 
-    def at(s, c, d, by=0):
-        return edge[s, c, pl.ds(row_of(d) + by, ROWS), :]
-
     def div_at(s, d, by=0):
         return edge_div[s, pl.ds(row_of(d) + by, ROWS), :]
 
@@ -314,6 +314,11 @@
         return jnp.where(first_planes if s else last_planes, own, value)
 
     def edge_step(level):
+        edge, target = edges.at[level % 2], edges.at[(level + 1) % 2]
+
+        def at(s, c, d, by=0):
+            return edge[s, c, pl.ds(row_of(d) + by, ROWS), :]
+
         for s in both:
             for c in comps:
                 join_blocks(edge, (s, c))
@@ -329,7 +334,6 @@
         norms, crosses = [], []
         for c in comps:
             norm, cross = blank, blank
-            images = []
             for d in range(depth):
                 pair = []
                 for s in both:
@@ -345,21 +349,19 @@
                         total = total + (div_at(s, d + 1) - div_at(s, d - 1))
                     total = total + (at(s, c, d - 1) + at(s, c, d + 1))
                     total = total + (at(s, c, d, 1) + at(s, c, d, -1))
-                    pair.append((edge_diag[s, d] * x - total) * keep[s])
-                images.append(pair)
+                    image = (edge_diag[s, d] * x - total) * keep[s]
+                    pair.append(image)
+                    if level + 1 < ITERS:
+                        image = image if c else joined(s, image, inner[level, d])
+                        target[s, c, pl.ds(row_of(d), ROWS), :] = image
                 old = fixes[level][c, d]
                 new = jnp.where(first_half, pair[1], pair[0])
                 fixes[level + 1][c, d] = new
-                norm = norm + old * old
+                if level:
+                    norm = norm + old * old
                 cross = cross + old * new
             norms.append(norm)
             crosses.append(cross)
-            if level + 1 == ITERS:
-                continue
-            for d in range(depth):
-                for s in both:
-                    value = images[d][s] if c else joined(s, images[d][s], inner[level, d])
-                    edge[s, c, pl.ds(row_of(d), ROWS), :] = value
         return norms, crosses
 
     edge_sums = [edge_step(level) for level in range(ITERS)]
@@ -409,19 +411,91 @@
 
     sums[...] = jnp.zeros(sums.shape, jnp.float32)
     sums[0:bearing_rows, :] = total[0:bearing_rows]
-    low = lane_iota((1, LANES)) < LANES // 2
-    for pair in range(3):
-        halves = []
-        for part in parts[2 * pair : 2 * pair + 2]:
-            flat = jnp.sum(part, axis=0, keepdims=True)
-            halves.append(flat + turn(flat, LANES // 2))
-        sums[bearing_rows + pair : bearing_rows + pair + 1, :] = jnp.where(low, *halves)
-    out = sums[...]
+    flat = jnp.concatenate(
+        [jnp.sum(part, axis=0, keepdims=True) for part in parts]
+        + [jnp.zeros((ROWS - MOMENTS, LANES), jnp.float32)],
+        axis=0,
+    )
+    amount = LANES // 2
+    while amount >= SPREAD:
+        flat = flat + turn(flat, amount)
+        amount //= 2
+    row, first_lane = divmod(blocks * (LANES // per), LANES)
+    number = lax.broadcasted_iota(jnp.int32, (ROWS, LANES), 0)
+    held = lane // SPREAD == number + first_lane // SPREAD
+    flat = jnp.sum(jnp.where(held & (number < MOMENTS), flat, 0.0), axis=0, keepdims=True)
+    sums[row : row + 1, :] = sums[row : row + 1, :] + flat
+    out = jnp.concatenate(
+        [sums[row : row + 1, :] for row in range(payload.shape[2] // LANES)], axis=1
+    )
     for device in range(payload.shape[0]):
         payload[device] = out
 
 
-def coefficients(moment):
+def added(parts):
+    while len(parts) > 1:
+        parts = [sum(parts[i + 1 : i + 2], parts[i]) for i in range(0, len(parts), 2)]
+    return parts[0]
+
+
+def two_sum(a, b):
+    total = a + b
+    part = total - a
+    return total, (a - (total - part)) + (b - part)
+
+
+def high_half(x):
+    scaled = 4097.0 * x
+    return scaled - (scaled - x)
+
+
+def less_multiple(a, theta, b):
+    upper = high_half(b[0])
+    high, error = two_sum(a[0], -theta * upper)
+    high, more = two_sum(high, -theta * (b[0] - upper))
+    low = (error + more) + (a[1] - theta * b[1])
+    total = high + low
+    return total, low - (total - high)
+
+
+def exact_sums(sent, first_lane):
+    number = lane_iota(sent[0].shape) // SPREAD - first_lane // SPREAD
+
+    def sums(row):
+        return [
+            jnp.sum(jnp.where(number == n, row, 0.0), axis=1, keepdims=True)
+            for n in range(MOMENTS)
+        ]
+
+    bound = jnp.zeros_like(sent[0])
+    for n, total in enumerate(sums(added([jnp.abs(x) for x in sent]))):
+        bound = jnp.where(number == n, 2.0 * total, bound)
+    upper = [(x + bound) - bound for x in sent]
+    lower = [x - u for x, u in zip(sent, upper)]
+    return list(zip(sums(added(upper)), sums(added(lower))))
+
+
+def centred(moments):
+    theta = high_half(moments[1][0] / moments[0][0])
+    moments = list(moments)
+    for first in range(1, MOMENTS):
+        for n in range(MOMENTS - 1, first - 1, -1):
+            moments[n] = less_multiple(moments[n], theta, moments[n - 1])
+    return theta, [high + low for high, low in moments]
+
+
+def expanded(terms, theta):
+    out = [terms[-1]]
+    for term in terms[-2::-1]:
+        out = (
+            [term - theta * out[0]]
+            + [out[i] - theta * out[i + 1] for i in range(len(out) - 1)]
+            + [out[-1]]
+        )
+    return out
+
+
+def coefficients(moment, shift):
     def dot(a, b):
         total = None
         for i, left in enumerate(a):
@@ -434,7 +508,7 @@
     solved, direction, increment = [one], [one], []
     norm = moment[0]
     for iteration in range(ITERS):
-        image = [SHIFT * p for p in direction] + [jnp.zeros_like(one)]
+        image = [shift * p for p in direction] + [jnp.zeros_like(one)]
         for i, p in enumerate(direction):
             image[i + 1] = image[i + 1] + p
         alpha = norm / dot(direction, image)
@@ -467,18 +541,15 @@
     variants = ends.shape[0]
     pieces = 1 if per > 1 else variants
     width = min(bearings, LANES)
-    bearing_rows = -(-9 * pieces // per)
-    parts = [gathered[i] for i in range(gathered.shape[0])]
-    while len(parts) > 1:
-        parts = [sum(parts[i : i + 2]) for i in range(0, len(parts), 2)]
-    total = parts[0]
-    low = lane_iota((1, LANES)) < LANES // 2
-    moments = []
-    for n in range(6):
-        row = total[bearing_rows + n // 2 : bearing_rows + n // 2 + 1]
-        row = jnp.where(low == (n % 2 == 0), row, 0.0)
-        moments.append(jnp.sum(row, axis=1, keepdims=True))
-    grow, keep = coefficients(moments)
+    blocks = 3 * ITERS * pieces
+    row, first_lane = divmod(blocks * (LANES // per), LANES)
+    received = [gathered[device] for device in range(gathered.shape[0])]
+    sent = [x[:, row * LANES : (row + 1) * LANES] for x in received]
+    theta, moments = centred(exact_sums(sent, first_lane))
+    grow, keep = (
+        expanded(terms, theta) for terms in coefficients(moments, SHIFT + theta)
+    )
+    total = added(received)
 
     forces[...] = jnp.zeros(forces.shape, jnp.float32)
     lane = lane_iota((1, width))
@@ -489,7 +560,7 @@
             value = None
             for k in range(ITERS):
                 block = (3 * k + c) * pieces + piece
-                row = total[block // per : block // per + 1]
+                row = total[:, block // per * LANES : (block // per + 1) * LANES]
                 if per > 1 and block % per:
                     row = turn(row, LANES - (block % per) * bearings)
                 term = grow[k] * row[:, :width]
@@ -624,17 +695,18 @@
     depth = packed.shape[1]
     variants = ends.shape[0]
     edges = (3, depth, ROWS, LANES)
+    tall = -(-rows // ROWS) * ROWS
     return pl.pallas_call(
         functools.partial(edge_kernel, per),
-        out_shape=(pltpu.VMEM(edges, f32),) * 3 + (pltpu.VMEM((count, rows, LANES), f32),),
+        out_shape=(pltpu.VMEM(edges, f32),) * 3 + (pltpu.VMEM((count, 1, rows * LANES), f32),),
         in_specs=[vmem_spec()] * 9,
         out_specs=(vmem_spec(),) * 4,
         scratch_shapes=[
-            pltpu.VMEM((2, 3, (depth + 2) * PITCH, LANES), f32),
+            pltpu.VMEM((2, 2, 3, (depth + 2) * PITCH, LANES), f32),
             pltpu.VMEM((2, (depth + 2) * PITCH, LANES), f32),
             pltpu.VMEM((2, depth, ROWS, LANES), f32),
-            pltpu.VMEM((rows, LANES), f32),
-            pltpu.VMEM((rows, 2 * variants * LANES), f32),
+            pltpu.VMEM((tall, LANES), f32),
+            pltpu.VMEM((tall, 2 * variants * LANES), f32),
         ],
         compiler_params=LIMIT,
         name="edge",
@@ -673,7 +745,8 @@
     per = LANES // bearings if bearings <= LANES else 1
     variants = per if bearings <= LANES else bearings // LANES
     pieces = 1 if per > 1 else variants
-    rows = -(-(-(-3 * ITERS * pieces // per) + 3) // ROWS) * ROWS
+    sent = 3 * ITERS * pieces * (LANES // per) + MOMENTS * SPREAD
+    rows = -(-sent // LANES)
 
     field, mass, packed, message_a, message_b = pack_call(right_side, mass_field)
     pairs_a = [p for i in range(0, count - 1, 2) for p in ((i, i + 1), (i + 1, i))]
@@ -686,7 +759,7 @@
     *fixes, payload = edge_call(
         per, rows, packed, got_a, got_b, inner, field, first, second, early, ends, count
     )
-    gathered = lax.all_to_all(payload, AXES, 0, 0)
+    gathered = lax.all_to_all(payload, AXES, 0, 0, tiled=True)
     return combine_call(
         per, gathered, field, first, second, third, (packed, *fixes), ends,
         stick_flags.reshape(1, bearings), normal_load.reshape(1, bearings), prior_friction,

time: 31.2 us -> 30.8 us (0.987)
  blocking collectives: 16.8 us -> 16.1 us
    all_to_all x1, blocking collectives: 16.8 us -> 16.1 us  [shards(): gathered = lax.all_to_all(payload, AXES, 0, 0, tiled=True)]
where the time goes in v6:
time: 30.8 us; the launch traced here: 30.6 us
  blocking collectives  16.1 us (52%)
  Pallas kernels  12.5 us (41%)
  starting transfers between devices  1.17 us (4%)
  between operations  0.72 us (2%)
    all_to_all x1, blocking collectives, shards(): gathered = lax.all_to_all(payload, AXES, 0, 0, tiled=True)  16.1 us
    pallas_call x1, Pallas kernels, cyclic_call(): pl.pallas_call(cyclic_kernel, out_shape=(pltpu.VMEM((3,) + padded, f32),...  5.91 us
    pallas_call x1, Pallas kernels, combine_call(): pl.pallas_call(functools.partial(combine_kernel, per), out_shape=(jax.Sha...  2.4 us
    pallas_call x1, Pallas kernels, pack_call(): pl.pallas_call(pack_kernel, out_shape=(pltpu.VMEM((3, depth + 2, across +...  2.2 us
    pallas_call x1, Pallas kernels, edge_call(): pl.pallas_call(functools.partial(edge_kernel, per), out_shape=(pltpu.VMEM...  2.03 us
    ppermute x1, starting transfers between devices, shards(): got_b = lax.ppermute(message_b, AXES, pairs_b)  0.66 us
  transfers between devices with their start and end apart: 2, of which 0 were waited for; matrix products, arithmetic and copies ran while one was open for 0% of the time, Pallas kernels for 19%

profile of v6, /device:TPU:0, one launch (start us, length us, event | category | flops | bytes accessed | tf_op | source)
XLA Modules:
  0.0 30.6 jit_solution(18173049158887846604)
XLA Ops:
  0.6 0.0 copy-start.1
  0.6 2.2 %pack.1 = (f32[3,18,80,128]{3,2,1,0:T(8,128)S(1)}, f32[16,64,128]{2,1,0:T(8,128)S(1)}, f32[4,16,8,128]{3,2,1,0:T(8,128)S(1)}, f32[4,8,8,128]{3,2,1,0:T(8,128)S(1)}, f32[4,8,8,128]{3,2,1,0:T(8,128)S(1)}) custom-call(f32[3,16,64,128]{3,2,1,0:T(8,128)} %right_hbm.1, f32[16,64,128]{2,1,0:T(8,128)} %mass_hbm.1), custom_call_target="tpu_custom_call" | custom-call | tf_op jit(solution)/shard_map/pack/pallas_call | solution.py:650
  2.8 0.5 %collective-permute-start = (f32[4,8,8,128]{3,2,1,0:T(8,128)S(1)}, f32[4,8,8,128]{3,2,1,0:T(8,128)S(1)}, u32[]{:S(2)}, u32[]{:S(2)}) collective-permute-start(f32[4,8,8,128]{3,2,1,0:T(8,128)S(1)} %get-tuple-element.19), channel_id=1, source_target_pairs={{0,1},{1,0},{2,3},{3,2},{4,5},{5,4},{6,7},{7,6},{8,9},{9,8},{10,11... | collective-permute-start | bytes 393224 | tf_op jit(solution)/shard_map/ppermute | solution.py:754
  3.4 0.7 %collective-permute-start.1 = (f32[4,8,8,128]{3,2,1,0:T(8,128)S(1)}, f32[4,8,8,128]{3,2,1,0:T(8,128)S(1)}, u32[]{:S(2)}, u32[]{:S(2)}) collective-permute-start(f32[4,8,8,128]{3,2,1,0:T(8,128)S(1)} %get-tuple-element.20), channel_id=1, source_target_pairs={{1,2},{2,1},{3,4},{4,3},{5,6},{6,5},{7,8},{8,7},{9,10},{10,9},{11,... | collective-permute-start | bytes 393224 | tf_op jit(solution)/shard_map/ppermute | solution.py:755
  4.0 0.0 copy-done.1
  4.0 5.9 %cyclic.1 = (f32[3,18,80,128]{3,2,1,0:T(8,128)S(1)}, f32[3,18,80,128]{3,2,1,0:T(8,128)S(1)}, f32[3,16,64,128]{3,2,1,0:T(8,128)S(1)}, f32[3,16,8,128]{3,2,1,0:T(8...) custom-call(f32[3,18,80,128]{3,2,1,0:T(8,128)S(1)} %get-tuple-element.21.field, ...), custom_call_target="tpu_custom_call" | custom-call | flops 60000000 | bytes 12000000 | tf_op jit(solution)/shard_map/cyclic/pallas_call | solution.py:674
  10.0 0.0 collective-permute-done.got_a
  10.0 0.0 collective-permute-done.1.got_b
  10.0 0.0 copy-start
  10.0 0.0 copy-start.2
  10.0 0.0 copy-start.3
  10.0 2.0 %edge.1 = (f32[3,16,8,128]{3,2,1,0:T(8,128)S(1)}, f32[3,16,8,128]{3,2,1,0:T(8,128)S(1)}, f32[3,16,8,128]{3,2,1,0:T(8,128)S(1)}, f32[32,1,640]{2,1,0:T(1,128)S(1)}) custom-call(f32[4,16,8,128]{3,2,1,0:T(8,128)S(1)} %get-tuple-element.18.packed, f32[4,8,8,128]{3,2,1,0:T(8,128)S(1)} %collective-permute-done.got_a, ...), custom_call_target="tpu_custom_call" | custom-call | tf_op jit(solution)/shard_map/edge/pallas_call | solution.py:699
  12.1 16.1 %all_to_all.5.gathered = f32[32,1,640]{2,1,0:T(1,128)S(1)} all-to-all(f32[32,1,640]{2,1,0:T(1,128)S(1)} %get-tuple-element.28), channel_id=1, replica_groups=mesh['len'=8,'xs'=4] {'len','xs'}, dimensions={0} | all-to-all | bytes 163840 | tf_op jit(solution)/shard_map/all_to_all | solution.py:762
  28.2 0.0 copy-done
  28.2 0.0 copy-done.2
  28.2 0.0 copy-done.3
  28.2 2.4 %combine.1 = (f32[3,16,64,128]{3,2,1,0:T(8,128)}, f32[3,16,64,128]{3,2,1,0:T(8,128)}, f32[2,64]{1,0:T(2,128)}) custom-call(f32[32,1,640]{2,1,0:T(1,128)S(1)} %all_to_all.5.gathered, f32[3,18,80,128]{3,2,1,0:T(8,128)S(1)} %get-tuple-element.21.field, f32[3,18,80,128]{3,2,1,0:T(8,128)S(1)} %get-tuple-element.24.first, ...), custom_call_target="tpu_custom_call" | custom-call | tf_op jit(solution)/shard_map/combine/pallas_call | solution.py:720
Async XLA Ops:
  0.6 3.4 %copy-start.1 = (s32[32]{0:T(128)S(1)}, s32[32]{0:T(128)}, u32[]{:S(2)}) copy-start(s32[32]{0:T(128)} %param.8) | copy-start | bytes 388
  2.8 7.1 %collective-permute-start = (f32[4,8,8,128]{3,2,1,0:T(8,128)S(1)}, f32[4,8,8,128]{3,2,1,0:T(8,128)S(1)}, u32[]{:S(2)}, u32[]{:S(2)}) collective-permute-start(f32[4,8,8,128]{3,2,1,0:T(8,128)S(1)} %get-tuple-element.19), channel_id=1, source_target_pairs={{0,1},{1,0},{2,3},{3,2},{4,5},{5,4},{6,7},{7,6},{8,9},{9,8},{10,11... | collective-permute-start | bytes 393224 | tf_op jit(solution)/shard_map/ppermute | solution.py:754
  3.4 6.6 %collective-permute-start.1 = (f32[4,8,8,128]{3,2,1,0:T(8,128)S(1)}, f32[4,8,8,128]{3,2,1,0:T(8,128)S(1)}, u32[]{:S(2)}, u32[]{:S(2)}) collective-permute-start(f32[4,8,8,128]{3,2,1,0:T(8,128)S(1)} %get-tuple-element.20), channel_id=1, source_target_pairs={{1,2},{2,1},{3,4},{4,3},{5,6},{6,5},{7,8},{8,7},{9,10},{10,9},{11,... | collective-permute-start | bytes 393224 | tf_op jit(solution)/shard_map/ppermute | solution.py:755
  10.0 18.2 %copy-start = (f32[2,64]{1,0:T(2,128)S(1)}, f32[2,64]{1,0:T(2,128)}, u32[]{:S(2)}) copy-start(f32[2,64]{1,0:T(2,128)} %prior.1) | copy-start | bytes 1540
  10.0 18.2 %copy-start.2 = (s32[64]{0:T(128)S(1)}, s32[64]{0:T(128)}, u32[]{:S(2)}) copy-start(s32[64]{0:T(128)} %param.9) | copy-start | bytes 772
  10.0 18.2 %copy-start.3 = (f32[64]{0:T(128)S(1)}, f32[64]{0:T(128)}, u32[]{:S(2)}) copy-start(f32[64]{0:T(128)} %param.10) | copy-start | bytes 772

commit v7 on v6

--- a/solution.py
+++ b/solution.py
@@ -231,7 +231,7 @@
 
 
 def edge_kernel(
-    per, packed, got_a, got_b, inner, field, first, second, early, ends,
+    per, packed, got_b, got_a, inner, field, first, second, early, ends,
     fix_first, fix_second, fix_third, payload,
     edges, edge_div, edge_diag, sums, picked,
 ):
@@ -710,7 +710,7 @@
         ],
         compiler_params=LIMIT,
         name="edge",
-    )(packed, got_a, got_b, inner, field, first, second, early, ends)
+    )(packed, got_b, got_a, inner, field, first, second, early, ends)
 
 
 def combine_call(per, gathered, field, first, second, third, edges, ends, stick, load, prior):

time: 30.8 us -> 30.8 us (level)
  starting transfers between devices: 1.17 us -> 5.06 us
  blocking collectives: 16.1 us -> 12.3 us
    ppermute x1, starting transfers between devices: 0.52 us -> 4.39 us  [shards(): got_a = lax.ppermute(message_a, AXES, pairs_a)]
    all_to_all x1, blocking collectives: 16.1 us -> 12.3 us  [shards(): gathered = lax.all_to_all(payload, AXES, 0, 0, tiled=True)]
where the time goes in v7:
time: 30.8 us; the launch traced here: 30.6 us
  Pallas kernels  12.5 us (41%)
  blocking collectives  12.3 us (40%)
  starting transfers between devices  5.06 us (16%)
  between operations  0.71 us (2%)
    all_to_all x1, blocking collectives, shards(): gathered = lax.all_to_all(payload, AXES, 0, 0, tiled=True)  12.3 us
    pallas_call x1, Pallas kernels, cyclic_call(): pl.pallas_call(cyclic_kernel, out_shape=(pltpu.VMEM((3,) + padded, f32),...  5.9 us
    ppermute x1, starting transfers between devices, shards(): got_a = lax.ppermute(message_a, AXES, pairs_a)  4.39 us
    pallas_call x1, Pallas kernels, combine_call(): pl.pallas_call(functools.partial(combine_kernel, per), out_shape=(jax.Sha...  2.4 us
    pallas_call x1, Pallas kernels, pack_call(): pl.pallas_call(pack_kernel, out_shape=(pltpu.VMEM((3, depth + 2, across +...  2.2 us
    pallas_call x1, Pallas kernels, edge_call(): pl.pallas_call(functools.partial(edge_kernel, per), out_shape=(pltpu.VMEM...  2.03 us
    ppermute x1, starting transfers between devices, shards(): got_b = lax.ppermute(message_b, AXES, pairs_b)  0.67 us
  transfers between devices with their start and end apart: 2, of which 0 were waited for; matrix products, arithmetic and copies ran while one was open for 0% of the time, Pallas kernels for 19%

profile of v7, /device:TPU:0, one launch (start us, length us, event | category | flops | bytes accessed | tf_op | source)
XLA Modules:
  0.0 30.6 jit_solution(498258575996466851)
XLA Ops:
  0.6 0.0 copy-start.1
  0.6 2.2 %pack.1 = (f32[3,18,80,128]{3,2,1,0:T(8,128)S(1)}, f32[16,64,128]{2,1,0:T(8,128)S(1)}, f32[4,16,8,128]{3,2,1,0:T(8,128)S(1)}, f32[4,8,8,128]{3,2,1,0:T(8,128)S(1)}, f32[4,8,8,128]{3,2,1,0:T(8,128)S(1)}) custom-call(f32[3,16,64,128]{3,2,1,0:T(8,128)} %right_hbm.1, f32[16,64,128]{2,1,0:T(8,128)} %mass_hbm.1), custom_call_target="tpu_custom_call" | custom-call | tf_op jit(solution)/shard_map/pack/pallas_call | solution.py:650
  2.8 0.7 %collective-permute-start = (f32[4,8,8,128]{3,2,1,0:T(8,128)S(1)}, f32[4,8,8,128]{3,2,1,0:T(8,128)S(1)}, u32[]{:S(2)}, u32[]{:S(2)}) collective-permute-start(f32[4,8,8,128]{3,2,1,0:T(8,128)S(1)} %get-tuple-element.19), channel_id=1, source_target_pairs={{1,2},{2,1},{3,4},{4,3},{5,6},{6,5},{7,8},{8,7},{9,10},{10,9},{11,... | collective-permute-start | bytes 393224 | tf_op jit(solution)/shard_map/ppermute | solution.py:755
  3.5 4.4 %collective-permute-start.1 = (f32[4,8,8,128]{3,2,1,0:T(8,128)S(1)}, f32[4,8,8,128]{3,2,1,0:T(8,128)S(1)}, u32[]{:S(2)}, u32[]{:S(2)}) collective-permute-start(f32[4,8,8,128]{3,2,1,0:T(8,128)S(1)} %get-tuple-element.20), channel_id=1, source_target_pairs={{0,1},{1,0},{2,3},{3,2},{4,5},{5,4},{6,7},{7,6},{8,9},{9,8},{10,11... | collective-permute-start | bytes 393224 | tf_op jit(solution)/shard_map/ppermute | solution.py:754
  7.9 0.0 copy-done.1
  7.9 5.9 %cyclic.1 = (f32[3,18,80,128]{3,2,1,0:T(8,128)S(1)}, f32[3,18,80,128]{3,2,1,0:T(8,128)S(1)}, f32[3,16,64,128]{3,2,1,0:T(8,128)S(1)}, f32[3,16,8,128]{3,2,1,0:T(8...) custom-call(f32[3,18,80,128]{3,2,1,0:T(8,128)S(1)} %get-tuple-element.21.field, ...), custom_call_target="tpu_custom_call" | custom-call | flops 60000000 | bytes 12000000 | tf_op jit(solution)/shard_map/cyclic/pallas_call | solution.py:674
  13.8 0.0 collective-permute-done.got_b
  13.8 0.0 collective-permute-done.1.got_a
  13.8 0.0 copy-start
  13.9 0.0 copy-start.2
  13.9 0.0 copy-start.3
  13.9 2.0 %edge.1 = (f32[3,16,8,128]{3,2,1,0:T(8,128)S(1)}, f32[3,16,8,128]{3,2,1,0:T(8,128)S(1)}, f32[3,16,8,128]{3,2,1,0:T(8,128)S(1)}, f32[32,1,640]{2,1,0:T(1,128)S(1)}) custom-call(f32[4,16,8,128]{3,2,1,0:T(8,128)S(1)} %get-tuple-element.18.packed, f32[4,8,8,128]{3,2,1,0:T(8,128)S(1)} %collective-permute-done.got_b, ...), custom_call_target="tpu_custom_call" | custom-call | tf_op jit(solution)/shard_map/edge/pallas_call | solution.py:699
  15.9 12.3 %all_to_all.5.gathered = f32[32,1,640]{2,1,0:T(1,128)S(1)} all-to-all(f32[32,1,640]{2,1,0:T(1,128)S(1)} %get-tuple-element.28), channel_id=1, replica_groups=mesh['len'=8,'xs'=4] {'len','xs'}, dimensions={0} | all-to-all | bytes 163840 | tf_op jit(solution)/shard_map/all_to_all | solution.py:762
  28.2 0.0 copy-done
  28.2 0.0 copy-done.2
  28.2 0.0 copy-done.3
  28.2 2.4 %combine.1 = (f32[3,16,64,128]{3,2,1,0:T(8,128)}, f32[3,16,64,128]{3,2,1,0:T(8,128)}, f32[2,64]{1,0:T(2,128)}) custom-call(f32[32,1,640]{2,1,0:T(1,128)S(1)} %all_to_all.5.gathered, f32[3,18,80,128]{3,2,1,0:T(8,128)S(1)} %get-tuple-element.21.field, f32[3,18,80,128]{3,2,1,0:T(8,128)S(1)} %get-tuple-element.24.first, ...), custom_call_target="tpu_custom_call" | custom-call | tf_op jit(solution)/shard_map/combine/pallas_call | solution.py:720
Async XLA Ops:
  0.6 7.3 %copy-start.1 = (s32[32]{0:T(128)S(1)}, s32[32]{0:T(128)}, u32[]{:S(2)}) copy-start(s32[32]{0:T(128)} %param.8) | copy-start | bytes 388
  2.8 11.0 %collective-permute-start = (f32[4,8,8,128]{3,2,1,0:T(8,128)S(1)}, f32[4,8,8,128]{3,2,1,0:T(8,128)S(1)}, u32[]{:S(2)}, u32[]{:S(2)}) collective-permute-start(f32[4,8,8,128]{3,2,1,0:T(8,128)S(1)} %get-tuple-element.19), channel_id=1, source_target_pairs={{1,2},{2,1},{3,4},{4,3},{5,6},{6,5},{7,8},{8,7},{9,10},{10,9},{11,... | collective-permute-start | bytes 393224 | tf_op jit(solution)/shard_map/ppermute | solution.py:755
  3.5 10.3 %collective-permute-start.1 = (f32[4,8,8,128]{3,2,1,0:T(8,128)S(1)}, f32[4,8,8,128]{3,2,1,0:T(8,128)S(1)}, u32[]{:S(2)}, u32[]{:S(2)}) collective-permute-start(f32[4,8,8,128]{3,2,1,0:T(8,128)S(1)} %get-tuple-element.20), channel_id=1, source_target_pairs={{0,1},{1,0},{2,3},{3,2},{4,5},{5,4},{6,7},{7,6},{8,9},{9,8},{10,11... | collective-permute-start | bytes 393224 | tf_op jit(solution)/shard_map/ppermute | solution.py:754
  13.8 14.4 %copy-start = (f32[2,64]{1,0:T(2,128)S(1)}, f32[2,64]{1,0:T(2,128)}, u32[]{:S(2)}) copy-start(f32[2,64]{1,0:T(2,128)} %prior.1) | copy-start | bytes 1540
  13.9 14.4 %copy-start.2 = (s32[64]{0:T(128)S(1)}, s32[64]{0:T(128)}, u32[]{:S(2)}) copy-start(s32[64]{0:T(128)} %param.9) | copy-start | bytes 772
  13.9 14.4 %copy-start.3 = (f32[64]{0:T(128)S(1)}, f32[64]{0:T(128)}, u32[]{:S(2)}) copy-start(f32[64]{0:T(128)} %param.10) | copy-start | bytes 772

commit v8 on v7

--- a/solution.py
+++ b/solution.py
@@ -108,39 +108,33 @@
     return sum(x[i : i + ROWS] for i in range(0, x.shape[0], ROWS))
 
 
-def cyclic_step(source, mass, div, store, step, inner_source=None, inner_div=None):
+def cyclic_step(source, mass, div, store, inner_source=None, inner_div=None):
     depth, across = mass.shape[0], mass.shape[1]
     chunks = range(0, across, CHUNK)
     block_of = lane_iota((ROWS, LANES)) // EDGE
 
     def pack(edge, r, tile):
-        for i in range(0, CHUNK, ROWS):
+        for i in range(0, tile.shape[0], ROWS):
             b = (r + i) // ROWS
             moved = turn(tile[i : i + ROWS], EDGE * b + HALF)
             edge = moved if edge is None else jnp.where(block_of == b, moved, edge)
         return edge
 
     def divergence(d, carry):
-        edge, edge_div = None, None
-        for r in chunks:
-            here, up, down = (pl.ds(PAD + r + by, CHUNK) for by in (0, 1, -1))
-            x = source[0, d + 1, here, :]
-            w = turn(x, -1) - turn(x, 1)
-            w = w + (source[1, d + 1, up, :] - source[1, d + 1, down, :])
-            w = w + (source[2, d + 2, here, :] - source[2, d, here, :])
-            w = w * (0.25 * BULK)
-            div[d + 1, here, :] = w
-            if inner_source is not None:
-                edge = pack(edge, r, x)
-            if inner_div is not None:
-                edge_div = pack(edge_div, r, w)
+        here, up, down = (pl.ds(PAD + by, across) for by in (0, 1, -1))
+        x = source[0, d + 1, here, :]
+        w = turn(x, -1) - turn(x, 1)
+        w = w + (source[1, d + 1, up, :] - source[1, d + 1, down, :])
+        w = w + (source[2, d + 2, here, :] - source[2, d, here, :])
+        w = w * (0.25 * BULK)
+        div[d + 1, here, :] = w
         if inner_source is not None:
-            inner_source[d] = edge
+            inner_source[d] = pack(None, 0, x)
         if inner_div is not None:
-            inner_div[d] = edge_div
+            inner_div[d] = pack(None, 0, w)
         return carry
 
-    loop(depth, step, divergence, 0)
+    loop(depth, 4, divergence, 0)
 
     def image(d, carry):
         norm, cross, cross_rest = carry
@@ -170,7 +164,7 @@
             cross_rest = cross_rest + folded(crosses[1] + crosses[2])
         return norm, cross, cross_rest
 
-    return loop(depth, step, image, (jnp.zeros((ROWS, LANES), jnp.float32),) * 3)
+    return loop(depth, depth, image, (jnp.zeros((ROWS, LANES), jnp.float32),) * 3)
 
 
 def interior(value, margin):
@@ -194,14 +188,14 @@
     def store_third(c, d, r, out):
         third[c, d, r : r + CHUNK, :] = out
 
-    norm, cross, cross_rest = cyclic_step(field, mass, div, store_first, 4)
+    norm, cross, cross_rest = cyclic_step(field, mass, div, store_first)
     moments[0] = norm
     moments[1] = interior(cross + cross_rest, 2)
-    norm, cross, cross_rest = cyclic_step(first, mass, div, store_second, 4, inner.at[0])
+    norm, cross, cross_rest = cyclic_step(first, mass, div, store_second, inner.at[0])
     moments[2] = interior(norm, 2)
     moments[3] = interior(cross + cross_rest, 4)
     norm, cross, cross_rest = cyclic_step(
-        second, mass, div, store_third, 4, inner.at[1], inner.at[2]
+        second, mass, div, store_third, inner.at[1], inner.at[2]
     )
     moments[4] = interior(norm, 4)
     moments[5] = interior(cross, MARGINS[0]) + interior(cross_rest, MARGINS[1])

time: 30.8 us -> 29.9 us (0.971)
  Pallas kernels: 12.5 us -> 11.6 us
    pallas_call x1, Pallas kernels: 5.9 us -> 4.95 us  [cyclic_call(): pl.pallas_call(cyclic_kernel, out_shape=(pltpu.VMEM((3,) + padded, f32),...]
  transfers between devices with their start and end apart: 2 -> 2, of which waited for: 0 -> 0; matrix products, arithmetic and copies ran while one was open for 0% -> 0% of each run, Pallas kernels for 19% -> 17%
where the time goes in v8:
time: 29.9 us; the launch traced here: 29.7 us
  blocking collectives  12.3 us (41%)
  Pallas kernels  11.6 us (39%)
  starting transfers between devices  5.06 us (17%)
  between operations  0.71 us (2%)
    all_to_all x1, blocking collectives, shards(): gathered = lax.all_to_all(payload, AXES, 0, 0, tiled=True)  12.3 us
    pallas_call x1, Pallas kernels, cyclic_call(): pl.pallas_call(cyclic_kernel, out_shape=(pltpu.VMEM((3,) + padded, f32),...  4.95 us
    ppermute x1, starting transfers between devices, shards(): got_a = lax.ppermute(message_a, AXES, pairs_a)  4.39 us
    pallas_call x1, Pallas kernels, combine_call(): pl.pallas_call(functools.partial(combine_kernel, per), out_shape=(jax.Sha...  2.4 us
    pallas_call x1, Pallas kernels, pack_call(): pl.pallas_call(pack_kernel, out_shape=(pltpu.VMEM((3, depth + 2, across +...  2.2 us
    pallas_call x1, Pallas kernels, edge_call(): pl.pallas_call(functools.partial(edge_kernel, per), out_shape=(pltpu.VMEM...  2.03 us
    ppermute x1, starting transfers between devices, shards(): got_b = lax.ppermute(message_b, AXES, pairs_b)  0.67 us
  transfers between devices with their start and end apart: 2, of which 0 were waited for; matrix products, arithmetic and copies ran while one was open for 0% of the time, Pallas kernels for 17%

profile of v8, /device:TPU:0, one launch (start us, length us, event | category | flops | bytes accessed | tf_op | source)
XLA Modules:
  0.0 29.7 jit_solution(14057458520667779438)
XLA Ops:
  0.6 0.0 copy-start.1
  0.6 2.2 %pack.1 = (f32[3,18,80,128]{3,2,1,0:T(8,128)S(1)}, f32[16,64,128]{2,1,0:T(8,128)S(1)}, f32[4,16,8,128]{3,2,1,0:T(8,128)S(1)}, f32[4,8,8,128]{3,2,1,0:T(8,128)S(1)}, f32[4,8,8,128]{3,2,1,0:T(8,128)S(1)}) custom-call(f32[3,16,64,128]{3,2,1,0:T(8,128)} %right_hbm.1, f32[16,64,128]{2,1,0:T(8,128)} %mass_hbm.1), custom_call_target="tpu_custom_call" | custom-call | tf_op jit(solution)/shard_map/pack/pallas_call | solution.py:644
  2.8 0.7 %collective-permute-start = (f32[4,8,8,128]{3,2,1,0:T(8,128)S(1)}, f32[4,8,8,128]{3,2,1,0:T(8,128)S(1)}, u32[]{:S(2)}, u32[]{:S(2)}) collective-permute-start(f32[4,8,8,128]{3,2,1,0:T(8,128)S(1)} %get-tuple-element.19), channel_id=1, source_target_pairs={{1,2},{2,1},{3,4},{4,3},{5,6},{6,5},{7,8},{8,7},{9,10},{10,9},{11,... | collective-permute-start | bytes 393224 | tf_op jit(solution)/shard_map/ppermute | solution.py:749
  3.5 4.4 %collective-permute-start.1 = (f32[4,8,8,128]{3,2,1,0:T(8,128)S(1)}, f32[4,8,8,128]{3,2,1,0:T(8,128)S(1)}, u32[]{:S(2)}, u32[]{:S(2)}) collective-permute-start(f32[4,8,8,128]{3,2,1,0:T(8,128)S(1)} %get-tuple-element.20), channel_id=1, source_target_pairs={{0,1},{1,0},{2,3},{3,2},{4,5},{5,4},{6,7},{7,6},{8,9},{9,8},{10,11... | collective-permute-start | bytes 393224 | tf_op jit(solution)/shard_map/ppermute | solution.py:748
  7.9 0.0 copy-done.1
  7.9 5.0 %cyclic.1 = (f32[3,18,80,128]{3,2,1,0:T(8,128)S(1)}, f32[3,18,80,128]{3,2,1,0:T(8,128)S(1)}, f32[3,16,64,128]{3,2,1,0:T(8,128)S(1)}, f32[3,16,8,128]{3,2,1,0:T(8...) custom-call(f32[3,18,80,128]{3,2,1,0:T(8,128)S(1)} %get-tuple-element.21.field, ...), custom_call_target="tpu_custom_call" | custom-call | flops 60000000 | bytes 12000000 | tf_op jit(solution)/shard_map/cyclic/pallas_call | solution.py:668
  12.9 0.0 collective-permute-done.got_b
  12.9 0.0 collective-permute-done.1.got_a
  12.9 0.0 copy-start
  12.9 0.0 copy-start.2
  12.9 0.0 copy-start.3
  12.9 2.0 %edge.1 = (f32[3,16,8,128]{3,2,1,0:T(8,128)S(1)}, f32[3,16,8,128]{3,2,1,0:T(8,128)S(1)}, f32[3,16,8,128]{3,2,1,0:T(8,128)S(1)}, f32[32,1,640]{2,1,0:T(1,128)S(1)}) custom-call(f32[4,16,8,128]{3,2,1,0:T(8,128)S(1)} %get-tuple-element.18.packed, f32[4,8,8,128]{3,2,1,0:T(8,128)S(1)} %collective-permute-done.got_b, ...), custom_call_target="tpu_custom_call" | custom-call | tf_op jit(solution)/shard_map/edge/pallas_call | solution.py:693
  15.0 12.3 %all_to_all.5.gathered = f32[32,1,640]{2,1,0:T(1,128)S(1)} all-to-all(f32[32,1,640]{2,1,0:T(1,128)S(1)} %get-tuple-element.28), channel_id=1, replica_groups=mesh['len'=8,'xs'=4] {'len','xs'}, dimensions={0} | all-to-all | bytes 163840 | tf_op jit(solution)/shard_map/all_to_all | solution.py:756
  27.3 0.0 copy-done
  27.3 0.0 copy-done.2
  27.3 0.0 copy-done.3
  27.3 2.4 %combine.1 = (f32[3,16,64,128]{3,2,1,0:T(8,128)}, f32[3,16,64,128]{3,2,1,0:T(8,128)}, f32[2,64]{1,0:T(2,128)}) custom-call(f32[32,1,640]{2,1,0:T(1,128)S(1)} %all_to_all.5.gathered, f32[3,18,80,128]{3,2,1,0:T(8,128)S(1)} %get-tuple-element.21.field, f32[3,18,80,128]{3,2,1,0:T(8,128)S(1)} %get-tuple-element.24.first, ...), custom_call_target="tpu_custom_call" | custom-call | tf_op jit(solution)/shard_map/combine/pallas_call | solution.py:714
Async XLA Ops:
  0.6 7.3 %copy-start.1 = (s32[32]{0:T(128)S(1)}, s32[32]{0:T(128)}, u32[]{:S(2)}) copy-start(s32[32]{0:T(128)} %param.8) | copy-start | bytes 388
  2.8 10.0 %collective-permute-start = (f32[4,8,8,128]{3,2,1,0:T(8,128)S(1)}, f32[4,8,8,128]{3,2,1,0:T(8,128)S(1)}, u32[]{:S(2)}, u32[]{:S(2)}) collective-permute-start(f32[4,8,8,128]{3,2,1,0:T(8,128)S(1)} %get-tuple-element.19), channel_id=1, source_target_pairs={{1,2},{2,1},{3,4},{4,3},{5,6},{6,5},{7,8},{8,7},{9,10},{10,9},{11,... | collective-permute-start | bytes 393224 | tf_op jit(solution)/shard_map/ppermute | solution.py:749
  3.5 9.4 %collective-permute-start.1 = (f32[4,8,8,128]{3,2,1,0:T(8,128)S(1)}, f32[4,8,8,128]{3,2,1,0:T(8,128)S(1)}, u32[]{:S(2)}, u32[]{:S(2)}) collective-permute-start(f32[4,8,8,128]{3,2,1,0:T(8,128)S(1)} %get-tuple-element.20), channel_id=1, source_target_pairs={{0,1},{1,0},{2,3},{3,2},{4,5},{5,4},{6,7},{7,6},{8,9},{9,8},{10,11... | collective-permute-start | bytes 393224 | tf_op jit(solution)/shard_map/ppermute | solution.py:748
  12.9 14.4 %copy-start = (f32[2,64]{1,0:T(2,128)S(1)}, f32[2,64]{1,0:T(2,128)}, u32[]{:S(2)}) copy-start(f32[2,64]{1,0:T(2,128)} %prior.1) | copy-start | bytes 1540
  12.9 14.4 %copy-start.2 = (s32[64]{0:T(128)S(1)}, s32[64]{0:T(128)}, u32[]{:S(2)}) copy-start(s32[64]{0:T(128)} %param.9) | copy-start | bytes 772
  12.9 14.4 %copy-start.3 = (f32[64]{0:T(128)S(1)}, f32[64]{0:T(128)}, u32[]{:S(2)}) copy-start(f32[64]{0:T(128)} %param.10) | copy-start | bytes 772

commit v9 on v8

--- a/solution.py
+++ b/solution.py
@@ -65,13 +65,17 @@
 
 def pack_kernel(right_hbm, mass_hbm, field, mass, packed, message_a, message_b, sems):
     depth, across = mass.shape[0], mass.shape[1]
-    copies = [
-        pltpu.make_async_copy(
-            right_hbm.at[c], field.at[c, pl.ds(1, depth), pl.ds(PAD, across)], sems.at[c]
-        )
-        for c in range(3)
-    ]
-    copies.append(pltpu.make_async_copy(mass_hbm, mass, sems.at[3]))
+    half = depth // 2
+    copies = []
+    for c in range(4):
+        for part in range(2):
+            begin = part * half
+            if c < 3:
+                source = right_hbm.at[c, pl.ds(begin, half)]
+                target = field.at[c, pl.ds(1 + begin, half), pl.ds(PAD, across)]
+            else:
+                source, target = mass_hbm.at[pl.ds(begin, half)], mass.at[pl.ds(begin, half)]
+            copies.append(pltpu.make_async_copy(source, target, sems.at[2 * c + part]))
     for copy in copies:
         copy.start()
     for c in range(3):
@@ -81,9 +85,10 @@
     block_of = lane // EDGE
     first_half = lane % EDGE < HALF
     for c in range(4):
-        copies[c].wait()
         edges = []
         for d in range(depth):
+            if d % half == 0:
+                copies[2 * c + d // half].wait()
             edge = None
             for b in range(across // ROWS):
                 row = pl.ds(b * ROWS + (PAD if c < 3 else 0), ROWS)
@@ -652,7 +657,7 @@
         ),
         in_specs=[hbm_spec()] * 2,
         out_specs=(vmem_spec(),) * 5,
-        scratch_shapes=[pltpu.SemaphoreType.DMA((4,))],
+        scratch_shapes=[pltpu.SemaphoreType.DMA((8,))],
         compiler_params=LIMIT,
         name="pack",
     )(

time: 29.9 us -> 30.1 us (level)
  no operation moved by 1% of the time
where the time goes in v9:
time: 30.1 us; the launch traced here: 29.9 us
  blocking collectives  12.3 us (41%)
  Pallas kernels  11.8 us (39%)
  starting transfers between devices  5.06 us (17%)
  between operations  0.71 us (2%)
    all_to_all x1, blocking collectives, shards(): gathered = lax.all_to_all(payload, AXES, 0, 0, tiled=True)  12.3 us
    pallas_call x1, Pallas kernels, cyclic_call(): pl.pallas_call(cyclic_kernel, out_shape=(pltpu.VMEM((3,) + padded, f32),...  4.95 us
    ppermute x1, starting transfers between devices, shards(): got_a = lax.ppermute(message_a, AXES, pairs_a)  4.39 us
    pallas_call x1, Pallas kernels, pack_call(): pl.pallas_call(pack_kernel, out_shape=(pltpu.VMEM((3, depth + 2, across +...  2.42 us
    pallas_call x1, Pallas kernels, combine_call(): pl.pallas_call(functools.partial(combine_kernel, per), out_shape=(jax.Sha...  2.4 us
    pallas_call x1, Pallas kernels, edge_call(): pl.pallas_call(functools.partial(edge_kernel, per), out_shape=(pltpu.VMEM...  2.03 us
    ppermute x1, starting transfers between devices, shards(): got_b = lax.ppermute(message_b, AXES, pairs_b)  0.67 us
  transfers between devices with their start and end apart: 2, of which 0 were waited for; matrix products, arithmetic and copies ran while one was open for 0% of the time, Pallas kernels for 17%

profile of v9, /device:TPU:0, one launch (start us, length us, event | category | flops | bytes accessed | tf_op | source)
XLA Modules:
  0.0 29.9 jit_solution(15648803252818717358)
XLA Ops:
  0.6 0.0 copy-start.1
  0.6 2.4 %pack.1 = (f32[3,18,80,128]{3,2,1,0:T(8,128)S(1)}, f32[16,64,128]{2,1,0:T(8,128)S(1)}, f32[4,16,8,128]{3,2,1,0:T(8,128)S(1)}, f32[4,8,8,128]{3,2,1,0:T(8,128)S(1)}, f32[4,8,8,128]{3,2,1,0:T(8,128)S(1)}) custom-call(f32[3,16,64,128]{3,2,1,0:T(8,128)} %right_hbm.1, f32[16,64,128]{2,1,0:T(8,128)} %mass_hbm.1), custom_call_target="tpu_custom_call" | custom-call | tf_op jit(solution)/shard_map/pack/pallas_call | solution.py:649
  3.1 0.7 %collective-permute-start = (f32[4,8,8,128]{3,2,1,0:T(8,128)S(1)}, f32[4,8,8,128]{3,2,1,0:T(8,128)S(1)}, u32[]{:S(2)}, u32[]{:S(2)}) collective-permute-start(f32[4,8,8,128]{3,2,1,0:T(8,128)S(1)} %get-tuple-element.19), channel_id=1, source_target_pairs={{1,2},{2,1},{3,4},{4,3},{5,6},{6,5},{7,8},{8,7},{9,10},{10,9},{11,... | collective-permute-start | bytes 393224 | tf_op jit(solution)/shard_map/ppermute | solution.py:754
  3.7 4.4 %collective-permute-start.1 = (f32[4,8,8,128]{3,2,1,0:T(8,128)S(1)}, f32[4,8,8,128]{3,2,1,0:T(8,128)S(1)}, u32[]{:S(2)}, u32[]{:S(2)}) collective-permute-start(f32[4,8,8,128]{3,2,1,0:T(8,128)S(1)} %get-tuple-element.20), channel_id=1, source_target_pairs={{0,1},{1,0},{2,3},{3,2},{4,5},{5,4},{6,7},{7,6},{8,9},{9,8},{10,11... | collective-permute-start | bytes 393224 | tf_op jit(solution)/shard_map/ppermute | solution.py:753
  8.1 0.0 copy-done.1
  8.1 5.0 %cyclic.1 = (f32[3,18,80,128]{3,2,1,0:T(8,128)S(1)}, f32[3,18,80,128]{3,2,1,0:T(8,128)S(1)}, f32[3,16,64,128]{3,2,1,0:T(8,128)S(1)}, f32[3,16,8,128]{3,2,1,0:T(8...) custom-call(f32[3,18,80,128]{3,2,1,0:T(8,128)S(1)} %get-tuple-element.21.field, ...), custom_call_target="tpu_custom_call" | custom-call | flops 60000000 | bytes 12000000 | tf_op jit(solution)/shard_map/cyclic/pallas_call | solution.py:673
  13.1 0.0 collective-permute-done.got_b
  13.1 0.0 collective-permute-done.1.got_a
  13.1 0.0 copy-start
  13.1 0.0 copy-start.2
  13.1 0.0 copy-start.3
  13.2 2.0 %edge.1 = (f32[3,16,8,128]{3,2,1,0:T(8,128)S(1)}, f32[3,16,8,128]{3,2,1,0:T(8,128)S(1)}, f32[3,16,8,128]{3,2,1,0:T(8,128)S(1)}, f32[32,1,640]{2,1,0:T(1,128)S(1)}) custom-call(f32[4,16,8,128]{3,2,1,0:T(8,128)S(1)} %get-tuple-element.18.packed, f32[4,8,8,128]{3,2,1,0:T(8,128)S(1)} %collective-permute-done.got_b, ...), custom_call_target="tpu_custom_call" | custom-call | tf_op jit(solution)/shard_map/edge/pallas_call | solution.py:698
  15.2 12.3 %all_to_all.5.gathered = f32[32,1,640]{2,1,0:T(1,128)S(1)} all-to-all(f32[32,1,640]{2,1,0:T(1,128)S(1)} %get-tuple-element.28), channel_id=1, replica_groups=mesh['len'=8,'xs'=4] {'len','xs'}, dimensions={0} | all-to-all | bytes 163840 | tf_op jit(solution)/shard_map/all_to_all | solution.py:761
  27.5 0.0 copy-done
  27.5 0.0 copy-done.2
  27.5 0.0 copy-done.3
  27.5 2.4 %combine.1 = (f32[3,16,64,128]{3,2,1,0:T(8,128)}, f32[3,16,64,128]{3,2,1,0:T(8,128)}, f32[2,64]{1,0:T(2,128)}) custom-call(f32[32,1,640]{2,1,0:T(1,128)S(1)} %all_to_all.5.gathered, f32[3,18,80,128]{3,2,1,0:T(8,128)S(1)} %get-tuple-element.21.field, f32[3,18,80,128]{3,2,1,0:T(8,128)S(1)} %get-tuple-element.24.first, ...), custom_call_target="tpu_custom_call" | custom-call | tf_op jit(solution)/shard_map/combine/pallas_call | solution.py:719
Async XLA Ops:
  0.6 7.5 %copy-start.1 = (s32[32]{0:T(128)S(1)}, s32[32]{0:T(128)}, u32[]{:S(2)}) copy-start(s32[32]{0:T(128)} %param.8) | copy-start | bytes 388
  3.1 10.0 %collective-permute-start = (f32[4,8,8,128]{3,2,1,0:T(8,128)S(1)}, f32[4,8,8,128]{3,2,1,0:T(8,128)S(1)}, u32[]{:S(2)}, u32[]{:S(2)}) collective-permute-start(f32[4,8,8,128]{3,2,1,0:T(8,128)S(1)} %get-tuple-element.19), channel_id=1, source_target_pairs={{1,2},{2,1},{3,4},{4,3},{5,6},{6,5},{7,8},{8,7},{9,10},{10,9},{11,... | collective-permute-start | bytes 393224 | tf_op jit(solution)/shard_map/ppermute | solution.py:754
  3.7 9.4 %collective-permute-start.1 = (f32[4,8,8,128]{3,2,1,0:T(8,128)S(1)}, f32[4,8,8,128]{3,2,1,0:T(8,128)S(1)}, u32[]{:S(2)}, u32[]{:S(2)}) collective-permute-start(f32[4,8,8,128]{3,2,1,0:T(8,128)S(1)} %get-tuple-element.20), channel_id=1, source_target_pairs={{0,1},{1,0},{2,3},{3,2},{4,5},{5,4},{6,7},{7,6},{8,9},{9,8},{10,11... | collective-permute-start | bytes 393224 | tf_op jit(solution)/shard_map/ppermute | solution.py:753
  13.1 14.4 %copy-start = (f32[2,64]{1,0:T(2,128)S(1)}, f32[2,64]{1,0:T(2,128)}, u32[]{:S(2)}) copy-start(f32[2,64]{1,0:T(2,128)} %prior.1) | copy-start | bytes 1540
  13.1 14.4 %copy-start.2 = (s32[64]{0:T(128)S(1)}, s32[64]{0:T(128)}, u32[]{:S(2)}) copy-start(s32[64]{0:T(128)} %param.9) | copy-start | bytes 772
  13.1 14.4 %copy-start.3 = (f32[64]{0:T(128)S(1)}, f32[64]{0:T(128)}, u32[]{:S(2)}) copy-start(f32[64]{0:T(128)} %param.10) | copy-start | bytes 772
